TPU v7x, 256 devices: a whole 4x4x8 slice. The times are simulated.
256 devices in a mesh: east: 16 (over y, z_hi), north: 16 (over z_lo, x, core).
Axes of the slice: x: 4, y: 4, z: 8 (z_hi: 4, z_lo: 2; z = z_hi * 2 + z_lo), core: 2. Of those that a mesh axis runs over, the one named last changes fastest.
Arguments:
- head_old: float32 [64, 256, 2048], P(None, 'east', 'north'), may hold values from -6 to 6
- source: float32 [64, 256, 2048], P(None, 'east', 'north'), may hold values from -6 to 6
- mode_coeffs: float32 [8, 8, 8], replicated, may hold values from -4 to 4
- records: float32 [32, 1048576], P(None, ('east', 'north')), may hold values from -6 to 6
- cell_index: int32 [1048576], P(('east', 'north')), may hold values from 0 to 131071
- coupling: float32 [3, 32], replicated, may hold values from -3.5 to 3.5
- send_list: int32 [4, 131072], P(None, ('east', 'north')), may hold values from 0 to 4095, as said below
- send_count: int32 [4, 256], P(None, ('east', 'north')), may hold values from 0 to 512, as said below
Outputs:
- heads: float32 [64, 256, 2048], P(None, 'east', 'north')
- moved: float32 [32, 1048576], P(None, ('east', 'north'))
- arrivals: float32 [4, 32, 131072], P(None, None, ('east', 'north'))
Inputs may be any that keep to these rules, and one draw needn't show every extreme that they name: `send_list`: within one tile's block the 512 slots of all four directions name distinct particles of that tile. `send_count`: some tile fills all 512 slots of some direction.
All inputs are finite; a program needn't handle non-finite values.
Results may differ from a plain program's by a relative error of at most 0.000076.
Values sent between devices are 32-bit elements; how exact they have to be, the bound alone decides.
No kernel may reach another device: no remote copies, remote signals or barrier semaphores. Data moves between devices by JAX's collectives and lax.ppermute only.
A program may use at most 64 MiB of HBM per device.

v0:
```python
import jax
import jax.numpy as jnp
from jax import lax
from jax.sharding import PartitionSpec as P

ITERS = 4


gardner_rate = 1.0
step_size = 0.25
mean_log = 0.0
spread_log = 1.0
highest = lax.Precision.HIGHEST


def with_halo(block, sides, width):
    for axis, dim in sides:
        count = lax.axis_size(axis)
        forward = [(i, i + 1) for i in range(count - 1)]
        backward = [(target, source) for source, target in forward]
        low = lax.ppermute(
            lax.slice_in_dim(block, block.shape[dim] - width, None, axis=dim), axis, forward
        )
        high = lax.ppermute(lax.slice_in_dim(block, 0, width, axis=dim), axis, backward)
        block = jnp.concatenate([low, block, high], axis=dim)
    return block


def shifted(value, axis, steps):
    count = lax.axis_size(axis)
    initial, last = (max(0, -steps), min(count, count - steps))
    return lax.ppermute(value, axis, [(source, source + steps) for source in range(initial, last)])


def mode_table(coords, count, total):
    orders = jnp.arange(count).astype(jnp.float32)
    return jnp.cos(jnp.pi * orders[:, None] * (coords.astype(jnp.float32)[None, :] + 0.5) / total)


def mode_weights(mode_coeffs):
    order_z = jnp.arange(mode_coeffs.shape[0]).astype(jnp.float32)
    order_x = jnp.arange(mode_coeffs.shape[1]).astype(jnp.float32)
    order_y = jnp.arange(mode_coeffs.shape[2]).astype(jnp.float32)
    spectrum = 1.0 / (
        1.0
        + (order_z[:, None, None] ** 2 + order_x[None, :, None] ** 2 + order_y[None, None, :] ** 2)
        / 4.0
    )
    return mode_coeffs * jnp.sqrt(spectrum) * (spread_log / jnp.sqrt(jnp.sum(spectrum)))


def conductivity(weights, table_z, table_x, table_y):
    partial_y = jnp.einsum("cab,by->cay", weights, table_y, precision=highest)
    partial_x = jnp.einsum("cay,ax->cxy", partial_y, table_x, precision=highest)
    return jnp.exp(mean_log + jnp.einsum("cl,cxy->lxy", table_z, partial_x, precision=highest))


def relative(head_field):
    return jnp.exp(gardner_rate * jnp.minimum(head_field, 0.0))


def crop_rows(field, margin):
    return field[:, margin : field.shape[1] - margin]


def face_rim(field):
    return with_halo(field, (("east", 1),), 1)


def side_columns(field):
    south_col = shifted(field[:, :, field.shape[2] - 1], "north", 1)
    north_col = shifted(field[:, :, 0], "north", -1)
    return (south_col, north_col)


def with_north(centre, column):
    return jnp.concatenate([centre[:, :, 1:], column[:, :, None]], 2)


def with_south(centre, column):
    return jnp.concatenate([column[:, :, None], centre[:, :, :-1]], 2)


def jacobi_sweep(
    head_ext,
    south_col,
    north_col,
    cond_ext,
    cond_sides,
    storage,
    head_old,
    source,
    inside_x,
    mask_south,
    mask_north,
):
    darcy_k = cond_ext * relative(head_ext)
    centre = darcy_k[:, 1:-1]
    head_centre = head_ext[:, 1:-1]
    face_east = 0.5 * (centre + darcy_k[:, 2:]) * inside_x[2:][None, :, None]
    face_west = 0.5 * (centre + darcy_k[:, :-2]) * inside_x[:-2][None, :, None]
    k_south = cond_sides[:, :, 0] * relative(south_col)
    k_north = cond_sides[:, :, 1] * relative(north_col)
    face_north = 0.5 * (centre + with_north(centre, k_north)) * mask_north
    face_south = 0.5 * (centre + with_south(centre, k_south)) * mask_south
    head_north = with_north(head_centre, north_col)
    head_south = with_south(head_centre, south_col)
    zero_z = jnp.zeros_like(centre[:1])
    faces_z = 0.5 * (centre[1:] + centre[:-1])
    face_up = jnp.concatenate([faces_z, zero_z], 0)
    face_down = jnp.concatenate([zero_z, faces_z], 0)
    head_up = jnp.concatenate([head_centre[1:], zero_z], 0)
    head_down = jnp.concatenate([zero_z, head_centre[:-1]], 0)
    numerator = (
        storage * head_old
        + face_east * head_ext[:, 2:]
        + face_west * head_ext[:, :-2]
        + face_north * head_north
        + face_south * head_south
        + face_up * head_up
        + face_down * head_down
        + face_up
        - face_down
        + source
    )
    denominator = storage + face_east + face_west + face_north + face_south + face_up + face_down
    return numerator / denominator


def darcy_velocity(head_ext, south_col, north_col, cond_centre):
    head_centre = head_ext[:, 1:-1]
    darcy_k = cond_centre * relative(head_centre)
    flow_x = -darcy_k * 0.5 * (head_ext[:, 2:] - head_ext[:, :-2])
    flow_y = (
        -darcy_k * 0.5 * (with_north(head_centre, north_col) - with_south(head_centre, south_col))
    )
    padded = jnp.pad(head_centre, ((1, 1), (0, 0), (0, 0)))
    flow_z = -darcy_k * (0.5 * (padded[2:] - padded[:-2]) + 1.0)
    return jnp.stack([flow_x, flow_y, flow_z])


def on_device(head_old, source, mode_coeffs, records, cell_index, coupling, send_list, send_count):
    layers, cols_x, cols_y = head_old.shape
    total_x = cols_x * lax.axis_size("east")
    total_y = cols_y * lax.axis_size("north")
    start_x = lax.axis_index("east") * cols_x
    start_y = lax.axis_index("north") * cols_y
    ghost_depth = 1
    coords_x = start_x + jnp.arange(-ghost_depth, cols_x + ghost_depth)
    coords_y = start_y + jnp.arange(cols_y)
    side_y = start_y + jnp.array([-1, cols_y])
    inside_x = ((coords_x >= 0) & (coords_x < total_x)).astype(jnp.float32)
    column_ids = jnp.arange(cols_y)
    lower_live = (start_y > 0).astype(jnp.float32)
    upper_live = (start_y + cols_y < total_y).astype(jnp.float32)
    mask_south = jnp.where(column_ids == 0, lower_live, 1.0)[None, None, :]
    mask_north = jnp.where(column_ids == cols_y - 1, upper_live, 1.0)[None, None, :]
    weights = mode_weights(mode_coeffs)
    table_z = mode_table(jnp.arange(layers), mode_coeffs.shape[0], layers)
    table_x = mode_table(coords_x, mode_coeffs.shape[1], total_x)
    cond_wide = conductivity(
        weights, table_z, table_x, mode_table(coords_y, mode_coeffs.shape[2], total_y)
    )
    sides_wide = conductivity(
        weights, table_z, table_x, mode_table(side_y, mode_coeffs.shape[2], total_y)
    )
    storage = 0.5 + 0.5 * relative(head_old)
    sides_centre = crop_rows(sides_wide, 1)
    head_field = head_old
    for number in range(ITERS):
        south_col, north_col = side_columns(head_field)
        head_field = jacobi_sweep(
            face_rim(head_field),
            south_col,
            north_col,
            cond_wide,
            sides_centre,
            storage,
            head_old,
            source,
            inside_x,
            mask_south,
            mask_north,
        )
    final_ext = face_rim(head_field)
    south_col, north_col = side_columns(head_field)
    velocity = darcy_velocity(final_ext, south_col, north_col, crop_rows(cond_wide, ghost_depth))
    heads_out = final_ext[:, 1:-1]
    row_table = velocity.reshape(3, layers * cols_x, cols_y)
    row_of = cell_index // cols_y
    column_of = cell_index % cols_y
    fetched = jnp.take(row_table, row_of, axis=1)
    picker = (column_of[:, None] == column_ids[None, :]).astype(jnp.float32)
    sampled = jnp.sum(fetched * picker[None], axis=2)
    moved = records + step_size * jnp.dot(coupling.T, sampled, precision=highest)
    slots = send_list.shape[1]
    picked = jnp.take(moved, send_list.reshape(-1), axis=1).reshape(moved.shape[0], 4, slots)
    live_slots = (jnp.arange(slots)[None, :] < send_count).astype(jnp.float32)
    buffers = picked * live_slots[None]
    from_low_east = shifted(buffers[:, 0], "east", 1)
    from_high_east = shifted(buffers[:, 1], "east", -1)
    from_low_north = shifted(buffers[:, 2], "north", 1)
    from_high_north = shifted(buffers[:, 3], "north", -1)
    arrivals = jnp.stack([from_low_east, from_high_east, from_low_north, from_high_north])
    return (heads_out, moved, arrivals)


def solution(mesh):
    return jax.shard_map(
        on_device,
        mesh=mesh,
        in_specs=(
            P(None, "east", "north"),
            P(None, "east", "north"),
            P(),
            P(None, ("east", "north")),
            P(("east", "north")),
            P(),
            P(None, ("east", "north")),
            P(None, ("east", "north")),
        ),
        out_specs=(
            P(None, "east", "north"),
            P(None, ("east", "north")),
            P(None, None, ("east", "north")),
        ),
        check_vma=False,
    )
```

profile of v0, /device:TPU:31, one launch (start us, length us, event | category | flops | bytes accessed | tf_op | source)
XLA Modules:
  0.0 260.5 jit_solution(7502043315954168908)
XLA Ops:
  0.6 1.2 copy.1222
  1.9 4.9 %collective-permute-start = (f32[64,1,128]{2,0,1:T(8,128)S(1)}, f32[64,1,128]{2,0,1:T(8,128)S(1)}, u32[]{:S(2)}, u32[]{:S(2)}) collective-permute-start(f32[64,1,128]{2,0,1:T(8,128)S(1)} %get-tuple-element.126), channel_id=1, source_target_pairs={{0,16},{16,32},{32,48},{48,64},{64,80},{80,96},{96,112},{112,128},... | collective-permute-start | bytes 98312 | tf_op jit(solution)/shard_map/ppermute | solution.py:21
  6.8 5.1 %collective-permute-start.1 = (f32[64,1,128]{2,0,1:T(8,128)S(1)}, f32[64,1,128]{2,0,1:T(8,128)S(1)}, u32[]{:S(2)}, u32[]{:S(2)}) collective-permute-start(f32[64,1,128]{2,0,1:T(8,128)S(1)} %get-tuple-element.125), channel_id=1, source_target_pairs={{16,0},{32,16},{48,32},{64,48},{80,64},{96,80},{112,96},{128,112},... | collective-permute-start | bytes 98312 | tf_op jit(solution)/shard_map/ppermute | solution.py:24
  11.9 1.4 fusion.150
  13.6 2.9 %collective-permute-start.2 = (f32[64,16]{0,1:T(8,128)S(1)}, f32[64,16]{0,1:T(8,128)S(1)}, u32[]{:S(2)}, u32[]{:S(2)}) collective-permute-start(f32[64,16]{0,1:T(8,128)S(1)} %bitcast.127), channel_id=1, source_target_pairs={{1,0},{2,1},{3,2},{4,3},{5,4},{6,5},{7,6},{8,7},{9,8},{10,9},{11,1... | collective-permute-start | bytes 12296 | tf_op jit(solution)/shard_map/ppermute | solution.py:32
  16.8 4.8 %collective-permute-start.3 = (f32[64,16]{0,1:T(8,128)S(1)}, f32[64,16]{0,1:T(8,128)S(1)}, u32[]{:S(2)}, u32[]{:S(2)}) collective-permute-start(f32[64,16]{0,1:T(8,128)S(1)} %bitcast.128), channel_id=1, source_target_pairs={{0,1},{1,2},{2,3},{3,4},{4,5},{5,6},{6,7},{7,8},{8,9},{9,10},{10,1... | collective-permute-start | bytes 12296 | tf_op jit(solution)/shard_map/ppermute | solution.py:32
  21.7 1.1 fusion.149
  22.8 1.1 fusion.151
  27.1 2.9 %fusion.2 = f32[4096,128]{1,0:T(8,128)} fusion(s32[4096]{0:T(1024)S(1)} %get-tuple-element.139), kind=kLoop, calls=%fused_computation.8 | loop fusion | flops 1048576 | bytes 2113536 | tf_op jit(solution)/shard_map/convert_element_type | solution.py:193
  36.7 1.3 fusion.73
  38.6 1.1 fusion.146
  39.6 1.1 fusion.147
  40.7 1.9 collective-permute-start.6
  42.7 5.8 %collective-permute-start.7 = (f32[64,16]{0,1:T(8,128)S(1)}, f32[64,16]{0,1:T(8,128)S(1)}, u32[]{:S(2)}, u32[]{:S(2)}) collective-permute-start(f32[64,16]{0,1:T(8,128)S(1)} %get-tuple-element.84), channel_id=1, source_target_pairs={{0,1},{1,2},{2,3},{3,4},{4,5},{5,6},{6,7},{7,8},{8,9},{9,10},{10,1... | collective-permute-start | bytes 12296 | tf_op jit(solution)/shard_map/ppermute | solution.py:32
  48.4 2.9 %collective-permute-start.4 = (f32[64,1,128]{2,0,1:T(8,128)S(1)}, f32[64,1,128]{2,0,1:T(8,128)S(1)}, u32[]{:S(2)}, u32[]{:S(2)}) collective-permute-start(f32[64,1,128]{2,0,1:T(8,128)S(1)} %get-tuple-element.118), channel_id=1, source_target_pairs={{0,16},{16,32},{32,48},{48,64},{64,80},{80,96},{96,112},{112,128},... | collective-permute-start | bytes 98312 | tf_op jit(solution)/shard_map/ppermute | solution.py:21
  51.3 5.4 %collective-permute-start.5 = (f32[64,1,128]{2,0,1:T(8,128)S(1)}, f32[64,1,128]{2,0,1:T(8,128)S(1)}, u32[]{:S(2)}, u32[]{:S(2)}) collective-permute-start(f32[64,1,128]{2,0,1:T(8,128)S(1)} %get-tuple-element.117), channel_id=1, source_target_pairs={{16,0},{32,16},{48,32},{64,48},{80,64},{96,80},{112,96},{128,112},... | collective-permute-start | bytes 98312 | tf_op jit(solution)/shard_map/ppermute | solution.py:24
  62.4 1.5 fusion.58
  64.3 1.1 fusion.143
  65.4 1.1 fusion.144
  66.5 1.9 collective-permute-start.10
  68.4 5.8 %collective-permute-start.11 = (f32[64,16]{0,1:T(8,128)S(1)}, f32[64,16]{0,1:T(8,128)S(1)}, u32[]{:S(2)}, u32[]{:S(2)}) collective-permute-start(f32[64,16]{0,1:T(8,128)S(1)} %get-tuple-element.82), channel_id=1, source_target_pairs={{0,1},{1,2},{2,3},{3,4},{4,5},{5,6},{6,7},{7,8},{8,9},{9,10},{10,1... | collective-permute-start | bytes 12296 | tf_op jit(solution)/shard_map/ppermute | solution.py:32
  74.2 3.4 %collective-permute-start.8 = (f32[64,1,128]{2,0,1:T(8,128)S(1)}, f32[64,1,128]{2,0,1:T(8,128)S(1)}, u32[]{:S(2)}, u32[]{:S(2)}) collective-permute-start(f32[64,1,128]{2,0,1:T(8,128)S(1)} %get-tuple-element.112), channel_id=1, source_target_pairs={{0,16},{16,32},{32,48},{48,64},{64,80},{80,96},{96,112},{112,128},... | collective-permute-start | bytes 98312 | tf_op jit(solution)/shard_map/ppermute | solution.py:21
  77.6 5.1 %collective-permute-start.9 = (f32[64,1,128]{2,0,1:T(8,128)S(1)}, f32[64,1,128]{2,0,1:T(8,128)S(1)}, u32[]{:S(2)}, u32[]{:S(2)}) collective-permute-start(f32[64,1,128]{2,0,1:T(8,128)S(1)} %get-tuple-element.111), channel_id=1, source_target_pairs={{16,0},{32,16},{48,32},{64,48},{80,64},{96,80},{112,96},{128,112},... | collective-permute-start | bytes 98312 | tf_op jit(solution)/shard_map/ppermute | solution.py:24
  88.2 1.5 fusion.43
  90.2 1.1 fusion.140
  91.3 1.1 fusion.141
  92.4 1.9 collective-permute-start.14
  94.3 5.8 %collective-permute-start.15 = (f32[64,16]{0,1:T(8,128)S(1)}, f32[64,16]{0,1:T(8,128)S(1)}, u32[]{:S(2)}, u32[]{:S(2)}) collective-permute-start(f32[64,16]{0,1:T(8,128)S(1)} %get-tuple-element.80), channel_id=1, source_target_pairs={{0,1},{1,2},{2,3},{3,4},{4,5},{5,6},{6,7},{7,8},{8,9},{9,10},{10,1... | collective-permute-start | bytes 12296 | tf_op jit(solution)/shard_map/ppermute | solution.py:32
  100.1 2.3 collective-permute-start.12
  102.4 6.0 %collective-permute-start.13 = (f32[64,1,128]{2,0,1:T(8,128)S(1)}, f32[64,1,128]{2,0,1:T(8,128)S(1)}, u32[]{:S(2)}, u32[]{:S(2)}) collective-permute-start(f32[64,1,128]{2,0,1:T(8,128)S(1)} %get-tuple-element.105), channel_id=1, source_target_pairs={{16,0},{32,16},{48,32},{64,48},{80,64},{96,80},{112,96},{128,112},... | collective-permute-start | bytes 98312 | tf_op jit(solution)/shard_map/ppermute | solution.py:24
  113.9 1.5 fusion.28
  115.9 1.9 collective-permute-start.18
  117.8 5.8 %collective-permute-start.19 = (f32[64,16]{0,1:T(8,128)S(1)}, f32[64,16]{0,1:T(8,128)S(1)}, u32[]{:S(2)}, u32[]{:S(2)}) collective-permute-start(f32[64,16]{0,1:T(8,128)S(1)} %get-tuple-element.78), channel_id=1, source_target_pairs={{0,1},{1,2},{2,3},{3,4},{4,5},{5,6},{6,7},{7,8},{8,9},{9,10},{10,1... | collective-permute-start | bytes 12296 | tf_op jit(solution)/shard_map/ppermute | solution.py:32
  123.6 4.2 %collective-permute-start.16 = (f32[64,1,128]{2,0,1:T(8,128)S(1)}, f32[64,1,128]{2,0,1:T(8,128)S(1)}, u32[]{:S(2)}, u32[]{:S(2)}) collective-permute-start(f32[64,1,128]{2,0,1:T(8,128)S(1)} %get-tuple-element.97), channel_id=1, source_target_pairs={{16,0},{32,16},{48,32},{64,48},{80,64},{96,80},{112,96},{128,112},... | collective-permute-start | bytes 98312 | tf_op jit(solution)/shard_map/ppermute | solution.py:24
  127.8 2.2 collective-permute-start.17
  130.8 4.8 %collective-permute-done.17 = f32[64,1,128]{2,0,1:T(8,128)S(1)} collective-permute-done((f32[64,1,128]{2,0,1:T(8,128)S(1)}, f32[64,1,128]{2,0,1:T(8,128)S(1)}, u32[]{:S(2)}, u32[]{:S(2)}) %collective-permute-start.17) | collective-permute-done | bytes 32800 | tf_op jit(solution)/shard_map/ppermute | solution.py:21
  136.9 1.4 pad_maximum_fusion
  138.3 30.3 %gather_fusion = f32[4096,3,128]{2,1,0:T(4,128)} fusion(f32[3,1024,128]{2,0,1:T(4,128)S(1)} %pad_maximum_fusion, s32[4096]{0:T(1024)S(1)} %get-tuple-element.140), kind=kCustom, calls=%fused_computation | custom fusion | bytes 12599296 | tf_op jit(solution)/shard_map/jit(_take)/gather | solution.py:192
  168.6 59.1 %multiply_reduce_fusion = f32[4096,3]{1,0:T(8,128)S(1)} fusion(f32[4096,3,128]{2,1,0:T(4,128)} %gather_fusion, f32[4096,128]{1,0:T(8,128)} %fusion.2, pred[4096]{0:T(1024)(128)(4,1)S(1)} %compare_and_fusion), kind=kLoop, calls=%fused_computation.2 | loop fusion | flops 4706304 | bytes 8441856 | tf_op jit(solution)/shard_map/reduce_sum | solution.py:194
  227.6 2.3 fusion.1
  230.6 7.6 %gather_fusion.1 = f32[2048,32]{1,0:T(8,128)} fusion(f32[32,4096]{0,1:T(8,128)S(1)} %copy.1265, s32[2048]{0:T(1024)S(1)} %broadcast_clamp_fusion.1), kind=kCustom, calls=%fused_computation.1 | custom fusion | bytes 532480 | tf_op jit(solution)/shard_map/jit(_take)/gather | solution.py:197
  238.2 1.5 copy.1266
  239.8 1.9 collective-permute-start.20
  241.7 6.4 %collective-permute-start.21 = (f32[32,512]{1,0:T(8,128)S(1)}, f32[32,512]{1,0:T(8,128)S(1)}, u32[]{:S(2)}, u32[]{:S(2)}) collective-permute-start(f32[32,512]{1,0:T(8,128)S(1)} %get-tuple-element.130), channel_id=1, source_target_pairs={{16,0},{32,16},{48,32},{64,48},{80,64},{96,80},{112,96},{128,112},... | collective-permute-start | bytes 196616 | tf_op jit(solution)/shard_map/ppermute | solution.py:32
  248.1 3.9 %collective-permute-start.22 = (f32[32,512]{1,0:T(8,128)S(1)}, f32[32,512]{1,0:T(8,128)S(1)}, u32[]{:S(2)}, u32[]{:S(2)}) collective-permute-start(f32[32,512]{1,0:T(8,128)S(1)} %get-tuple-element.129), channel_id=1, source_target_pairs={{0,1},{1,2},{2,3},{3,4},{4,5},{5,6},{6,7},{7,8},{8,9},{9,10},{10,1... | collective-permute-start | bytes 196616 | tf_op jit(solution)/shard_map/ppermute | solution.py:32
  252.0 1.9 collective-permute-start.23
  254.0 1.1 copy.1267
  255.1 4.7 %collective-permute-done.23 = f32[32,512]{1,0:T(8,128)S(1)} collective-permute-done((f32[32,512]{1,0:T(8,128)S(1)}, f32[32,512]{1,0:T(8,128)S(1)}, u32[]{:S(2)}, u32[]{:S(2)}) %collective-permute-start.23) | collective-permute-done | bytes 65568 | tf_op jit(solution)/shard_map/ppermute | solution.py:32
  (174 shorter events, 31.6 us)
Async XLA Ops:
  0.6 227.0 %copy-start = (f32[3,32]{1,0:T(4,128)S(1)}, f32[3,32]{1,0:T(4,128)}, u32[]{:S(2)}) copy-start(f32[3,32]{1,0:T(4,128)} %param.14) | copy-start | bytes 1156
  1.9 32.0 %collective-permute-start = (f32[64,1,128]{2,0,1:T(8,128)S(1)}, f32[64,1,128]{2,0,1:T(8,128)S(1)}, u32[]{:S(2)}, u32[]{:S(2)}) collective-permute-start(f32[64,1,128]{2,0,1:T(8,128)S(1)} %get-tuple-element.126), channel_id=1, source_target_pairs={{0,16},{16,32},{32,48},{48,64},{64,80},{80,96},{96,112},{112,128},... | collective-permute-start | bytes 98312 | tf_op jit(solution)/shard_map/ppermute | solution.py:21
  6.8 27.1 %collective-permute-start.1 = (f32[64,1,128]{2,0,1:T(8,128)S(1)}, f32[64,1,128]{2,0,1:T(8,128)S(1)}, u32[]{:S(2)}, u32[]{:S(2)}) collective-permute-start(f32[64,1,128]{2,0,1:T(8,128)S(1)} %get-tuple-element.125), channel_id=1, source_target_pairs={{16,0},{32,16},{48,32},{64,48},{80,64},{96,80},{112,96},{128,112},... | collective-permute-start | bytes 98312 | tf_op jit(solution)/shard_map/ppermute | solution.py:24
  13.6 16.8 %collective-permute-start.2 = (f32[64,16]{0,1:T(8,128)S(1)}, f32[64,16]{0,1:T(8,128)S(1)}, u32[]{:S(2)}, u32[]{:S(2)}) collective-permute-start(f32[64,16]{0,1:T(8,128)S(1)} %bitcast.127), channel_id=1, source_target_pairs={{1,0},{2,1},{3,2},{4,3},{5,4},{6,5},{7,6},{8,7},{9,8},{10,9},{11,1... | collective-permute-start | bytes 12296 | tf_op jit(solution)/shard_map/ppermute | solution.py:32
  16.8 13.7 %collective-permute-start.3 = (f32[64,16]{0,1:T(8,128)S(1)}, f32[64,16]{0,1:T(8,128)S(1)}, u32[]{:S(2)}, u32[]{:S(2)}) collective-permute-start(f32[64,16]{0,1:T(8,128)S(1)} %bitcast.128), channel_id=1, source_target_pairs={{0,1},{1,2},{2,3},{3,4},{4,5},{5,6},{6,7},{7,8},{8,9},{9,10},{10,1... | collective-permute-start | bytes 12296 | tf_op jit(solution)/shard_map/ppermute | solution.py:32
  21.7 2.2 copy-start.33
  21.7 3.7 %copy-start.37 = (s32[2]{0:T(128)S(1)}, s32[2]{0:T(128)}, u32[]{:S(2)}) copy-start(s32[2]{0:T(128)} %constant.112.clone) | copy-start | bytes 28
  21.7 3.7 %copy-start.36 = (f32[8,8,8]{2,1,0:T(8,128)S(1)}, f32[8,8,8]{2,1,0:T(8,128)}, u32[]{:S(2)}) copy-start(f32[8,8,8]{2,1,0:T(8,128)} %param.11) | copy-start | bytes 6148
  22.8 7.2 %copy-start.34 = (s32[4,512]{1,0:T(4,128)S(1)}, s32[4,512]{1,0:T(4,128)}, u32[]{:S(2)}) copy-start(s32[4,512]{1,0:T(4,128)} %param.15) | copy-start | bytes 24580
  22.8 7.3 %copy-start.35 = (s32[4,1]{0,1:T(1,128)S(1)}, s32[4,1]{0,1:T(1,128)}, u32[]{:S(2)}) copy-start(s32[4,1]{0,1:T(1,128)} %param.16) | copy-start | bytes 52
  34.7 1.5 copy-start.5
  34.7 1.7 copy-start.6
  34.7 1.8 copy-start.7
  34.8 2.0 copy-start.8
  40.7 16.0 %collective-permute-start.6 = (f32[64,16]{0,1:T(8,128)S(1)}, f32[64,16]{0,1:T(8,128)S(1)}, u32[]{:S(2)}, u32[]{:S(2)}) collective-permute-start(f32[64,16]{0,1:T(8,128)S(1)} %get-tuple-element.85), channel_id=1, source_target_pairs={{1,0},{2,1},{3,2},{4,3},{5,4},{6,5},{7,6},{8,7},{9,8},{10,9},{11,1... | collective-permute-start | bytes 12296 | tf_op jit(solution)/shard_map/ppermute | solution.py:32
  42.7 14.1 %collective-permute-start.7 = (f32[64,16]{0,1:T(8,128)S(1)}, f32[64,16]{0,1:T(8,128)S(1)}, u32[]{:S(2)}, u32[]{:S(2)}) collective-permute-start(f32[64,16]{0,1:T(8,128)S(1)} %get-tuple-element.84), channel_id=1, source_target_pairs={{0,1},{1,2},{2,3},{3,4},{4,5},{5,6},{6,7},{7,8},{8,9},{9,10},{10,1... | collective-permute-start | bytes 12296 | tf_op jit(solution)/shard_map/ppermute | solution.py:32
  48.4 11.7 %collective-permute-start.4 = (f32[64,1,128]{2,0,1:T(8,128)S(1)}, f32[64,1,128]{2,0,1:T(8,128)S(1)}, u32[]{:S(2)}, u32[]{:S(2)}) collective-permute-start(f32[64,1,128]{2,0,1:T(8,128)S(1)} %get-tuple-element.118), channel_id=1, source_target_pairs={{0,16},{16,32},{32,48},{48,64},{64,80},{80,96},{96,112},{112,128},... | collective-permute-start | bytes 98312 | tf_op jit(solution)/shard_map/ppermute | solution.py:21
  51.3 8.8 %collective-permute-start.5 = (f32[64,1,128]{2,0,1:T(8,128)S(1)}, f32[64,1,128]{2,0,1:T(8,128)S(1)}, u32[]{:S(2)}, u32[]{:S(2)}) collective-permute-start(f32[64,1,128]{2,0,1:T(8,128)S(1)} %get-tuple-element.117), channel_id=1, source_target_pairs={{16,0},{32,16},{48,32},{64,48},{80,64},{96,80},{112,96},{128,112},... | collective-permute-start | bytes 98312 | tf_op jit(solution)/shard_map/ppermute | solution.py:24
  60.3 1.6 copy-start.17
  60.3 1.7 copy-start.24
  60.3 1.9 copy-start.25
  60.3 2.0 copy-start.26
  66.5 16.2 %collective-permute-start.10 = (f32[64,16]{0,1:T(8,128)S(1)}, f32[64,16]{0,1:T(8,128)S(1)}, u32[]{:S(2)}, u32[]{:S(2)}) collective-permute-start(f32[64,16]{0,1:T(8,128)S(1)} %get-tuple-element.83), channel_id=1, source_target_pairs={{1,0},{2,1},{3,2},{4,3},{5,4},{6,5},{7,6},{8,7},{9,8},{10,9},{11,1... | collective-permute-start | bytes 12296 | tf_op jit(solution)/shard_map/ppermute | solution.py:32
  68.4 14.3 %collective-permute-start.11 = (f32[64,16]{0,1:T(8,128)S(1)}, f32[64,16]{0,1:T(8,128)S(1)}, u32[]{:S(2)}, u32[]{:S(2)}) collective-permute-start(f32[64,16]{0,1:T(8,128)S(1)} %get-tuple-element.82), channel_id=1, source_target_pairs={{0,1},{1,2},{2,3},{3,4},{4,5},{5,6},{6,7},{7,8},{8,9},{9,10},{10,1... | collective-permute-start | bytes 12296 | tf_op jit(solution)/shard_map/ppermute | solution.py:32
  74.2 11.9 %collective-permute-start.8 = (f32[64,1,128]{2,0,1:T(8,128)S(1)}, f32[64,1,128]{2,0,1:T(8,128)S(1)}, u32[]{:S(2)}, u32[]{:S(2)}) collective-permute-start(f32[64,1,128]{2,0,1:T(8,128)S(1)} %get-tuple-element.112), channel_id=1, source_target_pairs={{0,16},{16,32},{32,48},{48,64},{64,80},{80,96},{96,112},{112,128},... | collective-permute-start | bytes 98312 | tf_op jit(solution)/shard_map/ppermute | solution.py:21
  77.6 8.5 %collective-permute-start.9 = (f32[64,1,128]{2,0,1:T(8,128)S(1)}, f32[64,1,128]{2,0,1:T(8,128)S(1)}, u32[]{:S(2)}, u32[]{:S(2)}) collective-permute-start(f32[64,1,128]{2,0,1:T(8,128)S(1)} %get-tuple-element.111), channel_id=1, source_target_pairs={{16,0},{32,16},{48,32},{64,48},{80,64},{96,80},{112,96},{128,112},... | collective-permute-start | bytes 98312 | tf_op jit(solution)/shard_map/ppermute | solution.py:24
  86.3 1.5 copy-start.28
  86.3 1.6 copy-start.29
  86.3 1.8 copy-start.30
  86.3 1.9 copy-start.31
  92.4 16.0 %collective-permute-start.14 = (f32[64,16]{0,1:T(8,128)S(1)}, f32[64,16]{0,1:T(8,128)S(1)}, u32[]{:S(2)}, u32[]{:S(2)}) collective-permute-start(f32[64,16]{0,1:T(8,128)S(1)} %get-tuple-element.81), channel_id=1, source_target_pairs={{1,0},{2,1},{3,2},{4,3},{5,4},{6,5},{7,6},{8,7},{9,8},{10,9},{11,1... | collective-permute-start | bytes 12296 | tf_op jit(solution)/shard_map/ppermute | solution.py:32
  94.3 14.1 %collective-permute-start.15 = (f32[64,16]{0,1:T(8,128)S(1)}, f32[64,16]{0,1:T(8,128)S(1)}, u32[]{:S(2)}, u32[]{:S(2)}) collective-permute-start(f32[64,16]{0,1:T(8,128)S(1)} %get-tuple-element.80), channel_id=1, source_target_pairs={{0,1},{1,2},{2,3},{3,4},{4,5},{5,6},{6,7},{7,8},{8,9},{9,10},{10,1... | collective-permute-start | bytes 12296 | tf_op jit(solution)/shard_map/ppermute | solution.py:32
  100.1 11.7 %collective-permute-start.12 = (f32[64,1,128]{2,0,1:T(8,128)S(1)}, f32[64,1,128]{2,0,1:T(8,128)S(1)}, u32[]{:S(2)}, u32[]{:S(2)}) collective-permute-start(f32[64,1,128]{2,0,1:T(8,128)S(1)} %get-tuple-element.106), channel_id=1, source_target_pairs={{0,16},{16,32},{32,48},{48,64},{64,80},{80,96},{96,112},{112,128},... | collective-permute-start | bytes 98312 | tf_op jit(solution)/shard_map/ppermute | solution.py:21
  102.4 9.4 %collective-permute-start.13 = (f32[64,1,128]{2,0,1:T(8,128)S(1)}, f32[64,1,128]{2,0,1:T(8,128)S(1)}, u32[]{:S(2)}, u32[]{:S(2)}) collective-permute-start(f32[64,1,128]{2,0,1:T(8,128)S(1)} %get-tuple-element.105), channel_id=1, source_target_pairs={{16,0},{32,16},{48,32},{64,48},{80,64},{96,80},{112,96},{128,112},... | collective-permute-start | bytes 98312 | tf_op jit(solution)/shard_map/ppermute | solution.py:24
  111.9 1.5 copy-start.20
  112.0 1.6 copy-start.21
  112.0 1.8 copy-start.22
  112.0 1.9 copy-start.23
  115.9 14.3 %collective-permute-start.18 = (f32[64,16]{0,1:T(8,128)S(1)}, f32[64,16]{0,1:T(8,128)S(1)}, u32[]{:S(2)}, u32[]{:S(2)}) collective-permute-start(f32[64,16]{0,1:T(8,128)S(1)} %get-tuple-element.79), channel_id=1, source_target_pairs={{1,0},{2,1},{3,2},{4,3},{5,4},{6,5},{7,6},{8,7},{9,8},{10,9},{11,1... | collective-permute-start | bytes 12296 | tf_op jit(solution)/shard_map/ppermute | solution.py:32
  117.8 12.6 %collective-permute-start.19 = (f32[64,16]{0,1:T(8,128)S(1)}, f32[64,16]{0,1:T(8,128)S(1)}, u32[]{:S(2)}, u32[]{:S(2)}) collective-permute-start(f32[64,16]{0,1:T(8,128)S(1)} %get-tuple-element.78), channel_id=1, source_target_pairs={{0,1},{1,2},{2,3},{3,4},{4,5},{5,6},{6,7},{7,8},{8,9},{9,10},{10,1... | collective-permute-start | bytes 12296 | tf_op jit(solution)/shard_map/ppermute | solution.py:32
  123.6 7.1 %collective-permute-start.16 = (f32[64,1,128]{2,0,1:T(8,128)S(1)}, f32[64,1,128]{2,0,1:T(8,128)S(1)}, u32[]{:S(2)}, u32[]{:S(2)}) collective-permute-start(f32[64,1,128]{2,0,1:T(8,128)S(1)} %get-tuple-element.97), channel_id=1, source_target_pairs={{16,0},{32,16},{48,32},{64,48},{80,64},{96,80},{112,96},{128,112},... | collective-permute-start | bytes 98312 | tf_op jit(solution)/shard_map/ppermute | solution.py:24
  127.8 7.7 %collective-permute-start.17 = (f32[64,1,128]{2,0,1:T(8,128)S(1)}, f32[64,1,128]{2,0,1:T(8,128)S(1)}, u32[]{:S(2)}, u32[]{:S(2)}) collective-permute-start(f32[64,1,128]{2,0,1:T(8,128)S(1)} %get-tuple-element.98), channel_id=1, source_target_pairs={{0,16},{16,32},{32,48},{48,64},{64,80},{80,96},{96,112},{112,128},... | collective-permute-start | bytes 98312 | tf_op jit(solution)/shard_map/ppermute | solution.py:21
  168.6 59.1 %copy-start.32 = (f32[32,4096]{1,0:T(8,128)S(1)}, f32[32,4096]{1,0:T(8,128)}, u32[]{:S(2)}) copy-start(f32[32,4096]{1,0:T(8,128)} %param.12) | copy-start | bytes 1572868
  230.0 8.2 %copy-start.10 = (f32[32,4096]{1,0:T(8,128)}, f32[32,4096]{1,0:T(8,128)S(1)}, u32[]{:S(2)}) copy-start(f32[32,4096]{1,0:T(8,128)S(1)} %fusion.1) | copy-start | bytes 1572868
  239.8 15.3 %collective-permute-start.20 = (f32[32,512]{1,0:T(8,128)S(1)}, f32[32,512]{1,0:T(8,128)S(1)}, u32[]{:S(2)}, u32[]{:S(2)}) collective-permute-start(f32[32,512]{1,0:T(8,128)S(1)} %get-tuple-element.127), channel_id=1, source_target_pairs={{0,16},{16,32},{32,48},{48,64},{64,80},{80,96},{96,112},{112,128},... | collective-permute-start | bytes 196616 | tf_op jit(solution)/shard_map/ppermute | solution.py:32
  241.7 13.4 %collective-permute-start.21 = (f32[32,512]{1,0:T(8,128)S(1)}, f32[32,512]{1,0:T(8,128)S(1)}, u32[]{:S(2)}, u32[]{:S(2)}) collective-permute-start(f32[32,512]{1,0:T(8,128)S(1)} %get-tuple-element.130), channel_id=1, source_target_pairs={{16,0},{32,16},{48,32},{64,48},{80,64},{96,80},{112,96},{128,112},... | collective-permute-start | bytes 196616 | tf_op jit(solution)/shard_map/ppermute | solution.py:32
  248.1 7.0 %collective-permute-start.22 = (f32[32,512]{1,0:T(8,128)S(1)}, f32[32,512]{1,0:T(8,128)S(1)}, u32[]{:S(2)}, u32[]{:S(2)}) collective-permute-start(f32[32,512]{1,0:T(8,128)S(1)} %get-tuple-element.129), channel_id=1, source_target_pairs={{0,1},{1,2},{2,3},{3,4},{4,5},{5,6},{6,7},{7,8},{8,9},{9,10},{10,1... | collective-permute-start | bytes 196616 | tf_op jit(solution)/shard_map/ppermute | solution.py:32
  252.0 7.7 %collective-permute-start.23 = (f32[32,512]{1,0:T(8,128)S(1)}, f32[32,512]{1,0:T(8,128)S(1)}, u32[]{:S(2)}, u32[]{:S(2)}) collective-permute-start(f32[32,512]{1,0:T(8,128)S(1)} %get-tuple-element.128), channel_id=1, source_target_pairs={{1,0},{2,1},{3,2},{4,3},{5,4},{6,5},{7,6},{8,7},{9,8},{10,9},{11,1... | collective-permute-start | bytes 196616 | tf_op jit(solution)/shard_map/ppermute | solution.py:32
  (14 other events, 16.9 us)
where the time goes:
time: 261 us; the launch traced here: 260 us
  starting transfers between devices  93.9 us (36%)
  local copies, waits for them, and re-layouts  77.8 us (30%)
  other arithmetic  71.9 us (28%)
  waiting for transfers between devices  9.47 us (4%)
  matrix products  4.97 us (2%)
    reduce_sum x1, other arithmetic, on_device(): sampled = jnp.sum(fetched * picker[None], axis=2)  59.1 us
    ppermute x14, starting transfers between devices, shifted(): lax.ppermute(value, axis, [(source, source + steps) for source in range(i...  52.5 us
    gather x1, local copies, waits for them, and re-layouts, on_device(): fetched = jnp.take(row_table, row_of, axis=1)  30.3 us
    ppermute x5, starting transfers between devices, with_halo(): lax.ppermute(lax.slice_in_dim(block, 0, width, axis=dim), axis, backward)  25.8 us
    ppermute x5, starting transfers between devices, with_halo(): lax.ppermute(lax.slice_in_dim(block, block.shape[dim] - width, None, axis...  15.7 us
    unnamed x81, local copies, waits for them, and re-layouts  9.65 us
    gather x2, local copies, waits for them, and re-layouts, on_device(): jnp.take(moved, send_list.reshape(-1), axis=1)  9.12 us
    broadcast_in_dim x9, local copies, waits for them, and re-layouts, with_south(): return jnp.concatenate([column[:, :, None], centre[:, :, :-1]], 2)  8.62 us
  transfers between devices with their start and end apart: 24, of which 2 were waited for; matrix products, arithmetic and copies ran while one was open for 10% of the time, Pallas kernels for 0%

commit v1 on v0

v1 whole, which is shorter than its diff:
```python
import functools

import jax
import jax.numpy as jnp
from jax import lax
from jax.experimental import pallas as pl
from jax.experimental.pallas import tpu as pltpu
from jax.sharding import PartitionSpec as P

ITERS = 4
LZ, CX, CY = 64, 16, 128
HALF = CY // 2
WIDE = ITERS + 1
EXT = CX + 2 * WIDE
ROWS = HALF + 16
PAD = ROWS + 16
NX, NY = 256, 2048
NSIDE = WIDE - 1
ESEND = WIDE * HALF + NSIDE * HALF + 2 * NSIDE * 8
STEP = 0.25
F32 = jnp.float32
VMEM = pl.BlockSpec(memory_space=pltpu.VMEM)
SMEM = pl.BlockSpec(memory_space=pltpu.SMEM)


def lanes(shape):
    return lax.broadcasted_iota(jnp.int32, shape, len(shape) - 1)


def swap(v):
    return pltpu.roll(v, 64, 1)


def turn_kernel(h_ref, s_ref, ht_ref, st_ref, nlo_ref, nhi_ref):
    low = lanes((8, 128)) < 64

    def turned(ref, x):
        t = ref[pl.ds(x, LZ, stride=CX), :].T
        return jnp.concatenate([t[:HALF], t[HALF:]], axis=1)

    for x in range(CX):
        h, s = turned(h_ref, x), turned(s_ref, x)
        ht_ref[x] = h
        st_ref[x] = s
        nlo_ref[x] = jnp.where(low, swap(h[HALF - 8 :]), s[HALF - 8 :])
        nhi_ref[x] = jnp.where(low, h[:8], swap(s[:8]))


def pack_kernel(ht_ref, st_ref, nlo_ref, nhi_ref, elo_ref, ehi_ref):
    for ref, at, at_s in ((elo_ref, CX - WIDE, CX - NSIDE), (ehi_ref, 0, 0)):
        row = 0
        for source, start, count in (
            (ht_ref, at, WIDE),
            (st_ref, at_s, NSIDE),
            (nlo_ref, at_s, NSIDE),
            (nhi_ref, at_s, NSIDE),
        ):
            height = source.shape[1]
            for i in range(count):
                ref[row : row + height] = source[start + i]
                row += height


def cond_kernel(w_ref, out_ref, base_ref, xrow_ref):
    start_x = lax.axis_index("east") * CX - WIDE
    start_y = lax.axis_index("north") * CY - 8
    lane = lanes((ROWS, 128))
    row = lax.broadcasted_iota(jnp.int32, (ROWS, 128), 0)
    y = start_y + row + (lane // 64) * HALF
    inside_y = (y >= 0) & (y < NY)
    coord = y.astype(F32) + 0.5
    base = jnp.broadcast_to(w_ref[0:1, :], (ROWS, 128))
    for b in range(1, 8):
        base = base + w_ref[b : b + 1, :] * jnp.cos(jnp.pi * float(b) * coord / NY)
    base_ref[...] = base
    lane_x = lanes((32, 128))
    x = start_x + lax.broadcasted_iota(jnp.int32, (32, 128), 0)
    order = (lane_x % 8).astype(F32)
    xrow_ref[...] = jnp.cos(jnp.pi * order * (x.astype(F32) + 0.5) / NX)
    lane_z = lanes((128, 128))
    mode = lax.broadcasted_iota(jnp.int32, (128, 128), 0)
    order = ((mode % 64) // 8).astype(F32)
    table = jnp.cos(jnp.pi * order * ((lane_z % 64).astype(F32) + 0.5) / LZ)
    table = jnp.where(mode // 64 == lane_z // 64, table, 0.0)

    def step(i, carry):
        scaled = base_ref[...] * xrow_ref[pl.ds(i, 1), :]
        log = jnp.dot(scaled, table, precision=lax.Precision.HIGHEST, preferred_element_type=F32)
        xg = start_x + i
        live = inside_y & (xg >= 0) & (xg < NX)
        out_ref[i] = jnp.where(live, 0.5 * jnp.exp(log), 0.0)
        return carry

    lax.fori_loop(0, EXT, step, 0)


def rel(h):
    return jnp.exp(jnp.minimum(h, 0.0))


def sweep_kernel(
    ht_ref, st_ref, nlo_ref, nhi_ref, elo_ref, ehi_ref, cond_ref,
    heads_ref, table_ref,
    ha, hb, ka, kb, sto_ref, src_ref, count_ref, mask_ref,
):
    east = lax.axis_index("east")
    north = lax.axis_index("north")
    low = lanes((8, 128)) < 64
    has_south, has_north = north > 0, north < 15
    has_west, has_east = east > 0, east < 15
    lane = lanes((ROWS, 128))
    row = lax.broadcasted_iota(jnp.int32, (ROWS, 128), 0)
    y = north * CY - 8 + row + (lane // 64) * HALF
    z = lane % 64
    one = lambda c: c.astype(F32)
    count_ref[...] = one(y > 0) + one(y < NY - 1) + one(z > 0) + one(z < LZ - 1)
    mask_ref[...] = one((y >= 0) & (y < NY))
    zl = lanes((8, 128)) % 64
    up_mask = one(zl < LZ - 1)
    down_mask = one(zl > 0)
    gravity = up_mask - down_mask
    zero = jnp.zeros((8, 128), F32)
    for buf in (ha, hb, ka, kb):
        for i in range(EXT):
            buf[i, 0:8] = zero
            buf[i, PAD - 8 : PAD] = zero

    def start(xi, h, s, nlo, nhi, with_source):
        nlo = jnp.where(has_south, nlo, 0.0)
        nhi = jnp.where(has_north, nhi, 0.0)
        pieces = [(0, jnp.where(low, nlo, swap(h[HALF - 8 :])))]
        pieces += [(8 + r, h[r : r + 8]) for r in range(0, HALF, 8)]
        pieces += [(ROWS - 8, swap(jnp.where(low, nhi, h[:8])))]
        if with_source:
            sources = [swap(jnp.where(low, s[HALF - 8 :], nlo))]
            sources += [s[r : r + 8] for r in range(0, HALF, 8)]
            sources += [jnp.where(low, swap(s[:8]), nhi)]
        for n, (r, piece) in enumerate(pieces):
            relative = rel(piece)
            ha[xi, 8 + r : 16 + r] = piece
            ka[xi, 8 + r : 16 + r] = cond_ref[xi, r : r + 8] * relative
            if with_source:
                sto = 0.5 + 0.5 * relative
                sto_ref[xi, r : r + 8] = sto
                src_ref[xi, r : r + 8] = sto * piece + sources[n]

    def own(x, carry):
        start(x + WIDE, ht_ref[x], st_ref[x], nlo_ref[x], nhi_ref[x], True)
        return carry

    lax.fori_loop(0, CX, own, 0)
    for ref, valid, first, flip in ((elo_ref, has_west, 0, 0), (ehi_ref, has_east, EXT - WIDE, 1)):
        for i in range(WIDE):
            h = jnp.where(valid, ref[i * HALF : (i + 1) * HALF], 0.0)
            j = i if flip else i - 1
            if 0 <= j < NSIDE:
                s_at = WIDE * HALF + j * HALF
                c_at = (WIDE + NSIDE) * HALF + j * 8
                s = jnp.where(valid, ref[s_at : s_at + HALF], 0.0)
                nlo = jnp.where(valid, ref[c_at : c_at + 8], 0.0)
                nhi = jnp.where(valid, ref[c_at + NSIDE * 8 : c_at + NSIDE * 8 + 8], 0.0)
                start(first + i, h, s, nlo, nhi, True)
            else:
                start(first + i, h, None, zero, zero, False)

    hin, kin, hout, kout = ha, ka, hb, kb
    for number in range(1, ITERS + 1):

        def sweep(xi, carry, hin=hin, kin=kin, hout=hout, kout=kout):
            xg = east * CX - WIDE + xi
            along_x = one(xg > 0) + one(xg < NX - 1)
            in_x = one((xg >= 0) & (xg < NX))
            for r in range(0, ROWS, 8):
                a = r + 8
                h, k = hin[xi, a : a + 8], kin[xi, a : a + 8]
                hu = pltpu.roll(h, 127, 1) * up_mask
                ku = pltpu.roll(k, 127, 1) * up_mask
                hd = pltpu.roll(h, 1, 1) * down_mask
                kd = pltpu.roll(k, 1, 1) * down_mask
                hn, kn = hin[xi, a + 1 : a + 9], kin[xi, a + 1 : a + 9]
                hs, ks = hin[xi, a - 1 : a + 7], kin[xi, a - 1 : a + 7]
                he, ke = hin[xi + 1, a : a + 8], kin[xi + 1, a : a + 8]
                hw, kw = hin[xi - 1, a : a + 8], kin[xi - 1, a : a + 8]
                sum_h = ((hu + hd) + (hn + hs)) + ((he + hw) + gravity)
                sum_k = ((ku + kd) + (kn + ks)) + (ke + kw)
                flux = ((ku * hu + kd * hd) + (kn * hn + ks * hs)) + (ke * he + kw * hw)
                top = (src_ref[xi, r : r + 8] + k * sum_h) + (flux + (ku - kd))
                below = (count_ref[r : r + 8] + along_x) * k + (sto_ref[xi, r : r + 8] + sum_k)
                inv = pl.reciprocal(below, approx=True)
                inv = inv * (2.0 - below * inv)
                inv = inv * (2.0 - below * inv)
                new = top * inv * in_x
                if r == 0 or r == ROWS - 8:
                    new = new * mask_ref[r : r + 8]
                hout[xi, a : a + 8] = new
                kout[xi, a : a + 8] = cond_ref[xi, r : r + 8] * rel(new)
            return carry

        lax.fori_loop(number, EXT - number, sweep, 0)
        hin, kin, hout, kout = hout, kout, hin, kin

    up2, down2 = up_mask, down_mask
    up2 = jnp.concatenate([up_mask, up_mask], axis=0)
    down2 = jnp.concatenate([down_mask, down_mask], axis=0)

    def velocity(x, carry):
        xi = x + WIDE
        for r in range(0, HALF, 16):
            a = r + 16
            h, k = hin[xi, a : a + 16], kin[xi, a : a + 16]
            heads_ref[x, r : r + 16] = h
            hu = pltpu.roll(h, 127, 1) * up2
            hd = pltpu.roll(h, 1, 1) * down2
            flow_x = -k * (hin[xi + 1, a : a + 16] - hin[xi - 1, a : a + 16])
            flow_y = -k * (hin[xi, a + 1 : a + 17] - hin[xi, a - 1 : a + 15])
            flow_z = -k * ((hu - hd) + 2.0)
            for c, flow in enumerate((flow_x, flow_y, flow_z)):
                big = flow.astype(jnp.bfloat16)
                at = pl.ds(pl.multiple_of(c * CX * HALF + x * HALF + r, 16), 16)
                table_ref[at, 0:128] = big
                table_ref[at, 128:256] = (flow - big.astype(F32)).astype(jnp.bfloat16)
        return carry

    lax.fori_loop(0, CX, velocity, 0)


def onehot_pair(index):
    hot = lax.broadcasted_iota(jnp.int32, (128, index.shape[1]), 0) == index
    hot = jnp.where(hot, 1.0, 0.0).astype(jnp.bfloat16)
    return jnp.concatenate([hot, hot], axis=0)


def choose(get, first, count, bits):
    if count == 1:
        return get(first)
    level = count.bit_length() - 2
    half = count // 2
    low = choose(get, first, half, bits)
    high = choose(get, first + half, half, bits)
    return jnp.where(bits[level], high, low)


BLOCK = 256


def sample_kernel(table_ref, cell_ref, rec_ref, couple_ref, list_ref, count_ref, moved_ref, send_ref, pick_ref):
    def block(n, carry):
        cell = jnp.concatenate([cell_ref[pl.ds(n * 2, 1), :], cell_ref[pl.ds(n * 2 + 1, 1), :]], axis=1)
        layer, i, j = cell >> 11, (cell >> 7) & 15, cell & 127
        lane = (j >> 6) * 64 + layer
        row = i * 64 + (j & 63)
        got = jnp.dot(table_ref[...], onehot_pair(lane), preferred_element_type=F32)
        row8 = jnp.broadcast_to(row, (8, BLOCK))
        bits = [(row8 & (8 << b)) != 0 for b in range(7)]
        mine = lax.broadcasted_iota(jnp.int32, (8, BLOCK), 0) == (row8 & 7)
        at = pl.ds(pl.multiple_of(n * BLOCK, BLOCK), BLOCK)
        total = rec_ref[:, at]
        for c in range(3):
            picked = choose(lambda g: got[c * 1024 + g * 8 : c * 1024 + g * 8 + 8], 0, 128, bits)
            sampled = jnp.sum(jnp.where(mine, picked, 0.0), axis=0, keepdims=True)
            weight = couple_ref[c * 32 : (c + 1) * 32, :]
            total = total + jnp.concatenate([weight, weight], axis=1) * sampled
        moved_ref[:, at] = total
        for half in range(2):
            part = total[:, half * 128 : (half + 1) * 128]
            big = part.astype(jnp.bfloat16)
            rows = pl.ds(pl.multiple_of((n * 2 + half) * 32, 32), 32)
            pick_ref[rows, 0:128] = big
            pick_ref[rows, 128:256] = (part - big.astype(F32)).astype(jnp.bfloat16)
        return carry

    lax.fori_loop(0, 4096 // BLOCK, block, 0)
    for d in range(4):
        for part in range(2):
            index = list_ref[d : d + 1, part * BLOCK : (part + 1) * BLOCK]
            got = jnp.dot(pick_ref[...], onehot_pair(index & 127), preferred_element_type=F32)
            block_of = jnp.broadcast_to(index >> 7, (32, BLOCK))
            bits = [(block_of & (1 << b)) != 0 for b in range(5)]
            picked = choose(lambda g: got[g * 32 : (g + 1) * 32], 0, 32, bits)
            live = lanes((32, BLOCK)) + part * BLOCK < count_ref[d, 0]
            send_ref[d, :, part * BLOCK : (part + 1) * BLOCK] = jnp.where(live, picked, 0.0)


def back_kernel(ht_ref, out_ref):
    for x in range(CX):
        t = ht_ref[x].T
        out_ref[pl.ds(x, LZ, stride=CX), :] = jnp.concatenate([t[:LZ], t[LZ:]], axis=1)


def arrive_kernel(a_ref, b_ref, c_ref, d_ref, out_ref):
    east, north = lax.axis_index("east"), lax.axis_index("north")
    for d, (ref, valid) in enumerate(
        ((a_ref, east > 0), (b_ref, east < 15), (c_ref, north > 0), (d_ref, north < 15))
    ):
        out_ref[d] = jnp.where(valid, ref[...], 0.0)


def call(kernel, outs, ins, scratch=(), limit=None, specs=None, cost=None):
    params = {} if limit is None else dict(compiler_params=pltpu.CompilerParams(vmem_limit_bytes=limit))
    return pl.pallas_call(
        kernel,
        out_shape=[jax.ShapeDtypeStruct(s, t) for s, t in outs],
        in_specs=specs or [VMEM] * len(ins),
        out_specs=[VMEM] * len(outs),
        scratch_shapes=list(scratch),
        cost_estimate=cost,
        **params,
    )(*ins)


def ring(value, axis, steps):
    count = lax.axis_size(axis)
    return lax.ppermute(value, axis, [(i, (i + steps) % count) for i in range(count)])


def mode_weights(mode_coeffs):
    order = jnp.arange(8).astype(F32)
    spectrum = 1.0 / (
        1.0 + (order[:, None, None] ** 2 + order[None, :, None] ** 2 + order[None, None, :] ** 2) / 4.0
    )
    return mode_coeffs * jnp.sqrt(spectrum) * (1.0 / jnp.sqrt(jnp.sum(spectrum)))


def on_device(head_old, source, mode_coeffs, records, cell_index, coupling, send_list, send_count):
    flat = (LZ * CX, CY)
    tile = ((CX, HALF, 128), F32)
    side = ((CX, 8, 128), F32)
    ht, st, n_up, n_down = call(
        turn_kernel, [tile, tile, side, side], [head_old.reshape(flat), source.reshape(flat)]
    )
    nlo = ring(n_up, "north", 1)
    nhi = ring(n_down, "north", -1)
    edge = ((ESEND, 128), F32)
    e_up, e_down = call(pack_kernel, [edge, edge], [ht, st, nlo, nhi])
    elo = ring(e_up, "east", 1)
    ehi = ring(e_down, "east", -1)
    weights = jnp.transpose(mode_weights(mode_coeffs), (2, 0, 1)).reshape(8, 64)
    weights = jnp.concatenate([weights, weights], axis=1)
    (cond,) = call(
        cond_kernel,
        [((EXT, ROWS, 128), F32)],
        [weights],
        [pltpu.VMEM((ROWS, 128), F32), pltpu.VMEM((32, 128), F32)],
    )
    buf = pltpu.VMEM((EXT, PAD, 128), F32)
    ext = pltpu.VMEM((EXT, ROWS, 128), F32)
    plane = pltpu.VMEM((ROWS, 128), F32)
    heads, table = call(
        sweep_kernel,
        [tile, ((3 * CX * HALF, 256), jnp.bfloat16)],
        [ht, st, nlo, nhi, elo, ehi, cond],
        [buf, buf, buf, buf, ext, ext, plane, plane],
        limit=48 * 2**20,
    )
    couple = jnp.broadcast_to((STEP * coupling)[:, :, None], (3, 32, 128)).reshape(96, 128)
    moved, buffers = call(
        sample_kernel,
        [((32, 4096), F32), ((4, 32, 512), F32)],
        [table, cell_index.reshape(32, 128), records, couple, send_list, send_count],
        [pltpu.VMEM((1024, 256), jnp.bfloat16)],
        limit=48 * 2**20,
        specs=[VMEM] * 5 + [SMEM],
    )
    came = [
        ring(buffers[0], "east", 1),
        ring(buffers[1], "east", -1),
        ring(buffers[2], "north", 1),
        ring(buffers[3], "north", -1),
    ]
    (heads_out,) = call(back_kernel, [(flat, F32)], [heads])
    (arrivals,) = call(arrive_kernel, [((4, 32, 512), F32)], came)
    return (heads_out.reshape(LZ, CX, CY), moved, arrivals)


def solution(mesh):
    return jax.shard_map(
        on_device,
        mesh=mesh,
        in_specs=(
            P(None, "east", "north"),
            P(None, "east", "north"),
            P(),
            P(None, ("east", "north")),
            P(("east", "north")),
            P(),
            P(None, ("east", "north")),
            P(None, ("east", "north")),
        ),
        out_specs=(
            P(None, "east", "north"),
            P(None, ("east", "north")),
            P(None, None, ("east", "north")),
        ),
        check_vma=False,
    )
```

time: 261 us -> 82.3 us (0.32)
  the two profiles are of different devices: /device:TPU:31 before, /device:TPU:7 now
where the time goes in v1:
time: 82.3 us; the launch traced here: 81.9 us
  Pallas kernels  44.4 us (54%)
  starting transfers between devices  19 us (23%)
  waiting for transfers between devices  10 us (12%)
  local copies, waits for them, and re-layouts  4.52 us (5%)
  other arithmetic  2.37 us (3%)
  between operations  1.51 us (2%)
    pallas_call x7, Pallas kernels, call(): pl.pallas_call(kernel, out_shape=[jax.ShapeDtypeStruct(s, t) for s, t in...  44.4 us
    ppermute x8, starting transfers between devices, ring(): lax.ppermute(value, axis, [(i, (i + steps) % count) for i in range(count)])  19 us
    ppermute x8, waiting for transfers between devices, ring(): lax.ppermute(value, axis, [(i, (i + steps) % count) for i in range(count)])  10 us
    unnamed x35, local copies, waits for them, and re-layouts  4.29 us
  transfers between devices with their start and end apart: 8, of which 3 were waited for; matrix products, arithmetic and copies ran while one was open for 3% of the time, Pallas kernels for 13%

profile of v1, /device:TPU:7, one launch (start us, length us, event | category | flops | bytes accessed | tf_op | source)
XLA Modules:
  0.0 81.9 jit_solution(9827335714447340993)
XLA Ops:
  0.6 0.0 copy-start.15
  0.6 0.0 copy-start.16
  0.7 3.8 %shard_map.103 = (f32[16,64,128]{2,1,0:T(8,128)}, f32[16,64,128]{2,1,0:T(8,128)}, f32[16,8,128]{2,1,0:T(8,128)}, f32[16,8,128]{2,1,0:T(8,128)}) custom-call(f32[1024,128]{1,0:T(8,128)} %bitcast.17, f32[1024,128]{1,0:T(8,128)} %bitcast.18), custom_call_target="tpu_custom_call" | custom-call | tf_op jit(solution)/shard_map/pallas_call | solution.py:300
  4.5 2.2 %collective-permute-start = (f32[16,8,128]{2,1,0:T(8,128)}, f32[16,8,128]{2,1,0:T(8,128)S(1)}, u32[]{:S(2)}, u32[]{:S(2)}) collective-permute-start(f32[16,8,128]{2,1,0:T(8,128)} %get-tuple-element.15), channel_id=1, source_target_pairs={{0,1},{1,2},{2,3},{3,4},{4,5},{5,6},{6,7},{7,8},{8,9},{9,10},{10,1... | collective-permute-start | bytes 196616 | tf_op jit(solution)/shard_map/ppermute | solution.py:313
  6.7 0.0 collective-permute-start.1
  6.7 0.1 broadcast_add_fusion
  6.7 0.8 fusion
  8.3 0.9 %multiply_bitcast_fusion = f32[8,64]{0,1:T(8,128)S(1)} fusion(f32[8,8,8]{2,1,0:T(8,128)} %param.10, f32[]{:T(128)S(6)} %sqrt.7, f32[8]{0:T(128)S(1)} %convert_multiply_fusion, f32[8,8]{1,0:T(8,128)S(1)} %broadcast_add_fusion), kind=kLoop, calls=%fused_computation.4 | loop fusion | flops 3072 | bytes 4388 | tf_op jit(solution)/shard_map/reshape | solution.py:337
  9.1 0.1 copy.13
  9.2 0.0 collective-permute-done.nlo_ref
  9.2 3.5 %collective-permute-done.1.nhi_ref = f32[16,8,128]{2,1,0:T(8,128)S(1)} collective-permute-done((f32[16,8,128]{2,1,0:T(8,128)}, f32[16,8,128]{2,1,0:T(8,128)S(1)}, u32[]{:S(2)}, u32[]{:S(2)}) %collective-permute-start.1) | collective-permute-done | bytes 65568 | tf_op jit(solution)/shard_map/ppermute | solution.py:313
  12.7 0.0 copy-done.5
  12.7 0.6 copy-done.7
  13.3 2.1 %shard_map.104 = (f32[640,128]{1,0:T(8,128)}, f32[640,128]{1,0:T(8,128)}) custom-call(f32[16,64,128]{2,1,0:T(8,128)} %get-tuple-element.13.ht_ref, f32[16,64,128]{2,1,0:T(8,128)} %get-tuple-element.14.st_ref, f32[16,8,128]{2,1,0:T(8,128)} %copy-done.5, f32[16,8,128]{2,1,0:T(8,128)} %copy-done.7), custom_call_target="tpu_custom_call" | custom-call | tf_op jit(solution)/shard_map/pallas_call | solution.py:300
  15.4 3.0 %collective-permute-start.2 = (f32[640,128]{1,0:T(8,128)}, f32[640,128]{1,0:T(8,128)S(1)}, u32[]{:S(2)}, u32[]{:S(2)}) collective-permute-start(f32[640,128]{1,0:T(8,128)} %get-tuple-element.17), channel_id=1, source_target_pairs={{0,16},{16,32},{32,48},{48,64},{64,80},{80,96},{96,112},{112,128},... | collective-permute-start | bytes 983048 | tf_op jit(solution)/shard_map/ppermute | solution.py:313
  18.4 4.6 %collective-permute-start.3 = (f32[640,128]{1,0:T(8,128)}, f32[640,128]{1,0:T(8,128)S(1)}, u32[]{:S(2)}, u32[]{:S(2)}) collective-permute-start(f32[640,128]{1,0:T(8,128)} %get-tuple-element.18), channel_id=1, source_target_pairs={{0,240},{16,0},{32,16},{48,32},{64,48},{80,64},{96,80},{112,96},{1... | collective-permute-start | bytes 983048 | tf_op jit(solution)/shard_map/ppermute | solution.py:313
  22.9 0.7 pad_maximum_fusion.w_ref
  23.6 8.2 %shard_map.105.cond_ref = f32[26,80,128]{2,1,0:T(8,128)} custom-call(f32[8,128]{1,0:T(8,128)} %pad_maximum_fusion.w_ref), custom_call_target="tpu_custom_call" | custom-call | tf_op jit(solution)/shard_map/pallas_call | solution.py:300
  31.8 0.0 copy-done.15
  31.8 0.1 broadcast_in_dim.4
  31.9 0.0 copy-done.16
  31.9 0.1 copy.12.count_ref
  32.0 0.0 collective-permute-done.2.elo_ref
  32.0 3.1 %collective-permute-done.3.ehi_ref = f32[640,128]{1,0:T(8,128)S(1)} collective-permute-done((f32[640,128]{1,0:T(8,128)}, f32[640,128]{1,0:T(8,128)S(1)}, u32[]{:S(2)}, u32[]{:S(2)}) %collective-permute-start.3) | collective-permute-done | bytes 327712 | tf_op jit(solution)/shard_map/ppermute | solution.py:313
  35.2 0.0 copy-done.1
  35.2 0.0 copy-done.2
  35.2 1.2 %copy-done = f32[26,80,128]{2,1,0:T(8,128)S(1)} copy-done((f32[26,80,128]{2,1,0:T(8,128)S(1)}, f32[26,80,128]{2,1,0:T(8,128)}, u32[]{:S(2)}) %copy-start) | copy-done | bytes 1064984
  36.4 0.8 %copy-done.6 = f32[16,8,128]{2,1,0:T(8,128)S(1)} copy-done((f32[16,8,128]{2,1,0:T(8,128)S(1)}, f32[16,8,128]{2,1,0:T(8,128)}, u32[]{:S(2)}) %copy-start.6) | copy-done | bytes 65560
  37.2 0.8 %copy-done.8 = f32[16,8,128]{2,1,0:T(8,128)S(1)} copy-done((f32[16,8,128]{2,1,0:T(8,128)S(1)}, f32[16,8,128]{2,1,0:T(8,128)}, u32[]{:S(2)}) %copy-start.8) | copy-done | bytes 65560
  38.1 14.7 %shard_map.106 = (f32[16,64,128]{2,1,0:T(8,128)S(1)}, bf16[3072,256]{1,0:T(8,128)(2,1)S(1)}) custom-call(f32[16,64,128]{2,1,0:T(8,128)S(1)} %copy-done.1, f32[16,64,128]{2,1,0:T(8,128)S(1)} %copy-done.2, f32[16,8,128]{2,1,0:T(8,128)S(1)} %copy-done.6, f32[16,8,128]{2,1,0:T(8,128)S(1)} %copy-done.8, f32[640,128]{1,0:T(8,128)S(1)} %collective-permute-done.2.elo_ref, ...), custom_call_target="tpu_custom_call" | custom-call | tf_op jit(solution)/shard_map/pallas_call | solution.py:300
  52.8 0.0 copy-start.4
  52.8 0.1 broadcast_in_dim.5.couple_ref
  52.9 0.0 copy-done.3
  52.9 0.0 copy-done.9
  52.9 11.6 %shard_map.108 = (f32[32,4096]{1,0:T(8,128)}, f32[4,32,512]{2,1,0:T(8,128)S(1)}) custom-call(bf16[3072,256]{1,0:T(8,128)(2,1)S(1)} %get-tuple-element.20.table_ref, s32[32,128]{1,0:T(8,128)S(1)} %bitcast.16, f32[32,4096]{1,0:T(8,128)S(1)} %copy-done.3, f32[96,128]{1,0:T(8,128)S(1)} %broadcast_in_dim.5.couple_ref, s32[4,512]{1,0:T(4,128)S(1)} %copy-done.10, ...), custom_call_target="tpu_custom_call" | custom-call | tf_op jit(solution)/shard_map/pallas_call | solution.py:300
  64.5 3.6 %collective-permute-start.4 = (f32[32,512]{1,0:T(8,128)S(1)}, f32[32,512]{1,0:T(8,128)S(1)}, u32[]{:S(2)}, u32[]{:S(2)}) collective-permute-start(f32[32,512]{1,0:T(8,128)S(1)} %get-tuple-element.26), channel_id=1, source_target_pairs={{0,16},{16,32},{32,48},{48,64},{64,80},{80,96},{96,112},{112,128},... | collective-permute-start | bytes 196616 | tf_op jit(solution)/shard_map/ppermute | solution.py:313
  68.1 2.2 %collective-permute-start.5 = (f32[32,512]{1,0:T(8,128)S(1)}, f32[32,512]{1,0:T(8,128)S(1)}, u32[]{:S(2)}, u32[]{:S(2)}) collective-permute-start(f32[32,512]{1,0:T(8,128)S(1)} %get-tuple-element.25), channel_id=1, source_target_pairs={{0,240},{16,0},{32,16},{48,32},{64,48},{80,64},{96,80},{112,96},{1... | collective-permute-start | bytes 196616 | tf_op jit(solution)/shard_map/ppermute | solution.py:313
  70.3 3.5 %collective-permute-start.6 = (f32[32,512]{1,0:T(8,128)S(1)}, f32[32,512]{1,0:T(8,128)S(1)}, u32[]{:S(2)}, u32[]{:S(2)}) collective-permute-start(f32[32,512]{1,0:T(8,128)S(1)} %get-tuple-element.24), channel_id=1, source_target_pairs={{0,1},{1,2},{2,3},{3,4},{4,5},{5,6},{6,7},{7,8},{8,9},{9,10},{10,1... | collective-permute-start | bytes 196616 | tf_op jit(solution)/shard_map/ppermute | solution.py:313
  73.8 0.0 collective-permute-start.7
  73.8 2.4 %shard_map.107 = f32[1024,128]{1,0:T(8,128)} custom-call(f32[16,64,128]{2,1,0:T(8,128)} %copy-done.4), custom_call_target="tpu_custom_call" | custom-call | tf_op jit(solution)/shard_map/pallas_call | solution.py:300
  76.1 0.0 collective-permute-done.4.a_ref
  76.1 0.0 collective-permute-done.5.b_ref
  76.2 0.0 copy-start.12
  76.2 0.0 collective-permute-done.6.c_ref
  76.2 3.4 %collective-permute-done.7.d_ref = f32[32,512]{1,0:T(8,128)S(1)} collective-permute-done((f32[32,512]{1,0:T(8,128)S(1)}, f32[32,512]{1,0:T(8,128)S(1)}, u32[]{:S(2)}, u32[]{:S(2)}) %collective-permute-start.7) | collective-permute-done | bytes 65568 | tf_op jit(solution)/shard_map/ppermute | solution.py:313
  79.6 0.0 copy-done.12
  79.6 0.6 copy-done.14
  80.2 1.7 %shard_map.109 = f32[4,32,512]{2,1,0:T(8,128)} custom-call(f32[32,512]{1,0:T(8,128)} %copy-done.11, f32[32,512]{1,0:T(8,128)} %copy-done.12, f32[32,512]{1,0:T(8,128)} %copy-done.13, f32[32,512]{1,0:T(8,128)} %copy-done.14), custom_call_target="tpu_custom_call" | custom-call | tf_op jit(solution)/shard_map/pallas_call | solution.py:300
  (20 shorter events, 0.1 us)
Async XLA Ops:
  0.6 31.2 %copy-start.15 = (f32[3,32]{1,0:T(4,128)S(1)}, f32[3,32]{1,0:T(4,128)}, u32[]{:S(2)}) copy-start(f32[3,32]{1,0:T(4,128)} %param.13) | copy-start | bytes 1156
  0.6 31.3 %copy-start.16 = (s32[4,1]{0,1:T(1,128)S(1)}, s32[4,1]{0,1:T(1,128)}, u32[]{:S(2)}) copy-start(s32[4,1]{0,1:T(1,128)} %param.15) | copy-start | bytes 52
  4.5 30.7 %copy-start.1 = (f32[16,64,128]{2,1,0:T(8,128)S(1)}, f32[16,64,128]{2,1,0:T(8,128)}, u32[]{:S(2)}) copy-start(f32[16,64,128]{2,1,0:T(8,128)} %get-tuple-element.13.ht_ref) | copy-start | bytes 1572868
  4.5 30.7 %copy-start.2 = (f32[16,64,128]{2,1,0:T(8,128)S(1)}, f32[16,64,128]{2,1,0:T(8,128)}, u32[]{:S(2)}) copy-start(f32[16,64,128]{2,1,0:T(8,128)} %get-tuple-element.14.st_ref) | copy-start | bytes 1572868
  4.5 4.7 %collective-permute-start = (f32[16,8,128]{2,1,0:T(8,128)}, f32[16,8,128]{2,1,0:T(8,128)S(1)}, u32[]{:S(2)}, u32[]{:S(2)}) collective-permute-start(f32[16,8,128]{2,1,0:T(8,128)} %get-tuple-element.15), channel_id=1, source_target_pairs={{0,1},{1,2},{2,3},{3,4},{4,5},{5,6},{6,7},{7,8},{8,9},{9,10},{10,1... | collective-permute-start | bytes 196616 | tf_op jit(solution)/shard_map/ppermute | solution.py:313
  6.7 6.0 %collective-permute-start.1 = (f32[16,8,128]{2,1,0:T(8,128)}, f32[16,8,128]{2,1,0:T(8,128)S(1)}, u32[]{:S(2)}, u32[]{:S(2)}) collective-permute-start(f32[16,8,128]{2,1,0:T(8,128)} %get-tuple-element.16), channel_id=1, source_target_pairs={{0,15},{1,0},{2,1},{3,2},{4,3},{5,4},{6,5},{7,6},{8,7},{9,8},{10,9... | collective-permute-start | bytes 196616 | tf_op jit(solution)/shard_map/ppermute | solution.py:313
  9.2 3.5 %copy-start.5 = (f32[16,8,128]{2,1,0:T(8,128)}, f32[16,8,128]{2,1,0:T(8,128)S(1)}, u32[]{:S(2)}) copy-start(f32[16,8,128]{2,1,0:T(8,128)S(1)} %collective-permute-done.nlo_ref) | copy-start | bytes 196612
  12.7 0.6 copy-start.7
  15.4 16.7 %collective-permute-start.2 = (f32[640,128]{1,0:T(8,128)}, f32[640,128]{1,0:T(8,128)S(1)}, u32[]{:S(2)}, u32[]{:S(2)}) collective-permute-start(f32[640,128]{1,0:T(8,128)} %get-tuple-element.17), channel_id=1, source_target_pairs={{0,16},{16,32},{32,48},{48,64},{64,80},{80,96},{96,112},{112,128},... | collective-permute-start | bytes 983048 | tf_op jit(solution)/shard_map/ppermute | solution.py:313
  18.4 16.8 %collective-permute-start.3 = (f32[640,128]{1,0:T(8,128)}, f32[640,128]{1,0:T(8,128)S(1)}, u32[]{:S(2)}, u32[]{:S(2)}) collective-permute-start(f32[640,128]{1,0:T(8,128)} %get-tuple-element.18), channel_id=1, source_target_pairs={{0,240},{16,0},{32,16},{48,32},{64,48},{80,64},{96,80},{112,96},{1... | collective-permute-start | bytes 983048 | tf_op jit(solution)/shard_map/ppermute | solution.py:313
  23.6 29.3 %copy-start.3 = (f32[32,4096]{1,0:T(8,128)S(1)}, f32[32,4096]{1,0:T(8,128)}, u32[]{:S(2)}) copy-start(f32[32,4096]{1,0:T(8,128)} %rec_ref.1) | copy-start | bytes 1572868
  23.6 29.3 %copy-start.9 = (s32[4096]{0:T(1024)S(1)}, s32[4096]{0:T(1024)}, u32[]{:S(2)}) copy-start(s32[4096]{0:T(1024)} %param.12) | copy-start | bytes 49156
  31.8 21.1 %copy-start.10 = (s32[4,512]{1,0:T(4,128)S(1)}, s32[4,512]{1,0:T(4,128)}, u32[]{:S(2)}) copy-start(s32[4,512]{1,0:T(4,128)} %list_ref.1) | copy-start | bytes 24580
  35.2 1.2 %copy-start = (f32[26,80,128]{2,1,0:T(8,128)S(1)}, f32[26,80,128]{2,1,0:T(8,128)}, u32[]{:S(2)}) copy-start(f32[26,80,128]{2,1,0:T(8,128)} %shard_map.105.cond_ref) | copy-start | bytes 3194884
  36.4 0.8 %copy-start.6 = (f32[16,8,128]{2,1,0:T(8,128)S(1)}, f32[16,8,128]{2,1,0:T(8,128)}, u32[]{:S(2)}) copy-start(f32[16,8,128]{2,1,0:T(8,128)} %copy-done.5) | copy-start | bytes 196612
  37.2 0.8 %copy-start.8 = (f32[16,8,128]{2,1,0:T(8,128)S(1)}, f32[16,8,128]{2,1,0:T(8,128)}, u32[]{:S(2)}) copy-start(f32[16,8,128]{2,1,0:T(8,128)} %copy-done.7) | copy-start | bytes 196612
  52.8 11.7 %copy-start.4 = (f32[16,64,128]{2,1,0:T(8,128)}, f32[16,64,128]{2,1,0:T(8,128)S(1)}, u32[]{:S(2)}) copy-start(f32[16,64,128]{2,1,0:T(8,128)S(1)} %get-tuple-element.19.ht_ref) | copy-start | bytes 1572868
  64.5 11.6 %collective-permute-start.4 = (f32[32,512]{1,0:T(8,128)S(1)}, f32[32,512]{1,0:T(8,128)S(1)}, u32[]{:S(2)}, u32[]{:S(2)}) collective-permute-start(f32[32,512]{1,0:T(8,128)S(1)} %get-tuple-element.26), channel_id=1, source_target_pairs={{0,16},{16,32},{32,48},{48,64},{64,80},{80,96},{96,112},{112,128},... | collective-permute-start | bytes 196616 | tf_op jit(solution)/shard_map/ppermute | solution.py:313
  68.1 8.1 %collective-permute-start.5 = (f32[32,512]{1,0:T(8,128)S(1)}, f32[32,512]{1,0:T(8,128)S(1)}, u32[]{:S(2)}, u32[]{:S(2)}) collective-permute-start(f32[32,512]{1,0:T(8,128)S(1)} %get-tuple-element.25), channel_id=1, source_target_pairs={{0,240},{16,0},{32,16},{48,32},{64,48},{80,64},{96,80},{112,96},{1... | collective-permute-start | bytes 196616 | tf_op jit(solution)/shard_map/ppermute | solution.py:313
  70.3 5.9 %collective-permute-start.6 = (f32[32,512]{1,0:T(8,128)S(1)}, f32[32,512]{1,0:T(8,128)S(1)}, u32[]{:S(2)}, u32[]{:S(2)}) collective-permute-start(f32[32,512]{1,0:T(8,128)S(1)} %get-tuple-element.24), channel_id=1, source_target_pairs={{0,1},{1,2},{2,3},{3,4},{4,5},{5,6},{6,7},{7,8},{8,9},{9,10},{10,1... | collective-permute-start | bytes 196616 | tf_op jit(solution)/shard_map/ppermute | solution.py:313
  73.8 5.8 %collective-permute-start.7 = (f32[32,512]{1,0:T(8,128)S(1)}, f32[32,512]{1,0:T(8,128)S(1)}, u32[]{:S(2)}, u32[]{:S(2)}) collective-permute-start(f32[32,512]{1,0:T(8,128)S(1)} %get-tuple-element.23), channel_id=1, source_target_pairs={{0,15},{1,0},{2,1},{3,2},{4,3},{5,4},{6,5},{7,6},{8,7},{9,8},{10,9... | collective-permute-start | bytes 196616 | tf_op jit(solution)/shard_map/ppermute | solution.py:313
  76.1 3.4 %copy-start.11 = (f32[32,512]{1,0:T(8,128)}, f32[32,512]{1,0:T(8,128)S(1)}, u32[]{:S(2)}) copy-start(f32[32,512]{1,0:T(8,128)S(1)} %collective-permute-done.4.a_ref) | copy-start | bytes 196612
  76.2 3.4 %copy-start.12 = (f32[32,512]{1,0:T(8,128)}, f32[32,512]{1,0:T(8,128)S(1)}, u32[]{:S(2)}) copy-start(f32[32,512]{1,0:T(8,128)S(1)} %collective-permute-done.5.b_ref) | copy-start | bytes 196612
  76.2 3.4 %copy-start.13 = (f32[32,512]{1,0:T(8,128)}, f32[32,512]{1,0:T(8,128)S(1)}, u32[]{:S(2)}) copy-start(f32[32,512]{1,0:T(8,128)S(1)} %collective-permute-done.6.c_ref) | copy-start | bytes 196612
  79.6 0.6 copy-start.14

commit v2 on v1

--- a/solution.py
+++ b/solution.py
@@ -16,7 +16,7 @@
 PAD = ROWS + 16
 NX, NY = 256, 2048
 NSIDE = WIDE - 1
-ESEND = WIDE * HALF + NSIDE * HALF + 2 * NSIDE * 8
+ESEND = (WIDE + NSIDE) * HALF + NSIDE * 8
 STEP = 0.25
 F32 = jnp.float32
 VMEM = pl.BlockSpec(memory_space=pltpu.VMEM)
@@ -47,18 +47,16 @@
 
 
 def pack_kernel(ht_ref, st_ref, nlo_ref, nhi_ref, elo_ref, ehi_ref):
+    upper = lax.broadcasted_iota(jnp.int32, (8, 128), 0) < 4
     for ref, at, at_s in ((elo_ref, CX - WIDE, CX - NSIDE), (ehi_ref, 0, 0)):
         row = 0
-        for source, start, count in (
-            (ht_ref, at, WIDE),
-            (st_ref, at_s, NSIDE),
-            (nlo_ref, at_s, NSIDE),
-            (nhi_ref, at_s, NSIDE),
-        ):
-            height = source.shape[1]
+        for source, start, count in ((ht_ref, at, WIDE), (st_ref, at_s, NSIDE)):
             for i in range(count):
-                ref[row : row + height] = source[start + i]
-                row += height
+                ref[row : row + HALF] = source[start + i]
+                row += HALF
+        for i in range(NSIDE):
+            ref[row : row + 8] = jnp.where(upper, nhi_ref[at_s + i], nlo_ref[at_s + i])
+            row += 8
 
 
 def cond_kernel(w_ref, out_ref, base_ref, xrow_ref):
@@ -98,108 +96,155 @@
     return jnp.exp(jnp.minimum(h, 0.0))
 
 
-def sweep_kernel(
-    ht_ref, st_ref, nlo_ref, nhi_ref, elo_ref, ehi_ref, cond_ref,
+def one(condition):
+    return condition.astype(F32)
+
+
+def edges():
+    z = lanes((8, 128)) % 64
+    return one(z < LZ - 1), one(z > 0)
+
+
+def grid_tables(count_ref, mask_ref):
+    north = lax.axis_index("north")
+    lane = lanes((ROWS, 128))
+    y = north * CY - 8 + lax.broadcasted_iota(jnp.int32, (ROWS, 128), 0) + (lane // 64) * HALF
+    z = lane % 64
+    count_ref[...] = one(y > 0) + one(y < NY - 1) + one(z > 0) + one(z < LZ - 1)
+    mask_ref[...] = one((y >= 0) & (y < NY))
+
+
+def clear_pads(refs):
+    zero = jnp.zeros((8, 128), F32)
+    for ref in refs:
+        for i in range(ref.shape[0]):
+            ref[i, 0:8] = zero
+            ref[i, PAD - 8 : PAD] = zero
+
+
+def start_row(at, h, s, nlo, nhi, cond, ha, ka, sto_ref, src_ref):
+    low = lanes((8, 128)) < 64
+    north = lax.axis_index("north")
+    nlo = jnp.where(north > 0, nlo, 0.0)
+    nhi = jnp.where(north < 15, nhi, 0.0)
+    pieces = [(0, jnp.where(low, nlo, swap(h[HALF - 8 :])))]
+    pieces += [(8 + r, h[r : r + 8]) for r in range(0, HALF, 8)]
+    pieces += [(ROWS - 8, swap(jnp.where(low, nhi, h[:8])))]
+    if s is not None:
+        sources = [swap(jnp.where(low, s[HALF - 8 :], nlo))]
+        sources += [s[r : r + 8] for r in range(0, HALF, 8)]
+        sources += [jnp.where(low, swap(s[:8]), nhi)]
+    for n, (r, piece) in enumerate(pieces):
+        relative = rel(piece)
+        ha[at, 8 + r : 16 + r] = piece
+        ka[at, 8 + r : 16 + r] = cond(r) * relative
+        if s is not None:
+            sto = 0.5 + 0.5 * relative
+            sto_ref[at, r : r + 8] = sto
+            src_ref[at, r : r + 8] = sto * piece + sources[n]
+
+
+def sweep_row(at, xi, hin, kin, hout, kout, cond_ref, sto_ref, src_ref, count_ref, mask_ref):
+    up_mask, down_mask = edges()
+    gravity = up_mask - down_mask
+    xg = lax.axis_index("east") * CX - WIDE + xi
+    along_x = one(xg > 0) + one(xg < NX - 1)
+    in_x = one((xg >= 0) & (xg < NX))
+    for r in range(0, ROWS, 8):
+        a = r + 8
+        h, k = hin[at, a : a + 8], kin[at, a : a + 8]
+        hu = pltpu.roll(h, 127, 1) * up_mask
+        ku = pltpu.roll(k, 127, 1) * up_mask
+        hd = pltpu.roll(h, 1, 1) * down_mask
+        kd = pltpu.roll(k, 1, 1) * down_mask
+        hn, kn = hin[at, a + 1 : a + 9], kin[at, a + 1 : a + 9]
+        hs, ks = hin[at, a - 1 : a + 7], kin[at, a - 1 : a + 7]
+        he, ke = hin[at + 1, a : a + 8], kin[at + 1, a : a + 8]
+        hw, kw = hin[at - 1, a : a + 8], kin[at - 1, a : a + 8]
+        sum_h = ((hu + hd) + (hn + hs)) + ((he + hw) + gravity)
+        sum_k = ((ku + kd) + (kn + ks)) + (ke + kw)
+        flux = ((ku * hu + kd * hd) + (kn * hn + ks * hs)) + (ke * he + kw * hw)
+        top = (src_ref[at, r : r + 8] + k * sum_h) + (flux + (ku - kd))
+        below = (count_ref[r : r + 8] + along_x) * k + (sto_ref[at, r : r + 8] + sum_k)
+        inv = pltpu.reciprocal(below, approx=True)
+        inv = inv * (2.0 - below * inv)
+        inv = inv * (2.0 - below * inv)
+        new = top * inv * in_x
+        if r == 0 or r == ROWS - 8:
+            new = new * mask_ref[r : r + 8]
+        hout[at, a : a + 8] = new
+        kout[at, a : a + 8] = cond_ref[xi, r : r + 8] * rel(new)
+
+
+def inner_kernel(
+    ht_ref, st_ref, nlo_ref, nhi_ref, cond_ref, ha, hb, ka, kb, sto_ref, src_ref, count_ref, mask_ref
+):
+    grid_tables(count_ref, mask_ref)
+    clear_pads((ha, hb, ka, kb))
+
+    def own(x, carry):
+        cond = lambda r: cond_ref[x + WIDE, r : r + 8]
+        start_row(x, ht_ref[x], st_ref[x], nlo_ref[x], nhi_ref[x], cond, ha, ka, sto_ref, src_ref)
+        return carry
+
+    lax.fori_loop(0, CX, own, 0)
+    hin, kin, hout, kout = ha, ka, hb, kb
+    for number in range(1, ITERS + 1):
+
+        def sweep(x, carry, hin=hin, kin=kin, hout=hout, kout=kout):
+            sweep_row(x, x + WIDE, hin, kin, hout, kout, cond_ref, sto_ref, src_ref, count_ref, mask_ref)
+            return carry
+
+        lax.fori_loop(number, CX - number, sweep, 0)
+        hin, kin, hout, kout = hout, kout, hin, kin
+
+
+def outer_kernel(
+    ha0, hb0, ka0, kb0, sto0, src0, elo_ref, ehi_ref, cond_ref,
     heads_ref, table_ref,
     ha, hb, ka, kb, sto_ref, src_ref, count_ref, mask_ref,
 ):
     east = lax.axis_index("east")
-    north = lax.axis_index("north")
-    low = lanes((8, 128)) < 64
-    has_south, has_north = north > 0, north < 15
-    has_west, has_east = east > 0, east < 15
-    lane = lanes((ROWS, 128))
-    row = lax.broadcasted_iota(jnp.int32, (ROWS, 128), 0)
-    y = north * CY - 8 + row + (lane // 64) * HALF
-    z = lane % 64
-    one = lambda c: c.astype(F32)
-    count_ref[...] = one(y > 0) + one(y < NY - 1) + one(z > 0) + one(z < LZ - 1)
-    mask_ref[...] = one((y >= 0) & (y < NY))
-    zl = lanes((8, 128)) % 64
-    up_mask = one(zl < LZ - 1)
-    down_mask = one(zl > 0)
-    gravity = up_mask - down_mask
+    grid_tables(count_ref, mask_ref)
+    clear_pads((ha, hb, ka, kb))
+
+    def keep(x, carry):
+        for small, big in ((ha0, ha), (hb0, hb), (ka0, ka), (kb0, kb)):
+            big[x + WIDE, 8 : PAD - 8] = small[x, 8 : PAD - 8]
+        return carry
+
+    lax.fori_loop(0, CX, keep, 0)
+    for small, big in ((sto0, sto_ref), (src0, src_ref)):
+        for i in range(ITERS):
+            big[WIDE + i] = small[i]
+            big[EXT - 1 - WIDE - i] = small[CX - 1 - i]
     zero = jnp.zeros((8, 128), F32)
-    for buf in (ha, hb, ka, kb):
-        for i in range(EXT):
-            buf[i, 0:8] = zero
-            buf[i, PAD - 8 : PAD] = zero
-
-    def start(xi, h, s, nlo, nhi, with_source):
-        nlo = jnp.where(has_south, nlo, 0.0)
-        nhi = jnp.where(has_north, nhi, 0.0)
-        pieces = [(0, jnp.where(low, nlo, swap(h[HALF - 8 :])))]
-        pieces += [(8 + r, h[r : r + 8]) for r in range(0, HALF, 8)]
-        pieces += [(ROWS - 8, swap(jnp.where(low, nhi, h[:8])))]
-        if with_source:
-            sources = [swap(jnp.where(low, s[HALF - 8 :], nlo))]
-            sources += [s[r : r + 8] for r in range(0, HALF, 8)]
-            sources += [jnp.where(low, swap(s[:8]), nhi)]
-        for n, (r, piece) in enumerate(pieces):
-            relative = rel(piece)
-            ha[xi, 8 + r : 16 + r] = piece
-            ka[xi, 8 + r : 16 + r] = cond_ref[xi, r : r + 8] * relative
-            if with_source:
-                sto = 0.5 + 0.5 * relative
-                sto_ref[xi, r : r + 8] = sto
-                src_ref[xi, r : r + 8] = sto * piece + sources[n]
-
-    def own(x, carry):
-        start(x + WIDE, ht_ref[x], st_ref[x], nlo_ref[x], nhi_ref[x], True)
-        return carry
-
-    lax.fori_loop(0, CX, own, 0)
-    for ref, valid, first, flip in ((elo_ref, has_west, 0, 0), (ehi_ref, has_east, EXT - WIDE, 1)):
+    for ref, valid, first, flip in ((elo_ref, east > 0, 0, 0), (ehi_ref, east < 15, EXT - WIDE, 1)):
         for i in range(WIDE):
+            xi = first + i
             h = jnp.where(valid, ref[i * HALF : (i + 1) * HALF], 0.0)
+            s, corner = None, zero
             j = i if flip else i - 1
             if 0 <= j < NSIDE:
-                s_at = WIDE * HALF + j * HALF
+                s_at = (WIDE + j) * HALF
                 c_at = (WIDE + NSIDE) * HALF + j * 8
                 s = jnp.where(valid, ref[s_at : s_at + HALF], 0.0)
-                nlo = jnp.where(valid, ref[c_at : c_at + 8], 0.0)
-                nhi = jnp.where(valid, ref[c_at + NSIDE * 8 : c_at + NSIDE * 8 + 8], 0.0)
-                start(first + i, h, s, nlo, nhi, True)
-            else:
-                start(first + i, h, None, zero, zero, False)
+                corner = jnp.where(valid, ref[c_at : c_at + 8], 0.0)
+            cond = lambda r, xi=xi: cond_ref[xi, r : r + 8]
+            start_row(xi, h, s, corner, corner, cond, ha, ka, sto_ref, src_ref)
 
     hin, kin, hout, kout = ha, ka, hb, kb
     for number in range(1, ITERS + 1):
 
-        def sweep(xi, carry, hin=hin, kin=kin, hout=hout, kout=kout):
-            xg = east * CX - WIDE + xi
-            along_x = one(xg > 0) + one(xg < NX - 1)
-            in_x = one((xg >= 0) & (xg < NX))
-            for r in range(0, ROWS, 8):
-                a = r + 8
-                h, k = hin[xi, a : a + 8], kin[xi, a : a + 8]
-                hu = pltpu.roll(h, 127, 1) * up_mask
-                ku = pltpu.roll(k, 127, 1) * up_mask
-                hd = pltpu.roll(h, 1, 1) * down_mask
-                kd = pltpu.roll(k, 1, 1) * down_mask
-                hn, kn = hin[xi, a + 1 : a + 9], kin[xi, a + 1 : a + 9]
-                hs, ks = hin[xi, a - 1 : a + 7], kin[xi, a - 1 : a + 7]
-                he, ke = hin[xi + 1, a : a + 8], kin[xi + 1, a : a + 8]
-                hw, kw = hin[xi - 1, a : a + 8], kin[xi - 1, a : a + 8]
-                sum_h = ((hu + hd) + (hn + hs)) + ((he + hw) + gravity)
-                sum_k = ((ku + kd) + (kn + ks)) + (ke + kw)
-                flux = ((ku * hu + kd * hd) + (kn * hn + ks * hs)) + (ke * he + kw * hw)
-                top = (src_ref[xi, r : r + 8] + k * sum_h) + (flux + (ku - kd))
-                below = (count_ref[r : r + 8] + along_x) * k + (sto_ref[xi, r : r + 8] + sum_k)
-                inv = pl.reciprocal(below, approx=True)
-                inv = inv * (2.0 - below * inv)
-                inv = inv * (2.0 - below * inv)
-                new = top * inv * in_x
-                if r == 0 or r == ROWS - 8:
-                    new = new * mask_ref[r : r + 8]
-                hout[xi, a : a + 8] = new
-                kout[xi, a : a + 8] = cond_ref[xi, r : r + 8] * rel(new)
+        def sweep(i, carry, number=number, hin=hin, kin=kin, hout=hout, kout=kout):
+            xi = number + i + jnp.where(i < WIDE, 0, EXT - 2 * WIDE - 2 * number)
+            sweep_row(xi, xi, hin, kin, hout, kout, cond_ref, sto_ref, src_ref, count_ref, mask_ref)
             return carry
 
-        lax.fori_loop(number, EXT - number, sweep, 0)
+        lax.fori_loop(0, 2 * WIDE, sweep, 0)
         hin, kin, hout, kout = hout, kout, hin, kin
 
-    up2, down2 = up_mask, down_mask
+    up_mask, down_mask = edges()
     up2 = jnp.concatenate([up_mask, up_mask], axis=0)
     down2 = jnp.concatenate([down_mask, down_mask], axis=0)
 
@@ -295,16 +340,14 @@
         out_ref[d] = jnp.where(valid, ref[...], 0.0)
 
 
-def call(kernel, outs, ins, scratch=(), limit=None, specs=None, cost=None):
-    params = {} if limit is None else dict(compiler_params=pltpu.CompilerParams(vmem_limit_bytes=limit))
+def call(kernel, outs, ins, scratch=(), limit=6, specs=None):
     return pl.pallas_call(
         kernel,
         out_shape=[jax.ShapeDtypeStruct(s, t) for s, t in outs],
         in_specs=specs or [VMEM] * len(ins),
         out_specs=[VMEM] * len(outs),
         scratch_shapes=list(scratch),
-        cost_estimate=cost,
-        **params,
+        compiler_params=pltpu.CompilerParams(vmem_limit_bytes=limit * 2**20),
     )(*ins)
 
 
@@ -342,15 +385,20 @@
         [weights],
         [pltpu.VMEM((ROWS, 128), F32), pltpu.VMEM((32, 128), F32)],
     )
+    plane = pltpu.VMEM((ROWS, 128), F32)
+    level = ((CX, PAD, 128), F32)
+    base = ((CX, ROWS, 128), F32)
+    inner = call(
+        inner_kernel, [level] * 4 + [base] * 2, [ht, st, nlo, nhi, cond], [plane, plane], limit=12
+    )
     buf = pltpu.VMEM((EXT, PAD, 128), F32)
     ext = pltpu.VMEM((EXT, ROWS, 128), F32)
-    plane = pltpu.VMEM((ROWS, 128), F32)
     heads, table = call(
-        sweep_kernel,
+        outer_kernel,
         [tile, ((3 * CX * HALF, 256), jnp.bfloat16)],
-        [ht, st, nlo, nhi, elo, ehi, cond],
+        list(inner) + [elo, ehi, cond],
         [buf, buf, buf, buf, ext, ext, plane, plane],
-        limit=48 * 2**20,
+        limit=20,
     )
     couple = jnp.broadcast_to((STEP * coupling)[:, :, None], (3, 32, 128)).reshape(96, 128)
     moved, buffers = call(
@@ -358,7 +406,7 @@
         [((32, 4096), F32), ((4, 32, 512), F32)],
         [table, cell_index.reshape(32, 128), records, couple, send_list, send_count],
         [pltpu.VMEM((1024, 256), jnp.bfloat16)],
-        limit=48 * 2**20,
+        limit=24,
         specs=[VMEM] * 5 + [SMEM],
     )
     came = [

time: 82.3 us -> 67.4 us (0.82)
  Pallas kernels: 44.4 us -> 36.7 us
  waiting for transfers between devices: 10 us -> 7.89 us
  local copies, waits for them, and re-layouts: 4.52 us -> 2.43 us
  starting transfers between devices: 19 us -> 17 us
    pallas_call x7 -> x8, Pallas kernels: 44.4 us -> 36.7 us  [call(): pl.pallas_call(kernel, out_shape=[jax.ShapeDtypeStruct(s, t) for s, t in...]
    ppermute x8, waiting for transfers between devices: 10 us -> 7.89 us  [ring(): lax.ppermute(value, axis, [(i, (i + steps) % count) for i in range(count)])]
    unnamed x35 -> x15, local copies, waits for them, and re-layouts: 4.29 us -> 2.19 us
    ppermute x8, starting transfers between devices: 19 us -> 17 us  [ring(): lax.ppermute(value, axis, [(i, (i + steps) % count) for i in range(count)])]
  transfers between devices with their start and end apart: 8 -> 8, of which waited for: 3 -> 2; matrix products, arithmetic and copies ran while one was open for 3% -> 3% of each run, Pallas kernels for 13% -> 23%
where the time goes in v2:
time: 67.4 us; the launch traced here: 67.2 us
  Pallas kernels  36.7 us (54%)
  starting transfers between devices  17 us (25%)
  waiting for transfers between devices  7.89 us (12%)
  local copies, waits for them, and re-layouts  2.43 us (4%)
  other arithmetic  1.7 us (3%)
  between operations  1.47 us (2%)
    pallas_call x8, Pallas kernels, call(): pl.pallas_call(kernel, out_shape=[jax.ShapeDtypeStruct(s, t) for s, t in...  36.7 us
    ppermute x8, starting transfers between devices, ring(): lax.ppermute(value, axis, [(i, (i + steps) % count) for i in range(count)])  17 us
    ppermute x8, waiting for transfers between devices, ring(): lax.ppermute(value, axis, [(i, (i + steps) % count) for i in range(count)])  7.89 us
    unnamed x15, local copies, waits for them, and re-layouts  2.19 us
  transfers between devices with their start and end apart: 8, of which 2 were waited for; matrix products, arithmetic and copies ran while one was open for 3% of the time, Pallas kernels for 23%

profile of v2, /device:TPU:7, one launch (start us, length us, event | category | flops | bytes accessed | tf_op | source)
XLA Modules:
  0.0 67.2 jit_solution(10047728811281289546)
XLA Ops:
  0.6 0.0 copy-start.1
  0.6 1.0 %copy-done.1 = f32[64,16,128]{2,1,0:T(8,128)S(1)} copy-done((f32[64,16,128]{2,1,0:T(8,128)S(1)}, f32[64,16,128]{2,1,0:T(8,128)}, u32[]{:S(2)}) %copy-start.1) | copy-done | bytes 524312
  1.7 0.0 copy-start.2
  1.7 1.0 %copy-done.2 = f32[64,16,128]{2,1,0:T(8,128)S(1)} copy-done((f32[64,16,128]{2,1,0:T(8,128)S(1)}, f32[64,16,128]{2,1,0:T(8,128)}, u32[]{:S(2)}) %copy-start.2) | copy-done | bytes 524312
  2.7 0.0 copy-start.5
  2.7 0.0 copy-start.6
  2.7 1.7 %shard_map.103 = (f32[16,64,128]{2,1,0:T(8,128)S(1)}, f32[16,64,128]{2,1,0:T(8,128)S(1)}, f32[16,8,128]{2,1,0:T(8,128)S(1)}, f32[16,8,128]{2,1,0:T(8,128)S(1)}) custom-call(f32[1024,128]{1,0:T(8,128)S(1)} %bitcast.16, f32[1024,128]{1,0:T(8,128)S(1)} %bitcast.17), custom_call_target="tpu_custom_call" | custom-call | tf_op jit(solution)/shard_map/pallas_call | solution.py:344
  4.4 2.2 %collective-permute-start = (f32[16,8,128]{2,1,0:T(8,128)S(1)}, f32[16,8,128]{2,1,0:T(8,128)S(1)}, u32[]{:S(2)}, u32[]{:S(2)}) collective-permute-start(f32[16,8,128]{2,1,0:T(8,128)S(1)} %get-tuple-element.21), channel_id=1, source_target_pairs={{0,1},{1,2},{2,3},{3,4},{4,5},{5,6},{6,7},{7,8},{8,9},{9,10},{10,1... | collective-permute-start | bytes 196616 | tf_op jit(solution)/shard_map/ppermute | solution.py:356
  6.6 0.0 collective-permute-start.1
  6.6 0.1 broadcast_add_fusion
  6.7 0.7 %fusion = f32[]{:T(128)} fusion(f32[8]{0:T(128)S(1)} %convert_multiply_fusion, f32[8,8]{1,0:T(8,128)S(1)} %broadcast_add_fusion), kind=kLoop, calls=%fused_computation.6 | loop fusion | flops 2559 | bytes 292 | tf_op jit(solution)/shard_map/reduce_sum | solution.py:364
  8.1 0.9 %multiply_bitcast_fusion = f32[8,64]{0,1:T(8,128)S(1)} fusion(f32[8,8,8]{2,1,0:T(8,128)} %param.10, f32[]{:T(128)S(6)} %sqrt.7, f32[8]{0:T(128)S(1)} %convert_multiply_fusion, f32[8,8]{1,0:T(8,128)S(1)} %broadcast_add_fusion), kind=kLoop, calls=%fused_computation.4 | loop fusion | flops 3072 | bytes 4388 | tf_op jit(solution)/shard_map/reshape | solution.py:380
  8.9 0.1 copy.13
  9.0 0.0 collective-permute-done.nlo_ref
  9.0 3.4 %collective-permute-done.1.nhi_ref = f32[16,8,128]{2,1,0:T(8,128)S(1)} collective-permute-done((f32[16,8,128]{2,1,0:T(8,128)S(1)}, f32[16,8,128]{2,1,0:T(8,128)S(1)}, u32[]{:S(2)}, u32[]{:S(2)}) %collective-permute-start.1) | collective-permute-done | bytes 65568 | tf_op jit(solution)/shard_map/ppermute | solution.py:356
  12.4 3.1 %collective-permute-start.2 = (f32[608,128]{1,0:T(8,128)S(1)}, f32[608,128]{1,0:T(8,128)S(1)}, u32[]{:S(2)}, u32[]{:S(2)}) collective-permute-start(f32[608,128]{1,0:T(8,128)S(1)} %get-tuple-element.29), channel_id=1, source_target_pairs={{0,16},{16,32},{32,48},{48,64},{64,80},{80,96},{96,112},{112,128},... | collective-permute-start | bytes 933896 | tf_op jit(solution)/shard_map/ppermute | solution.py:356
  15.5 4.7 %collective-permute-start.3 = (f32[608,128]{1,0:T(8,128)S(1)}, f32[608,128]{1,0:T(8,128)S(1)}, u32[]{:S(2)}, u32[]{:S(2)}) collective-permute-start(f32[608,128]{1,0:T(8,128)S(1)} %get-tuple-element.30), channel_id=1, source_target_pairs={{0,240},{16,0},{32,16},{48,32},{64,48},{80,64},{96,80},{112,96},{1... | collective-permute-start | bytes 933896 | tf_op jit(solution)/shard_map/ppermute | solution.py:356
  20.2 0.1 pad_maximum_fusion.w_ref
  20.3 6.5 %shard_map.104.cond_ref = f32[26,80,128]{2,1,0:T(8,128)S(1)} custom-call(f32[8,128]{1,0:T(8,128)S(1)} %pad_maximum_fusion.w_ref), custom_call_target="tpu_custom_call" | custom-call | tf_op jit(solution)/shard_map/pallas_call | solution.py:344
  26.7 0.0 copy-done.5
  26.8 0.1 broadcast_in_dim.4
  26.9 0.0 copy-done.6
  26.9 0.1 copy.12.count_ref
  26.9 7.5 %shard_map.105 = (f32[16,96,128]{2,1,0:T(8,128)S(1)}, f32[16,96,128]{2,1,0:T(8,128)S(1)}, f32[16,96,128]{2,1,0:T(8,128)S(1)}, f32[16,96,128]{2,1,0:T(8,128)S(1)}...) custom-call(f32[16,64,128]{2,1,0:T(8,128)S(1)} %get-tuple-element.19.ht_ref, ...), custom_call_target="tpu_custom_call" | custom-call | tf_op jit(solution)/shard_map/pallas_call | solution.py:344
  34.5 0.0 collective-permute-done.2.elo_ref
  34.5 0.0 collective-permute-done.3.ehi_ref
  34.5 0.0 copy-start
  34.5 0.0 copy-start.3
  34.5 0.0 copy-start.4
  34.5 7.4 %shard_map.107 = (f32[16,64,128]{2,1,0:T(8,128)S(1)}, bf16[3072,256]{1,0:T(8,128)(2,1)S(1)}) custom-call(f32[16,96,128]{2,1,0:T(8,128)S(1)} %get-tuple-element.23.ha0, f32[16,96,128]{2,1,0:T(8,128)S(1)} %get-tuple-element.24.hb0, f32[16,96,128]{2,1,0:T(8,128)S(1)} %get-tuple-element.25.ka0, f32[16,96,128]{2,1,0:T(8,128)S(1)} %get-tuple-element.26.kb0, ...), custom_call_target="tpu_custom_call" | custom-call | tf_op jit(solution)/shard_map/pallas_call | solution.py:344
  41.9 0.1 broadcast_in_dim.5.couple_ref
  42.0 0.0 copy-done
  42.0 0.0 copy-done.3
  42.0 0.0 copy-done.4
  42.0 11.5 %shard_map.109 = (f32[32,4096]{1,0:T(8,128)}, f32[4,32,512]{2,1,0:T(8,128)S(1)}) custom-call(bf16[3072,256]{1,0:T(8,128)(2,1)S(1)} %get-tuple-element.32.table_ref, s32[32,128]{1,0:T(8,128)S(1)} %bitcast.18, f32[32,4096]{1,0:T(8,128)S(1)} %copy-done, f32[96,128]{1,0:T(8,128)S(1)} %broadcast_in_dim.5.couple_ref, s32[4,512]{1,0:T(4,128)S(1)} %copy-done.4, ...), custom_call_target="tpu_custom_call" | custom-call | tf_op jit(solution)/shard_map/pallas_call | solution.py:344
  53.6 0.7 collective-permute-start.4
  54.3 5.1 %collective-permute-start.5 = (f32[32,512]{1,0:T(8,128)S(1)}, f32[32,512]{1,0:T(8,128)S(1)}, u32[]{:S(2)}, u32[]{:S(2)}) collective-permute-start(f32[32,512]{1,0:T(8,128)S(1)} %get-tuple-element.37), channel_id=1, source_target_pairs={{0,240},{16,0},{32,16},{48,32},{64,48},{80,64},{96,80},{112,96},{1... | collective-permute-start | bytes 196616 | tf_op jit(solution)/shard_map/ppermute | solution.py:356
  59.4 1.3 %collective-permute-start.6 = (f32[32,512]{1,0:T(8,128)S(1)}, f32[32,512]{1,0:T(8,128)S(1)}, u32[]{:S(2)}, u32[]{:S(2)}) collective-permute-start(f32[32,512]{1,0:T(8,128)S(1)} %get-tuple-element.36), channel_id=1, source_target_pairs={{0,1},{1,2},{2,3},{3,4},{4,5},{5,6},{6,7},{7,8},{8,9},{9,10},{10,1... | collective-permute-start | bytes 196616 | tf_op jit(solution)/shard_map/ppermute | solution.py:356
  60.7 0.0 collective-permute-start.7
  60.7 1.3 %shard_map.108 = f32[1024,128]{1,0:T(8,128)} custom-call(f32[16,64,128]{2,1,0:T(8,128)S(1)} %get-tuple-element.31.ht_ref), custom_call_target="tpu_custom_call" | custom-call | tf_op jit(solution)/shard_map/pallas_call | solution.py:344
  62.0 0.0 collective-permute-done.4.a_ref
  62.0 0.0 collective-permute-done.5.b_ref
  62.0 0.0 collective-permute-done.6.c_ref
  62.0 4.5 %collective-permute-done.7.d_ref = f32[32,512]{1,0:T(8,128)S(1)} collective-permute-done((f32[32,512]{1,0:T(8,128)S(1)}, f32[32,512]{1,0:T(8,128)S(1)}, u32[]{:S(2)}, u32[]{:S(2)}) %collective-permute-start.7) | collective-permute-done | bytes 65568 | tf_op jit(solution)/shard_map/ppermute | solution.py:356
  66.5 0.7 %shard_map.110 = f32[4,32,512]{2,1,0:T(8,128)} custom-call(f32[32,512]{1,0:T(8,128)S(1)} %collective-permute-done.4.a_ref, f32[32,512]{1,0:T(8,128)S(1)} %collective-permute-done.5.b_ref, f32[32,512]{1,0:T(8,128)S(1)} %collective-permute-done.6.c_ref, f32[32,512]{1,0:T(8,128)S(1)} %collective-permute-done.7.d_ref), custom_call_target="tpu_custom_call" | custom-call | tf_op jit(solution)/shard_map/pallas_call | solution.py:344
  (4 shorter events, 0.1 us)
Async XLA Ops:
  0.6 1.0 %copy-start.1 = (f32[64,16,128]{2,1,0:T(8,128)S(1)}, f32[64,16,128]{2,1,0:T(8,128)}, u32[]{:S(2)}) copy-start(f32[64,16,128]{2,1,0:T(8,128)} %param.8) | copy-start | bytes 1572868
  1.7 1.0 %copy-start.2 = (f32[64,16,128]{2,1,0:T(8,128)S(1)}, f32[64,16,128]{2,1,0:T(8,128)}, u32[]{:S(2)}) copy-start(f32[64,16,128]{2,1,0:T(8,128)} %param.9) | copy-start | bytes 1572868
  2.7 24.0 %copy-start.5 = (f32[3,32]{1,0:T(4,128)S(1)}, f32[3,32]{1,0:T(4,128)}, u32[]{:S(2)}) copy-start(f32[3,32]{1,0:T(4,128)} %param.13) | copy-start | bytes 1156
  2.7 24.1 %copy-start.6 = (s32[4,1]{0,1:T(1,128)S(1)}, s32[4,1]{0,1:T(1,128)}, u32[]{:S(2)}) copy-start(s32[4,1]{0,1:T(1,128)} %param.15) | copy-start | bytes 52
  4.4 4.6 %collective-permute-start = (f32[16,8,128]{2,1,0:T(8,128)S(1)}, f32[16,8,128]{2,1,0:T(8,128)S(1)}, u32[]{:S(2)}, u32[]{:S(2)}) collective-permute-start(f32[16,8,128]{2,1,0:T(8,128)S(1)} %get-tuple-element.21), channel_id=1, source_target_pairs={{0,1},{1,2},{2,3},{3,4},{4,5},{5,6},{6,7},{7,8},{8,9},{9,10},{10,1... | collective-permute-start | bytes 196616 | tf_op jit(solution)/shard_map/ppermute | solution.py:356
  6.6 5.8 %collective-permute-start.1 = (f32[16,8,128]{2,1,0:T(8,128)S(1)}, f32[16,8,128]{2,1,0:T(8,128)S(1)}, u32[]{:S(2)}, u32[]{:S(2)}) collective-permute-start(f32[16,8,128]{2,1,0:T(8,128)S(1)} %get-tuple-element.22), channel_id=1, source_target_pairs={{0,15},{1,0},{2,1},{3,2},{4,3},{5,4},{6,5},{7,6},{8,7},{9,8},{10,9... | collective-permute-start | bytes 196616 | tf_op jit(solution)/shard_map/ppermute | solution.py:356
  12.4 22.0 %collective-permute-start.2 = (f32[608,128]{1,0:T(8,128)S(1)}, f32[608,128]{1,0:T(8,128)S(1)}, u32[]{:S(2)}, u32[]{:S(2)}) collective-permute-start(f32[608,128]{1,0:T(8,128)S(1)} %get-tuple-element.29), channel_id=1, source_target_pairs={{0,16},{16,32},{32,48},{48,64},{64,80},{80,96},{96,112},{112,128},... | collective-permute-start | bytes 933896 | tf_op jit(solution)/shard_map/ppermute | solution.py:356
  15.5 19.0 %collective-permute-start.3 = (f32[608,128]{1,0:T(8,128)S(1)}, f32[608,128]{1,0:T(8,128)S(1)}, u32[]{:S(2)}, u32[]{:S(2)}) collective-permute-start(f32[608,128]{1,0:T(8,128)S(1)} %get-tuple-element.30), channel_id=1, source_target_pairs={{0,240},{16,0},{32,16},{48,32},{64,48},{80,64},{96,80},{112,96},{1... | collective-permute-start | bytes 933896 | tf_op jit(solution)/shard_map/ppermute | solution.py:356
  34.5 7.5 %copy-start = (f32[32,4096]{1,0:T(8,128)S(1)}, f32[32,4096]{1,0:T(8,128)}, u32[]{:S(2)}) copy-start(f32[32,4096]{1,0:T(8,128)} %rec_ref.1) | copy-start | bytes 1572868
  34.5 7.5 %copy-start.3 = (s32[4096]{0:T(1024)S(1)}, s32[4096]{0:T(1024)}, u32[]{:S(2)}) copy-start(s32[4096]{0:T(1024)} %param.12) | copy-start | bytes 49156
  34.5 7.5 %copy-start.4 = (s32[4,512]{1,0:T(4,128)S(1)}, s32[4,512]{1,0:T(4,128)}, u32[]{:S(2)}) copy-start(s32[4,512]{1,0:T(4,128)} %list_ref.1) | copy-start | bytes 24580
  53.6 8.4 %collective-permute-start.4 = (f32[32,512]{1,0:T(8,128)S(1)}, f32[32,512]{1,0:T(8,128)S(1)}, u32[]{:S(2)}, u32[]{:S(2)}) collective-permute-start(f32[32,512]{1,0:T(8,128)S(1)} %get-tuple-element.38), channel_id=1, source_target_pairs={{0,16},{16,32},{32,48},{48,64},{64,80},{80,96},{96,112},{112,128},... | collective-permute-start | bytes 196616 | tf_op jit(solution)/shard_map/ppermute | solution.py:356
  54.3 7.7 %collective-permute-start.5 = (f32[32,512]{1,0:T(8,128)S(1)}, f32[32,512]{1,0:T(8,128)S(1)}, u32[]{:S(2)}, u32[]{:S(2)}) collective-permute-start(f32[32,512]{1,0:T(8,128)S(1)} %get-tuple-element.37), channel_id=1, source_target_pairs={{0,240},{16,0},{32,16},{48,32},{64,48},{80,64},{96,80},{112,96},{1... | collective-permute-start | bytes 196616 | tf_op jit(solution)/shard_map/ppermute | solution.py:356
  59.4 2.6 %collective-permute-start.6 = (f32[32,512]{1,0:T(8,128)S(1)}, f32[32,512]{1,0:T(8,128)S(1)}, u32[]{:S(2)}, u32[]{:S(2)}) collective-permute-start(f32[32,512]{1,0:T(8,128)S(1)} %get-tuple-element.36), channel_id=1, source_target_pairs={{0,1},{1,2},{2,3},{3,4},{4,5},{5,6},{6,7},{7,8},{8,9},{9,10},{10,1... | collective-permute-start | bytes 196616 | tf_op jit(solution)/shard_map/ppermute | solution.py:356
  60.7 5.8 %collective-permute-start.7 = (f32[32,512]{1,0:T(8,128)S(1)}, f32[32,512]{1,0:T(8,128)S(1)}, u32[]{:S(2)}, u32[]{:S(2)}) collective-permute-start(f32[32,512]{1,0:T(8,128)S(1)} %get-tuple-element.35), channel_id=1, source_target_pairs={{0,15},{1,0},{2,1},{3,2},{4,3},{5,4},{6,5},{7,6},{8,7},{9,8},{10,9... | collective-permute-start | bytes 196616 | tf_op jit(solution)/shard_map/ppermute | solution.py:356

commit v3 on v2

--- a/solution.py
+++ b/solution.py
@@ -1,5 +1,3 @@
-import functools
-
 import jax
 import jax.numpy as jnp
 from jax import lax
@@ -13,7 +11,9 @@
 WIDE = ITERS + 1
 EXT = CX + 2 * WIDE
 ROWS = HALF + 16
-PAD = ROWS + 16
+PAD = ROWS + 8
+MID = CX - 2 * WIDE
+OUT = CX - MID
 NX, NY = 256, 2048
 NSIDE = WIDE - 1
 ESEND = (WIDE + NSIDE) * HALF + NSIDE * 8
@@ -31,19 +31,23 @@
     return pltpu.roll(v, 64, 1)
 
 
-def turn_kernel(h_ref, s_ref, ht_ref, st_ref, nlo_ref, nhi_ref):
+def turned(ref, x):
+    t = ref[pl.ds(x, LZ, stride=CX), :].T
+    return jnp.concatenate([t[:HALF], t[HALF:]], axis=1)
+
+
+def turn_kernel(h_ref, ht_ref):
+    for x in range(CX):
+        ht_ref[x] = turned(h_ref, x)
+
+
+def turn_source_kernel(s_ref, ht_ref, st_ref, nlo_ref, nhi_ref):
     low = lanes((8, 128)) < 64
-
-    def turned(ref, x):
-        t = ref[pl.ds(x, LZ, stride=CX), :].T
-        return jnp.concatenate([t[:HALF], t[HALF:]], axis=1)
-
     for x in range(CX):
-        h, s = turned(h_ref, x), turned(s_ref, x)
-        ht_ref[x] = h
+        s = turned(s_ref, x)
         st_ref[x] = s
-        nlo_ref[x] = jnp.where(low, swap(h[HALF - 8 :]), s[HALF - 8 :])
-        nhi_ref[x] = jnp.where(low, h[:8], swap(s[:8]))
+        nlo_ref[x] = jnp.where(low, swap(ht_ref[x, HALF - 8 :]), s[HALF - 8 :])
+        nhi_ref[x] = jnp.where(low, ht_ref[x, :8], swap(s[:8]))
 
 
 def pack_kernel(ht_ref, st_ref, nlo_ref, nhi_ref, elo_ref, ehi_ref):
@@ -59,37 +63,43 @@
             row += 8
 
 
-def cond_kernel(w_ref, out_ref, base_ref, xrow_ref):
+def cond_kernel(modes_ref, out_ref, work_ref, xrow_ref):
     start_x = lax.axis_index("east") * CX - WIDE
     start_y = lax.axis_index("north") * CY - 8
-    lane = lanes((ROWS, 128))
-    row = lax.broadcasted_iota(jnp.int32, (ROWS, 128), 0)
-    y = start_y + row + (lane // 64) * HALF
-    inside_y = (y >= 0) & (y < NY)
-    coord = y.astype(F32) + 0.5
-    base = jnp.broadcast_to(w_ref[0:1, :], (ROWS, 128))
-    for b in range(1, 8):
-        base = base + w_ref[b : b + 1, :] * jnp.cos(jnp.pi * float(b) * coord / NY)
-    base_ref[...] = base
-    lane_x = lanes((32, 128))
+    exact = dict(precision=lax.Precision.HIGHEST, preferred_element_type=F32)
+    ca = lax.broadcasted_iota(jnp.int32, (64, 8), 0)
+    order_c, order_a, order_b = (ca // 8).astype(F32), (ca % 8).astype(F32), lanes((64, 8)).astype(F32)
+    spectrum = 1.0 / (1.0 + (order_c * order_c + order_a * order_a + order_b * order_b) / 4.0)
+    total = jnp.sum(jnp.sum(spectrum, axis=1, keepdims=True), axis=0, keepdims=True)
+    weights = modes_ref[...] * jnp.sqrt(spectrum) * (1.0 / jnp.sqrt(total))
+    row = lax.broadcasted_iota(jnp.int32, (ROWS, 8), 0)
+    order = lanes((ROWS, 8)).astype(F32)
+    halves = []
+    for half in range(2):
+        coord = (start_y + half * HALF + row).astype(F32) + 0.5
+        table = jnp.cos(jnp.pi * order * coord / NY)
+        halves.append(lax.dot_general(table, weights, (((1,), (1,)), ((), ())), **exact))
+    base = jnp.concatenate(halves, axis=1)
     x = start_x + lax.broadcasted_iota(jnp.int32, (32, 128), 0)
-    order = (lane_x % 8).astype(F32)
+    order = (lanes((32, 128)) % 8).astype(F32)
     xrow_ref[...] = jnp.cos(jnp.pi * order * (x.astype(F32) + 0.5) / NX)
     lane_z = lanes((128, 128))
     mode = lax.broadcasted_iota(jnp.int32, (128, 128), 0)
     order = ((mode % 64) // 8).astype(F32)
     table = jnp.cos(jnp.pi * order * ((lane_z % 64).astype(F32) + 0.5) / LZ)
     table = jnp.where(mode // 64 == lane_z // 64, table, 0.0)
-
-    def step(i, carry):
-        scaled = base_ref[...] * xrow_ref[pl.ds(i, 1), :]
-        log = jnp.dot(scaled, table, precision=lax.Precision.HIGHEST, preferred_element_type=F32)
-        xg = start_x + i
-        live = inside_y & (xg >= 0) & (xg < NX)
-        out_ref[i] = jnp.where(live, 0.5 * jnp.exp(log), 0.0)
-        return carry
-
-    lax.fori_loop(0, EXT, step, 0)
+    lane = lanes((ROWS, 128))
+    y = start_y + lax.broadcasted_iota(jnp.int32, (ROWS, 128), 0) + (lane // 64) * HALF
+    inside_y = one((y >= 0) & (y < NY))
+    for first in range(0, EXT, EXT // 2):
+        for i in range(EXT // 2):
+            work_ref[i * ROWS : (i + 1) * ROWS] = base * xrow_ref[first + i : first + i + 1, :]
+        log = jnp.dot(work_ref[...], table, **exact)
+        for i in range(EXT // 2):
+            xg = start_x + first + i
+            live = inside_y * one((xg >= 0) & (xg < NX))
+            value = jnp.exp(log[i * ROWS : (i + 1) * ROWS])
+            out_ref[first + i] = jnp.where(live > 0.0, 0.5 * value, 0.0)
 
 
 def rel(h):
@@ -98,6 +108,12 @@
 
 def one(condition):
     return condition.astype(F32)
+
+
+def split(ref, at, value):
+    big = value.astype(jnp.bfloat16)
+    ref[at, 0:128] = big
+    ref[at, 128:256] = (value - big.astype(F32)).astype(jnp.bfloat16)
 
 
 def edges():
@@ -136,8 +152,8 @@
         sources += [jnp.where(low, swap(s[:8]), nhi)]
     for n, (r, piece) in enumerate(pieces):
         relative = rel(piece)
-        ha[at, 8 + r : 16 + r] = piece
-        ka[at, 8 + r : 16 + r] = cond(r) * relative
+        ha[at, 4 + r : 12 + r] = piece
+        ka[at, 4 + r : 12 + r] = cond(r) * relative
         if s is not None:
             sto = 0.5 + 0.5 * relative
             sto_ref[at, r : r + 8] = sto
@@ -150,8 +166,8 @@
     xg = lax.axis_index("east") * CX - WIDE + xi
     along_x = one(xg > 0) + one(xg < NX - 1)
     in_x = one((xg >= 0) & (xg < NX))
-    for r in range(0, ROWS, 8):
-        a = r + 8
+    for a in range(8, PAD - 8, 8):
+        r = a - 4
         h, k = hin[at, a : a + 8], kin[at, a : a + 8]
         hu = pltpu.roll(h, 127, 1) * up_mask
         ku = pltpu.roll(k, 127, 1) * up_mask
@@ -170,17 +186,35 @@
         inv = inv * (2.0 - below * inv)
         inv = inv * (2.0 - below * inv)
         new = top * inv * in_x
-        if r == 0 or r == ROWS - 8:
+        if a == 8 or a == PAD - 16:
             new = new * mask_ref[r : r + 8]
         hout[at, a : a + 8] = new
         kout[at, a : a + 8] = cond_ref[xi, r : r + 8] * rel(new)
 
 
+def velocity_row(at, row, size, h_ref, k_ref, table_ref):
+    up_mask, down_mask = edges()
+    up_mask = jnp.concatenate([up_mask, up_mask], axis=0)
+    down_mask = jnp.concatenate([down_mask, down_mask], axis=0)
+    for r in range(0, HALF, 16):
+        a = r + 12
+        h, k = h_ref[at, a : a + 16], k_ref[at, a : a + 16]
+        hu = pltpu.roll(h, 127, 1) * up_mask
+        hd = pltpu.roll(h, 1, 1) * down_mask
+        flow_x = -k * (h_ref[at + 1, a : a + 16] - h_ref[at - 1, a : a + 16])
+        flow_y = -k * (h_ref[at, a + 1 : a + 17] - h_ref[at, a - 1 : a + 15])
+        flow_z = -k * ((hu - hd) + 2.0)
+        for c, flow in enumerate((flow_x, flow_y, flow_z)):
+            split(table_ref, pl.ds(pl.multiple_of(row + c * size + r, 16), 16), flow)
+
+
 def inner_kernel(
-    ht_ref, st_ref, nlo_ref, nhi_ref, cond_ref, ha, hb, ka, kb, sto_ref, src_ref, count_ref, mask_ref
+    ht_ref, st_ref, nlo_ref, nhi_ref, cond_ref,
+    ha, hb, ka, kb, sto_ref, src_ref, table_ref,
+    count_ref, mask_ref,
 ):
     grid_tables(count_ref, mask_ref)
-    clear_pads((ha, hb, ka, kb))
+    clear_pads((hb, kb))
 
     def own(x, carry):
         cond = lambda r: cond_ref[x + WIDE, r : r + 8]
@@ -197,6 +231,12 @@
 
         lax.fori_loop(number, CX - number, sweep, 0)
         hin, kin, hout, kout = hout, kout, hin, kin
+
+    def velocity(i, carry):
+        velocity_row(i + WIDE, i * HALF, MID * HALF, hin, kin, table_ref)
+        return carry
+
+    lax.fori_loop(0, MID, velocity, 0)
 
 
 def outer_kernel(
@@ -206,14 +246,13 @@
 ):
     east = lax.axis_index("east")
     grid_tables(count_ref, mask_ref)
-    clear_pads((ha, hb, ka, kb))
-
-    def keep(x, carry):
-        for small, big in ((ha0, ha), (hb0, hb), (ka0, ka), (kb0, kb)):
-            big[x + WIDE, 8 : PAD - 8] = small[x, 8 : PAD - 8]
-        return carry
-
-    lax.fori_loop(0, CX, keep, 0)
+    clear_pads((hb, kb))
+    for x in range(CX):
+        depth = min(x, CX - 1 - x)
+        if depth <= WIDE:
+            ha[x + WIDE], ka[x + WIDE] = ha0[x], ka0[x]
+        if 1 <= depth <= ITERS:
+            hb[x + WIDE], kb[x + WIDE] = hb0[x], kb0[x]
     for small, big in ((sto0, sto_ref), (src0, src_ref)):
         for i in range(ITERS):
             big[WIDE + i] = small[i]
@@ -244,29 +283,16 @@
         lax.fori_loop(0, 2 * WIDE, sweep, 0)
         hin, kin, hout, kout = hout, kout, hin, kin
 
-    up_mask, down_mask = edges()
-    up2 = jnp.concatenate([up_mask, up_mask], axis=0)
-    down2 = jnp.concatenate([down_mask, down_mask], axis=0)
-
-    def velocity(x, carry):
-        xi = x + WIDE
-        for r in range(0, HALF, 16):
-            a = r + 16
-            h, k = hin[xi, a : a + 16], kin[xi, a : a + 16]
-            heads_ref[x, r : r + 16] = h
-            hu = pltpu.roll(h, 127, 1) * up2
-            hd = pltpu.roll(h, 1, 1) * down2
-            flow_x = -k * (hin[xi + 1, a : a + 16] - hin[xi - 1, a : a + 16])
-            flow_y = -k * (hin[xi, a + 1 : a + 17] - hin[xi, a - 1 : a + 15])
-            flow_z = -k * ((hu - hd) + 2.0)
-            for c, flow in enumerate((flow_x, flow_y, flow_z)):
-                big = flow.astype(jnp.bfloat16)
-                at = pl.ds(pl.multiple_of(c * CX * HALF + x * HALF + r, 16), 16)
-                table_ref[at, 0:128] = big
-                table_ref[at, 128:256] = (flow - big.astype(F32)).astype(jnp.bfloat16)
+    for x in range(CX):
+        source, at = (ha0, x) if WIDE <= x < CX - WIDE else (hin, x + WIDE)
+        heads_ref[x] = source[at, 12 : 12 + HALF]
+
+    def velocity(i, carry):
+        at = i + WIDE + jnp.where(i < WIDE, 0, MID)
+        velocity_row(at, i * HALF, OUT * HALF, hin, kin, table_ref)
         return carry
 
-    lax.fori_loop(0, CX, velocity, 0)
+    lax.fori_loop(0, OUT, velocity, 0)
 
 
 def onehot_pair(index):
@@ -278,52 +304,73 @@
 def choose(get, first, count, bits):
     if count == 1:
         return get(first)
-    level = count.bit_length() - 2
-    half = count // 2
+    level = (count - 1).bit_length() - 1
+    half = 1 << level
     low = choose(get, first, half, bits)
-    high = choose(get, first + half, half, bits)
+    high = choose(get, first + half, count - half, bits)
     return jnp.where(bits[level], high, low)
 
 
-BLOCK = 256
-
-
-def sample_kernel(table_ref, cell_ref, rec_ref, couple_ref, list_ref, count_ref, moved_ref, send_ref, pick_ref):
+BLOCK = 512
+PARTS = BLOCK // 128
+
+
+def read_cells(cell_ref, n):
+    cell = jnp.concatenate([cell_ref[pl.ds(n * PARTS + i, 1), :] for i in range(PARTS)], axis=1)
+    layer, x, j = cell >> 11, (cell >> 7) & 15, cell & 127
+    return x, j & 63, (j >> 6) * 64 + layer
+
+
+def sampled_at(table_ref, count, place, inner_y, lane):
+    got = jnp.dot(table_ref[...], onehot_pair(lane), preferred_element_type=F32)
+    row8 = jnp.broadcast_to(place * 64 + inner_y, (8, BLOCK))
+    bits = [(row8 & (8 << b)) != 0 for b in range(7)]
+    mine = lax.broadcasted_iota(jnp.int32, (8, BLOCK), 0) == (row8 & 7)
+    size = count * HALF
+    for c in range(3):
+        picked = choose(lambda g: got[c * size + g * 8 : c * size + g * 8 + 8], 0, count * 8, bits)
+        yield c, jnp.sum(jnp.where(mine, picked, 0.0), axis=0, keepdims=True)
+
+
+def sample_inner_kernel(table_ref, cell_ref, part_ref):
     def block(n, carry):
-        cell = jnp.concatenate([cell_ref[pl.ds(n * 2, 1), :], cell_ref[pl.ds(n * 2 + 1, 1), :]], axis=1)
-        layer, i, j = cell >> 11, (cell >> 7) & 15, cell & 127
-        lane = (j >> 6) * 64 + layer
-        row = i * 64 + (j & 63)
-        got = jnp.dot(table_ref[...], onehot_pair(lane), preferred_element_type=F32)
-        row8 = jnp.broadcast_to(row, (8, BLOCK))
-        bits = [(row8 & (8 << b)) != 0 for b in range(7)]
-        mine = lax.broadcasted_iota(jnp.int32, (8, BLOCK), 0) == (row8 & 7)
+        x, inner_y, lane = read_cells(cell_ref, n)
+        at = pl.ds(pl.multiple_of(n * BLOCK, BLOCK), BLOCK)
+        for c, sampled in sampled_at(table_ref, MID, jnp.clip(x - WIDE, 0, MID - 1), inner_y, lane):
+            part_ref[c : c + 1, at] = sampled
+        return carry
+
+    lax.fori_loop(0, 4096 // BLOCK, block, 0)
+
+
+def sample_kernel(
+    table_ref, cell_ref, part_ref, rec_ref, couple_ref, list_ref, count_ref, moved_ref, send_ref, pick_ref
+):
+    def block(n, carry):
+        x, inner_y, lane = read_cells(cell_ref, n)
+        middle = (x >= WIDE) & (x < CX - WIDE)
+        place = jnp.where(x < WIDE, x, jnp.maximum(x - MID, 0))
         at = pl.ds(pl.multiple_of(n * BLOCK, BLOCK), BLOCK)
         total = rec_ref[:, at]
-        for c in range(3):
-            picked = choose(lambda g: got[c * 1024 + g * 8 : c * 1024 + g * 8 + 8], 0, 128, bits)
-            sampled = jnp.sum(jnp.where(mine, picked, 0.0), axis=0, keepdims=True)
+        for c, outer in sampled_at(table_ref, OUT, place, inner_y, lane):
+            sampled = jnp.where(middle, part_ref[c : c + 1, at], outer)
             weight = couple_ref[c * 32 : (c + 1) * 32, :]
-            total = total + jnp.concatenate([weight, weight], axis=1) * sampled
+            total = total + jnp.concatenate([weight] * PARTS, axis=1) * sampled
         moved_ref[:, at] = total
-        for half in range(2):
-            part = total[:, half * 128 : (half + 1) * 128]
-            big = part.astype(jnp.bfloat16)
-            rows = pl.ds(pl.multiple_of((n * 2 + half) * 32, 32), 32)
-            pick_ref[rows, 0:128] = big
-            pick_ref[rows, 128:256] = (part - big.astype(F32)).astype(jnp.bfloat16)
+        for i in range(PARTS):
+            rows = pl.ds(pl.multiple_of((n * PARTS + i) * 32, 32), 32)
+            split(pick_ref, rows, total[:, i * 128 : (i + 1) * 128])
         return carry
 
     lax.fori_loop(0, 4096 // BLOCK, block, 0)
     for d in range(4):
-        for part in range(2):
-            index = list_ref[d : d + 1, part * BLOCK : (part + 1) * BLOCK]
-            got = jnp.dot(pick_ref[...], onehot_pair(index & 127), preferred_element_type=F32)
-            block_of = jnp.broadcast_to(index >> 7, (32, BLOCK))
-            bits = [(block_of & (1 << b)) != 0 for b in range(5)]
-            picked = choose(lambda g: got[g * 32 : (g + 1) * 32], 0, 32, bits)
-            live = lanes((32, BLOCK)) + part * BLOCK < count_ref[d, 0]
-            send_ref[d, :, part * BLOCK : (part + 1) * BLOCK] = jnp.where(live, picked, 0.0)
+        index = list_ref[d : d + 1, :]
+        got = jnp.dot(pick_ref[...], onehot_pair(index & 127), preferred_element_type=F32)
+        block_of = jnp.broadcast_to(index >> 7, (32, BLOCK))
+        bits = [(block_of & (1 << b)) != 0 for b in range(5)]
+        picked = choose(lambda g: got[g * 32 : (g + 1) * 32], 0, 32, bits)
+        live = lanes((32, BLOCK)) < count_ref[d, 0]
+        send_ref[d] = jnp.where(live, picked, 0.0)
 
 
 def back_kernel(ht_ref, out_ref):
@@ -356,46 +403,42 @@
     return lax.ppermute(value, axis, [(i, (i + steps) % count) for i in range(count)])
 
 
-def mode_weights(mode_coeffs):
-    order = jnp.arange(8).astype(F32)
-    spectrum = 1.0 / (
-        1.0 + (order[:, None, None] ** 2 + order[None, :, None] ** 2 + order[None, None, :] ** 2) / 4.0
-    )
-    return mode_coeffs * jnp.sqrt(spectrum) * (1.0 / jnp.sqrt(jnp.sum(spectrum)))
-
-
 def on_device(head_old, source, mode_coeffs, records, cell_index, coupling, send_list, send_count):
     flat = (LZ * CX, CY)
     tile = ((CX, HALF, 128), F32)
     side = ((CX, 8, 128), F32)
-    ht, st, n_up, n_down = call(
-        turn_kernel, [tile, tile, side, side], [head_old.reshape(flat), source.reshape(flat)]
-    )
+    (ht,) = call(turn_kernel, [tile], [head_old.reshape(flat)])
+    st, n_up, n_down = call(turn_source_kernel, [tile, side, side], [source.reshape(flat), ht])
     nlo = ring(n_up, "north", 1)
     nhi = ring(n_down, "north", -1)
     edge = ((ESEND, 128), F32)
     e_up, e_down = call(pack_kernel, [edge, edge], [ht, st, nlo, nhi])
     elo = ring(e_up, "east", 1)
     ehi = ring(e_down, "east", -1)
-    weights = jnp.transpose(mode_weights(mode_coeffs), (2, 0, 1)).reshape(8, 64)
-    weights = jnp.concatenate([weights, weights], axis=1)
     (cond,) = call(
         cond_kernel,
         [((EXT, ROWS, 128), F32)],
-        [weights],
-        [pltpu.VMEM((ROWS, 128), F32), pltpu.VMEM((32, 128), F32)],
+        [mode_coeffs.reshape(64, 8)],
+        [pltpu.VMEM((EXT // 2 * ROWS, 128), F32), pltpu.VMEM((32, 128), F32)],
+        limit=12,
     )
     plane = pltpu.VMEM((ROWS, 128), F32)
     level = ((CX, PAD, 128), F32)
     base = ((CX, ROWS, 128), F32)
-    inner = call(
-        inner_kernel, [level] * 4 + [base] * 2, [ht, st, nlo, nhi, cond], [plane, plane], limit=12
+    cells = cell_index.reshape(32, 128)
+    *inner, table_mid = call(
+        inner_kernel,
+        [level] * 4 + [base] * 2 + [((3 * MID * HALF, 256), jnp.bfloat16)],
+        [ht, st, nlo, nhi, cond],
+        [plane, plane],
+        limit=12,
     )
+    (part,) = call(sample_inner_kernel, [((8, 4096), F32)], [table_mid, cells], limit=12)
     buf = pltpu.VMEM((EXT, PAD, 128), F32)
     ext = pltpu.VMEM((EXT, ROWS, 128), F32)
     heads, table = call(
         outer_kernel,
-        [tile, ((3 * CX * HALF, 256), jnp.bfloat16)],
+        [tile, ((3 * OUT * HALF, 256), jnp.bfloat16)],
         list(inner) + [elo, ehi, cond],
         [buf, buf, buf, buf, ext, ext, plane, plane],
         limit=20,
@@ -404,10 +447,10 @@
     moved, buffers = call(
         sample_kernel,
         [((32, 4096), F32), ((4, 32, 512), F32)],
-        [table, cell_index.reshape(32, 128), records, couple, send_list, send_count],
+        [table, cells, part, records, couple, send_list, send_count],
         [pltpu.VMEM((1024, 256), jnp.bfloat16)],
         limit=24,
-        specs=[VMEM] * 5 + [SMEM],
+        specs=[VMEM] * 6 + [SMEM],
     )
     came = [
         ring(buffers[0], "east", 1),

time: 67.4 us -> 61.4 us (0.911)
  Pallas kernels: 36.7 us -> 31.8 us
  waiting for transfers between devices: 7.89 us -> 10.3 us
  other arithmetic: 1.7 us -> 0.01 us
  between operations: 1.47 us -> 0.77 us
    pallas_call x8 -> x10, Pallas kernels: 36.7 us -> 31.8 us  [call(): pl.pallas_call(kernel, out_shape=[jax.ShapeDtypeStruct(s, t) for s, t in...]
    ppermute x8, waiting for transfers between devices: 7.89 us -> 10.3 us  [ring(): lax.ppermute(value, axis, [(i, (i + steps) % count) for i in range(count)])]
    reshape x1 -> x0, other arithmetic: 0.85 us -> none  [on_device(): weights = jnp.transpose(mode_weights(mode_coeffs), (2, 0, 1)).reshape(8, 64)]
    reduce_sum x1 -> x0, other arithmetic: 0.69 us -> none  [mode_weights(): jnp.sum(spectrum)]
    unnamed x15 -> x17, local copies, waits for them, and re-layouts: 2.19 us -> 1.69 us
  transfers between devices with their start and end apart: 8 -> 8, of which waited for: 2 -> 4; matrix products, arithmetic and copies ran while one was open for 3% -> 0% of each run, Pallas kernels for 23% -> 25%
where the time goes in v3:
time: 61.4 us; the launch traced here: 61.2 us
  Pallas kernels  31.8 us (52%)
  starting transfers between devices  16.5 us (27%)
  waiting for transfers between devices  10.3 us (17%)
  local copies, waits for them, and re-layouts  1.87 us (3%)
  between operations  0.77 us (1%)
    pallas_call x10, Pallas kernels, call(): pl.pallas_call(kernel, out_shape=[jax.ShapeDtypeStruct(s, t) for s, t in...  31.8 us
    ppermute x8, starting transfers between devices, ring(): lax.ppermute(value, axis, [(i, (i + steps) % count) for i in range(count)])  16.5 us
    ppermute x8, waiting for transfers between devices, ring(): lax.ppermute(value, axis, [(i, (i + steps) % count) for i in range(count)])  10.3 us
    unnamed x17, local copies, waits for them, and re-layouts  1.69 us
  transfers between devices with their start and end apart: 8, of which 4 were waited for; matrix products, arithmetic and copies ran while one was open for 0% of the time, Pallas kernels for 25%

profile of v3, /device:TPU:7, one launch (start us, length us, event | category | flops | bytes accessed | tf_op | source)
XLA Modules:
  0.0 61.2 jit_solution(16472773681973152704)
XLA Ops:
  0.6 0.0 copy-start
  0.6 1.0 %copy-done = f32[64,16,128]{2,1,0:T(8,128)S(1)} copy-done((f32[64,16,128]{2,1,0:T(8,128)S(1)}, f32[64,16,128]{2,1,0:T(8,128)}, u32[]{:S(2)}) %copy-start) | copy-done | bytes 524312
  1.7 0.0 copy-start.1
  1.7 0.5 shard_map.103.ht_ref
  2.2 0.5 copy-done.1
  2.7 0.0 copy-start.4
  2.7 0.9 %shard_map.104 = (f32[16,64,128]{2,1,0:T(8,128)S(1)}, f32[16,8,128]{2,1,0:T(8,128)S(1)}, f32[16,8,128]{2,1,0:T(8,128)S(1)}) custom-call(f32[1024,128]{1,0:T(8,128)S(1)} %bitcast.14, f32[16,64,128]{2,1,0:T(8,128)S(1)} %shard_map.103.ht_ref), custom_call_target="tpu_custom_call" | custom-call | tf_op jit(solution)/shard_map/pallas_call | solution.py:391
  3.6 2.2 %collective-permute-start = (f32[16,8,128]{2,1,0:T(8,128)S(1)}, f32[16,8,128]{2,1,0:T(8,128)S(1)}, u32[]{:S(2)}, u32[]{:S(2)}) collective-permute-start(f32[16,8,128]{2,1,0:T(8,128)S(1)} %get-tuple-element.20), channel_id=1, source_target_pairs={{0,1},{1,2},{2,3},{3,4},{4,5},{5,6},{6,7},{7,8},{8,9},{9,10},{10,1... | collective-permute-start | bytes 196616 | tf_op jit(solution)/shard_map/ppermute | solution.py:403
  5.8 0.0 collective-permute-start.1
  5.8 1.3 %collective-permute-done.nlo_ref = f32[16,8,128]{2,1,0:T(8,128)S(1)} collective-permute-done((f32[16,8,128]{2,1,0:T(8,128)S(1)}, f32[16,8,128]{2,1,0:T(8,128)S(1)}, u32[]{:S(2)}, u32[]{:S(2)}) %collective-permute-start) | collective-permute-done | bytes 65568 | tf_op jit(solution)/shard_map/ppermute | solution.py:403
  7.1 4.5 %collective-permute-done.1.nhi_ref = f32[16,8,128]{2,1,0:T(8,128)S(1)} collective-permute-done((f32[16,8,128]{2,1,0:T(8,128)S(1)}, f32[16,8,128]{2,1,0:T(8,128)S(1)}, u32[]{:S(2)}, u32[]{:S(2)}) %collective-permute-start.1) | collective-permute-done | bytes 65568 | tf_op jit(solution)/shard_map/ppermute | solution.py:403
  11.6 0.0 copy-start.6
  11.6 0.0 copy-start.7
  11.7 3.1 %collective-permute-start.2 = (f32[608,128]{1,0:T(8,128)S(1)}, f32[608,128]{1,0:T(8,128)S(1)}, u32[]{:S(2)}, u32[]{:S(2)}) collective-permute-start(f32[608,128]{1,0:T(8,128)S(1)} %get-tuple-element.28), channel_id=1, source_target_pairs={{0,16},{16,32},{32,48},{48,64},{64,80},{80,96},{96,112},{112,128},... | collective-permute-start | bytes 933896 | tf_op jit(solution)/shard_map/ppermute | solution.py:403
  14.7 4.7 %collective-permute-start.3 = (f32[608,128]{1,0:T(8,128)S(1)}, f32[608,128]{1,0:T(8,128)S(1)}, u32[]{:S(2)}, u32[]{:S(2)}) collective-permute-start(f32[608,128]{1,0:T(8,128)S(1)} %get-tuple-element.29), channel_id=1, source_target_pairs={{0,240},{16,0},{32,16},{48,32},{64,48},{80,64},{96,80},{112,96},{1... | collective-permute-start | bytes 933896 | tf_op jit(solution)/shard_map/ppermute | solution.py:403
  19.4 0.0 copy-done.4
  19.4 1.9 %shard_map.105.cond_ref = f32[26,80,128]{2,1,0:T(8,128)S(1)} custom-call(f32[64,8]{1,0:T(8,128)S(1)} %bitcast.17), custom_call_target="tpu_custom_call" | custom-call | tf_op jit(solution)/shard_map/pallas_call | solution.py:391
  21.3 0.0 copy-done.6
  21.3 0.1 broadcast_in_dim.8
  21.4 0.0 copy-done.7
  21.4 0.1 copy.11.count_ref
  21.5 0.0 copy-start.3
  21.5 8.0 %shard_map.106 = (f32[16,88,128]{2,1,0:T(8,128)S(1)}, f32[16,88,128]{2,1,0:T(8,128)S(1)}, f32[16,88,128]{2,1,0:T(8,128)S(1)}, f32[16,88,128]{2,1,0:T(8,128)S(1)}...) custom-call(f32[16,64,128]{2,1,0:T(8,128)S(1)} %shard_map.103.ht_ref, ...), custom_call_target="tpu_custom_call" | custom-call | tf_op jit(solution)/shard_map/pallas_call | solution.py:391
  29.5 0.0 copy-done.3
  29.5 4.0 %shard_map.110.part_ref = f32[8,4096]{1,0:T(8,128)S(1)} custom-call(bf16[1152,256]{1,0:T(8,128)(2,1)S(1)} %get-tuple-element.32.table_ref, s32[32,128]{1,0:T(8,128)S(1)} %bitcast.15), custom_call_target="tpu_custom_call" | custom-call | tf_op jit(solution)/shard_map/pallas_call | solution.py:391
  33.5 0.0 collective-permute-done.2.elo_ref
  33.5 0.0 collective-permute-done.3.ehi_ref
  33.5 0.0 copy-start.2
  33.5 0.0 copy-start.5
  33.5 6.7 %shard_map.108 = (f32[16,64,128]{2,1,0:T(8,128)S(1)}, bf16[1920,256]{1,0:T(8,128)(2,1)S(1)}) custom-call(f32[16,88,128]{2,1,0:T(8,128)S(1)} %get-tuple-element.22.ha0, f32[16,88,128]{2,1,0:T(8,128)S(1)} %get-tuple-element.23.hb0, f32[16,88,128]{2,1,0:T(8,128)S(1)} %get-tuple-element.24.ka0, f32[16,88,128]{2,1,0:T(8,128)S(1)} %get-tuple-element.25.kb0, ...), custom_call_target="tpu_custom_call" | custom-call | tf_op jit(solution)/shard_map/pallas_call | solution.py:391
  40.3 0.1 broadcast_in_dim.9.couple_ref
  40.3 0.0 copy-done.2
  40.3 0.0 copy-done.5
  40.4 7.7 %shard_map.111 = (f32[32,4096]{1,0:T(8,128)}, f32[4,32,512]{2,1,0:T(8,128)S(1)}) custom-call(bf16[1920,256]{1,0:T(8,128)(2,1)S(1)} %get-tuple-element.31.table_ref, s32[32,128]{1,0:T(8,128)S(1)} %bitcast.16, f32[8,4096]{1,0:T(8,128)S(1)} %shard_map.110.part_ref, f32[32,4096]{1,0:T(8,128)S(1)} %copy-done.2, f32[96,128]{1,0:T(8,128)S(1)} %broadcast_in_dim.9.couple_ref, ...), custom_call_target="tpu_custom_call" | custom-call | tf_op jit(solution)/shard_map/pallas_call | solution.py:391
  48.1 0.4 collective-permute-start.4
  48.5 5.4 %collective-permute-start.5 = (f32[32,512]{1,0:T(8,128)S(1)}, f32[32,512]{1,0:T(8,128)S(1)}, u32[]{:S(2)}, u32[]{:S(2)}) collective-permute-start(f32[32,512]{1,0:T(8,128)S(1)} %get-tuple-element.37), channel_id=1, source_target_pairs={{0,240},{16,0},{32,16},{48,32},{64,48},{80,64},{96,80},{112,96},{1... | collective-permute-start | bytes 196616 | tf_op jit(solution)/shard_map/ppermute | solution.py:403
  53.8 0.8 %collective-permute-start.6 = (f32[32,512]{1,0:T(8,128)S(1)}, f32[32,512]{1,0:T(8,128)S(1)}, u32[]{:S(2)}, u32[]{:S(2)}) collective-permute-start(f32[32,512]{1,0:T(8,128)S(1)} %get-tuple-element.36), channel_id=1, source_target_pairs={{0,1},{1,2},{2,3},{3,4},{4,5},{5,6},{6,7},{7,8},{8,9},{9,10},{10,1... | collective-permute-start | bytes 196616 | tf_op jit(solution)/shard_map/ppermute | solution.py:403
  54.7 0.0 collective-permute-start.7
  54.7 1.3 %shard_map.109 = f32[1024,128]{1,0:T(8,128)} custom-call(f32[16,64,128]{2,1,0:T(8,128)S(1)} %get-tuple-element.30.ht_ref), custom_call_target="tpu_custom_call" | custom-call | tf_op jit(solution)/shard_map/pallas_call | solution.py:391
  56.0 0.1 collective-permute-done.4.a_ref
  56.1 0.0 collective-permute-done.5.b_ref
  56.1 0.0 collective-permute-done.6.c_ref
  56.1 4.4 %collective-permute-done.7.d_ref = f32[32,512]{1,0:T(8,128)S(1)} collective-permute-done((f32[32,512]{1,0:T(8,128)S(1)}, f32[32,512]{1,0:T(8,128)S(1)}, u32[]{:S(2)}, u32[]{:S(2)}) %collective-permute-start.7) | collective-permute-done | bytes 65568 | tf_op jit(solution)/shard_map/ppermute | solution.py:403
  60.5 0.7 %shard_map.112 = f32[4,32,512]{2,1,0:T(8,128)} custom-call(f32[32,512]{1,0:T(8,128)S(1)} %collective-permute-done.4.a_ref, f32[32,512]{1,0:T(8,128)S(1)} %collective-permute-done.5.b_ref, f32[32,512]{1,0:T(8,128)S(1)} %collective-permute-done.6.c_ref, f32[32,512]{1,0:T(8,128)S(1)} %collective-permute-done.7.d_ref), custom_call_target="tpu_custom_call" | custom-call | tf_op jit(solution)/shard_map/pallas_call | solution.py:391
  (3 shorter events, 0.1 us)
Async XLA Ops:
  0.6 1.0 %copy-start = (f32[64,16,128]{2,1,0:T(8,128)S(1)}, f32[64,16,128]{2,1,0:T(8,128)}, u32[]{:S(2)}) copy-start(f32[64,16,128]{2,1,0:T(8,128)} %param.8) | copy-start | bytes 1572868
  1.7 1.0 %copy-start.1 = (f32[64,16,128]{2,1,0:T(8,128)S(1)}, f32[64,16,128]{2,1,0:T(8,128)}, u32[]{:S(2)}) copy-start(f32[64,16,128]{2,1,0:T(8,128)} %param.9) | copy-start | bytes 1572868
  2.7 16.7 %copy-start.4 = (f32[8,8,8]{2,1,0:T(8,128)S(1)}, f32[8,8,8]{2,1,0:T(8,128)}, u32[]{:S(2)}) copy-start(f32[8,8,8]{2,1,0:T(8,128)} %param.10) | copy-start | bytes 6148
  3.6 3.5 %collective-permute-start = (f32[16,8,128]{2,1,0:T(8,128)S(1)}, f32[16,8,128]{2,1,0:T(8,128)S(1)}, u32[]{:S(2)}, u32[]{:S(2)}) collective-permute-start(f32[16,8,128]{2,1,0:T(8,128)S(1)} %get-tuple-element.20), channel_id=1, source_target_pairs={{0,1},{1,2},{2,3},{3,4},{4,5},{5,6},{6,7},{7,8},{8,9},{9,10},{10,1... | collective-permute-start | bytes 196616 | tf_op jit(solution)/shard_map/ppermute | solution.py:403
  5.8 5.8 %collective-permute-start.1 = (f32[16,8,128]{2,1,0:T(8,128)S(1)}, f32[16,8,128]{2,1,0:T(8,128)S(1)}, u32[]{:S(2)}, u32[]{:S(2)}) collective-permute-start(f32[16,8,128]{2,1,0:T(8,128)S(1)} %get-tuple-element.21), channel_id=1, source_target_pairs={{0,15},{1,0},{2,1},{3,2},{4,3},{5,4},{6,5},{7,6},{8,7},{9,8},{10,9... | collective-permute-start | bytes 196616 | tf_op jit(solution)/shard_map/ppermute | solution.py:403
  11.6 9.7 %copy-start.6 = (f32[3,32]{1,0:T(4,128)S(1)}, f32[3,32]{1,0:T(4,128)}, u32[]{:S(2)}) copy-start(f32[3,32]{1,0:T(4,128)} %param.13) | copy-start | bytes 1156
  11.6 9.8 %copy-start.7 = (s32[4,1]{0,1:T(1,128)S(1)}, s32[4,1]{0,1:T(1,128)}, u32[]{:S(2)}) copy-start(s32[4,1]{0,1:T(1,128)} %param.15) | copy-start | bytes 52
  11.7 21.8 %collective-permute-start.2 = (f32[608,128]{1,0:T(8,128)S(1)}, f32[608,128]{1,0:T(8,128)S(1)}, u32[]{:S(2)}, u32[]{:S(2)}) collective-permute-start(f32[608,128]{1,0:T(8,128)S(1)} %get-tuple-element.28), channel_id=1, source_target_pairs={{0,16},{16,32},{32,48},{48,64},{64,80},{80,96},{96,112},{112,128},... | collective-permute-start | bytes 933896 | tf_op jit(solution)/shard_map/ppermute | solution.py:403
  14.7 18.8 %collective-permute-start.3 = (f32[608,128]{1,0:T(8,128)S(1)}, f32[608,128]{1,0:T(8,128)S(1)}, u32[]{:S(2)}, u32[]{:S(2)}) collective-permute-start(f32[608,128]{1,0:T(8,128)S(1)} %get-tuple-element.29), channel_id=1, source_target_pairs={{0,240},{16,0},{32,16},{48,32},{64,48},{80,64},{96,80},{112,96},{1... | collective-permute-start | bytes 933896 | tf_op jit(solution)/shard_map/ppermute | solution.py:403
  21.5 8.0 %copy-start.3 = (s32[4096]{0:T(1024)S(1)}, s32[4096]{0:T(1024)}, u32[]{:S(2)}) copy-start(s32[4096]{0:T(1024)} %param.12) | copy-start | bytes 49156
  33.5 6.8 %copy-start.2 = (f32[32,4096]{1,0:T(8,128)S(1)}, f32[32,4096]{1,0:T(8,128)}, u32[]{:S(2)}) copy-start(f32[32,4096]{1,0:T(8,128)} %rec_ref.1) | copy-start | bytes 1572868
  33.5 6.8 %copy-start.5 = (s32[4,512]{1,0:T(4,128)S(1)}, s32[4,512]{1,0:T(4,128)}, u32[]{:S(2)}) copy-start(s32[4,512]{1,0:T(4,128)} %list_ref.1) | copy-start | bytes 24580
  48.1 8.0 %collective-permute-start.4 = (f32[32,512]{1,0:T(8,128)S(1)}, f32[32,512]{1,0:T(8,128)S(1)}, u32[]{:S(2)}, u32[]{:S(2)}) collective-permute-start(f32[32,512]{1,0:T(8,128)S(1)} %get-tuple-element.38), channel_id=1, source_target_pairs={{0,16},{16,32},{32,48},{48,64},{64,80},{80,96},{96,112},{112,128},... | collective-permute-start | bytes 196616 | tf_op jit(solution)/shard_map/ppermute | solution.py:403
  48.5 7.6 %collective-permute-start.5 = (f32[32,512]{1,0:T(8,128)S(1)}, f32[32,512]{1,0:T(8,128)S(1)}, u32[]{:S(2)}, u32[]{:S(2)}) collective-permute-start(f32[32,512]{1,0:T(8,128)S(1)} %get-tuple-element.37), channel_id=1, source_target_pairs={{0,240},{16,0},{32,16},{48,32},{64,48},{80,64},{96,80},{112,96},{1... | collective-permute-start | bytes 196616 | tf_op jit(solution)/shard_map/ppermute | solution.py:403
  53.8 2.3 %collective-permute-start.6 = (f32[32,512]{1,0:T(8,128)S(1)}, f32[32,512]{1,0:T(8,128)S(1)}, u32[]{:S(2)}, u32[]{:S(2)}) collective-permute-start(f32[32,512]{1,0:T(8,128)S(1)} %get-tuple-element.36), channel_id=1, source_target_pairs={{0,1},{1,2},{2,3},{3,4},{4,5},{5,6},{6,7},{7,8},{8,9},{9,10},{10,1... | collective-permute-start | bytes 196616 | tf_op jit(solution)/shard_map/ppermute | solution.py:403
  54.7 5.8 %collective-permute-start.7 = (f32[32,512]{1,0:T(8,128)S(1)}, f32[32,512]{1,0:T(8,128)S(1)}, u32[]{:S(2)}, u32[]{:S(2)}) collective-permute-start(f32[32,512]{1,0:T(8,128)S(1)} %get-tuple-element.35), channel_id=1, source_target_pairs={{0,15},{1,0},{2,1},{3,2},{4,3},{5,4},{6,5},{7,6},{8,7},{9,8},{10,9... | collective-permute-start | bytes 196616 | tf_op jit(solution)/shard_map/ppermute | solution.py:403

commit v4 on v3

--- a/solution.py
+++ b/solution.py
@@ -340,7 +340,7 @@
             part_ref[c : c + 1, at] = sampled
         return carry
 
-    lax.fori_loop(0, 4096 // BLOCK, block, 0)
+    lax.fori_loop(0, 4096 // BLOCK, block, 0, unroll=2)
 
 
 def sample_kernel(
@@ -362,7 +362,7 @@
             split(pick_ref, rows, total[:, i * 128 : (i + 1) * 128])
         return carry
 
-    lax.fori_loop(0, 4096 // BLOCK, block, 0)
+    lax.fori_loop(0, 4096 // BLOCK, block, 0, unroll=2)
     for d in range(4):
         index = list_ref[d : d + 1, :]
         got = jnp.dot(pick_ref[...], onehot_pair(index & 127), preferred_element_type=F32)
@@ -411,10 +411,6 @@
     st, n_up, n_down = call(turn_source_kernel, [tile, side, side], [source.reshape(flat), ht])
     nlo = ring(n_up, "north", 1)
     nhi = ring(n_down, "north", -1)
-    edge = ((ESEND, 128), F32)
-    e_up, e_down = call(pack_kernel, [edge, edge], [ht, st, nlo, nhi])
-    elo = ring(e_up, "east", 1)
-    ehi = ring(e_down, "east", -1)
     (cond,) = call(
         cond_kernel,
         [((EXT, ROWS, 128), F32)],
@@ -422,6 +418,11 @@
         [pltpu.VMEM((EXT // 2 * ROWS, 128), F32), pltpu.VMEM((32, 128), F32)],
         limit=12,
     )
+    nlo, nhi, cond = lax.optimization_barrier((nlo, nhi, cond))
+    edge = ((ESEND, 128), F32)
+    e_up, e_down = call(pack_kernel, [edge, edge], [ht, st, nlo, nhi])
+    elo = ring(e_up, "east", 1)
+    ehi = ring(e_down, "east", -1)
     plane = pltpu.VMEM((ROWS, 128), F32)
     level = ((CX, PAD, 128), F32)
     base = ((CX, ROWS, 128), F32)
@@ -433,7 +434,7 @@
         [plane, plane],
         limit=12,
     )
-    (part,) = call(sample_inner_kernel, [((8, 4096), F32)], [table_mid, cells], limit=12)
+    (part,) = call(sample_inner_kernel, [((8, 4096), F32)], [table_mid, cells], limit=20)
     buf = pltpu.VMEM((EXT, PAD, 128), F32)
     ext = pltpu.VMEM((EXT, ROWS, 128), F32)
     heads, table = call(
@@ -449,7 +450,7 @@
         [((32, 4096), F32), ((4, 32, 512), F32)],
         [table, cells, part, records, couple, send_list, send_count],
         [pltpu.VMEM((1024, 256), jnp.bfloat16)],
-        limit=24,
+        limit=32,
         specs=[VMEM] * 6 + [SMEM],
     )
     came = [

time: 61.4 us -> 60.3 us (0.982)
  starting transfers between devices: 16.5 us -> 18.9 us
  waiting for transfers between devices: 10.3 us -> 8.34 us
  Pallas kernels: 31.8 us -> 30.3 us
    ppermute x8, starting transfers between devices: 16.5 us -> 18.9 us  [ring(): lax.ppermute(value, axis, [(i, (i + steps) % count) for i in range(count)])]
    ppermute x8, waiting for transfers between devices: 10.3 us -> 8.34 us  [ring(): lax.ppermute(value, axis, [(i, (i + steps) % count) for i in range(count)])]
    pallas_call x10, Pallas kernels: 31.8 us -> 30.3 us  [call(): pl.pallas_call(kernel, out_shape=[jax.ShapeDtypeStruct(s, t) for s, t in...]
  transfers between devices with their start and end apart: 8 -> 8, of which waited for: 4 -> 2; matrix products, arithmetic and copies ran while one was open for 0% -> 0% of each run, Pallas kernels for 25% -> 24%
where the time goes in v4:
time: 60.3 us; the launch traced here: 60.2 us
  Pallas kernels  30.3 us (50%)
  starting transfers between devices  18.9 us (31%)
  waiting for transfers between devices  8.34 us (14%)
  local copies, waits for them, and re-layouts  1.87 us (3%)
  between operations  0.77 us (1%)
    pallas_call x10, Pallas kernels, call(): pl.pallas_call(kernel, out_shape=[jax.ShapeDtypeStruct(s, t) for s, t in...  30.3 us
    ppermute x8, starting transfers between devices, ring(): lax.ppermute(value, axis, [(i, (i + steps) % count) for i in range(count)])  18.9 us
    ppermute x8, waiting for transfers between devices, ring(): lax.ppermute(value, axis, [(i, (i + steps) % count) for i in range(count)])  8.34 us
    unnamed x17, local copies, waits for them, and re-layouts  1.69 us
  transfers between devices with their start and end apart: 8, of which 2 were waited for; matrix products, arithmetic and copies ran while one was open for 0% of the time, Pallas kernels for 24%

profile of v4, /device:TPU:7, one launch (start us, length us, event | category | flops | bytes accessed | tf_op | source)
XLA Modules:
  0.0 60.2 jit_solution(6041905540183620844)
XLA Ops:
  0.6 0.0 copy-start
  0.6 1.0 %copy-done = f32[64,16,128]{2,1,0:T(8,128)S(1)} copy-done((f32[64,16,128]{2,1,0:T(8,128)S(1)}, f32[64,16,128]{2,1,0:T(8,128)}, u32[]{:S(2)}) %copy-start) | copy-done | bytes 524312
  1.7 0.0 copy-start.1
  1.7 0.0 copy-start.4
  1.7 0.5 shard_map.103.ht_ref
  2.2 0.5 copy-done.1
  2.7 0.9 %shard_map.104 = (f32[16,64,128]{2,1,0:T(8,128)S(1)}, f32[16,8,128]{2,1,0:T(8,128)S(1)}, f32[16,8,128]{2,1,0:T(8,128)S(1)}) custom-call(f32[1024,128]{1,0:T(8,128)S(1)} %bitcast.14, f32[16,64,128]{2,1,0:T(8,128)S(1)} %shard_map.103.ht_ref), custom_call_target="tpu_custom_call" | custom-call | tf_op jit(solution)/shard_map/pallas_call | solution.py:391
  3.6 2.2 %collective-permute-start = (f32[16,8,128]{2,1,0:T(8,128)S(1)}, f32[16,8,128]{2,1,0:T(8,128)S(1)}, u32[]{:S(2)}, u32[]{:S(2)}) collective-permute-start(f32[16,8,128]{2,1,0:T(8,128)S(1)} %get-tuple-element.23), channel_id=1, source_target_pairs={{0,1},{1,2},{2,3},{3,4},{4,5},{5,6},{6,7},{7,8},{8,9},{9,10},{10,1... | collective-permute-start | bytes 196616 | tf_op jit(solution)/shard_map/ppermute | solution.py:403
  5.8 0.0 collective-permute-start.1
  5.8 0.0 copy-done.4
  5.8 0.0 copy-start.6
  5.8 0.0 copy-start.7
  5.8 1.9 %shard_map.105.cond_ref = f32[26,80,128]{2,1,0:T(8,128)S(1)} custom-call(f32[64,8]{1,0:T(8,128)S(1)} %bitcast.17), custom_call_target="tpu_custom_call" | custom-call | tf_op jit(solution)/shard_map/pallas_call | solution.py:391
  7.7 0.0 collective-permute-done.nlo_ref
  7.7 3.9 %collective-permute-done.1.nhi_ref = f32[16,8,128]{2,1,0:T(8,128)S(1)} collective-permute-done((f32[16,8,128]{2,1,0:T(8,128)S(1)}, f32[16,8,128]{2,1,0:T(8,128)S(1)}, u32[]{:S(2)}, u32[]{:S(2)}) %collective-permute-start.1) | collective-permute-done | bytes 65568 | tf_op jit(solution)/shard_map/ppermute | solution.py:403
  11.6 3.1 %collective-permute-start.2 = (f32[608,128]{1,0:T(8,128)S(1)}, f32[608,128]{1,0:T(8,128)S(1)}, u32[]{:S(2)}, u32[]{:S(2)}) collective-permute-start(f32[608,128]{1,0:T(8,128)S(1)} %get-tuple-element.34), channel_id=1, source_target_pairs={{0,16},{16,32},{32,48},{48,64},{64,80},{80,96},{96,112},{112,128},... | collective-permute-start | bytes 933896 | tf_op jit(solution)/shard_map/ppermute | solution.py:403
  14.7 4.7 %collective-permute-start.3 = (f32[608,128]{1,0:T(8,128)S(1)}, f32[608,128]{1,0:T(8,128)S(1)}, u32[]{:S(2)}, u32[]{:S(2)}) collective-permute-start(f32[608,128]{1,0:T(8,128)S(1)} %get-tuple-element.35), channel_id=1, source_target_pairs={{0,240},{16,0},{32,16},{48,32},{64,48},{80,64},{96,80},{112,96},{1... | collective-permute-start | bytes 933896 | tf_op jit(solution)/shard_map/ppermute | solution.py:403
  19.4 0.0 copy-done.6
  19.4 0.1 broadcast_in_dim.8
  19.5 0.0 copy-done.7
  19.5 0.1 copy.11.count_ref
  19.6 0.0 copy-start.3
  19.6 8.0 %shard_map.106 = (f32[16,88,128]{2,1,0:T(8,128)S(1)}, f32[16,88,128]{2,1,0:T(8,128)S(1)}, f32[16,88,128]{2,1,0:T(8,128)S(1)}, f32[16,88,128]{2,1,0:T(8,128)S(1)}...) custom-call(f32[16,64,128]{2,1,0:T(8,128)S(1)} %shard_map.103.ht_ref, ...), custom_call_target="tpu_custom_call" | custom-call | tf_op jit(solution)/shard_map/pallas_call | solution.py:391
  27.5 0.0 copy-done.3
  27.6 3.3 %shard_map.110.part_ref = f32[8,4096]{1,0:T(8,128)S(1)} custom-call(bf16[1152,256]{1,0:T(8,128)(2,1)S(1)} %get-tuple-element.38.table_ref, s32[32,128]{1,0:T(8,128)S(1)} %bitcast.15), custom_call_target="tpu_custom_call" | custom-call | tf_op jit(solution)/shard_map/pallas_call | solution.py:391
  30.9 0.0 collective-permute-done.2.elo_ref
  30.9 0.0 collective-permute-done.3.ehi_ref
  30.9 0.0 copy-start.2
  30.9 0.0 copy-start.5
  30.9 6.7 %shard_map.108 = (f32[16,64,128]{2,1,0:T(8,128)S(1)}, bf16[1920,256]{1,0:T(8,128)(2,1)S(1)}) custom-call(f32[16,88,128]{2,1,0:T(8,128)S(1)} %get-tuple-element.28.ha0, f32[16,88,128]{2,1,0:T(8,128)S(1)} %get-tuple-element.29.hb0, f32[16,88,128]{2,1,0:T(8,128)S(1)} %get-tuple-element.30.ka0, f32[16,88,128]{2,1,0:T(8,128)S(1)} %get-tuple-element.31.kb0, ...), custom_call_target="tpu_custom_call" | custom-call | tf_op jit(solution)/shard_map/pallas_call | solution.py:391
  37.7 0.1 broadcast_in_dim.9.couple_ref
  37.7 0.0 copy-done.2
  37.7 0.0 copy-done.5
  37.7 6.9 %shard_map.111 = (f32[32,4096]{1,0:T(8,128)}, f32[4,32,512]{2,1,0:T(8,128)S(1)}) custom-call(bf16[1920,256]{1,0:T(8,128)(2,1)S(1)} %get-tuple-element.37.table_ref, s32[32,128]{1,0:T(8,128)S(1)} %bitcast.16, f32[8,4096]{1,0:T(8,128)S(1)} %shard_map.110.part_ref, f32[32,4096]{1,0:T(8,128)S(1)} %copy-done.2, f32[96,128]{1,0:T(8,128)S(1)} %broadcast_in_dim.9.couple_ref, ...), custom_call_target="tpu_custom_call" | custom-call | tf_op jit(solution)/shard_map/pallas_call | solution.py:391
  44.7 3.0 %collective-permute-start.4 = (f32[32,512]{1,0:T(8,128)S(1)}, f32[32,512]{1,0:T(8,128)S(1)}, u32[]{:S(2)}, u32[]{:S(2)}) collective-permute-start(f32[32,512]{1,0:T(8,128)S(1)} %get-tuple-element.44), channel_id=1, source_target_pairs={{0,16},{16,32},{32,48},{48,64},{64,80},{80,96},{96,112},{112,128},... | collective-permute-start | bytes 196616 | tf_op jit(solution)/shard_map/ppermute | solution.py:403
  47.7 2.8 %collective-permute-start.5 = (f32[32,512]{1,0:T(8,128)S(1)}, f32[32,512]{1,0:T(8,128)S(1)}, u32[]{:S(2)}, u32[]{:S(2)}) collective-permute-start(f32[32,512]{1,0:T(8,128)S(1)} %get-tuple-element.43), channel_id=1, source_target_pairs={{0,240},{16,0},{32,16},{48,32},{64,48},{80,64},{96,80},{112,96},{1... | collective-permute-start | bytes 196616 | tf_op jit(solution)/shard_map/ppermute | solution.py:403
  50.5 3.2 %collective-permute-start.6 = (f32[32,512]{1,0:T(8,128)S(1)}, f32[32,512]{1,0:T(8,128)S(1)}, u32[]{:S(2)}, u32[]{:S(2)}) collective-permute-start(f32[32,512]{1,0:T(8,128)S(1)} %get-tuple-element.42), channel_id=1, source_target_pairs={{0,1},{1,2},{2,3},{3,4},{4,5},{5,6},{6,7},{7,8},{8,9},{9,10},{10,1... | collective-permute-start | bytes 196616 | tf_op jit(solution)/shard_map/ppermute | solution.py:403
  53.7 0.0 collective-permute-start.7
  53.7 1.3 %shard_map.109 = f32[1024,128]{1,0:T(8,128)} custom-call(f32[16,64,128]{2,1,0:T(8,128)S(1)} %get-tuple-element.36.ht_ref), custom_call_target="tpu_custom_call" | custom-call | tf_op jit(solution)/shard_map/pallas_call | solution.py:391
  55.0 0.0 collective-permute-done.4.a_ref
  55.0 0.0 collective-permute-done.5.b_ref
  55.0 0.0 collective-permute-done.6.c_ref
  55.0 4.5 %collective-permute-done.7.d_ref = f32[32,512]{1,0:T(8,128)S(1)} collective-permute-done((f32[32,512]{1,0:T(8,128)S(1)}, f32[32,512]{1,0:T(8,128)S(1)}, u32[]{:S(2)}, u32[]{:S(2)}) %collective-permute-start.7) | collective-permute-done | bytes 65568 | tf_op jit(solution)/shard_map/ppermute | solution.py:403
  59.5 0.7 %shard_map.112 = f32[4,32,512]{2,1,0:T(8,128)} custom-call(f32[32,512]{1,0:T(8,128)S(1)} %collective-permute-done.4.a_ref, f32[32,512]{1,0:T(8,128)S(1)} %collective-permute-done.5.b_ref, f32[32,512]{1,0:T(8,128)S(1)} %collective-permute-done.6.c_ref, f32[32,512]{1,0:T(8,128)S(1)} %collective-permute-done.7.d_ref), custom_call_target="tpu_custom_call" | custom-call | tf_op jit(solution)/shard_map/pallas_call | solution.py:391
  (3 shorter events, 0.1 us)
Async XLA Ops:
  0.6 1.0 %copy-start = (f32[64,16,128]{2,1,0:T(8,128)S(1)}, f32[64,16,128]{2,1,0:T(8,128)}, u32[]{:S(2)}) copy-start(f32[64,16,128]{2,1,0:T(8,128)} %param.8) | copy-start | bytes 1572868
  1.7 1.0 %copy-start.1 = (f32[64,16,128]{2,1,0:T(8,128)S(1)}, f32[64,16,128]{2,1,0:T(8,128)}, u32[]{:S(2)}) copy-start(f32[64,16,128]{2,1,0:T(8,128)} %param.9) | copy-start | bytes 1572868
  1.7 4.1 %copy-start.4 = (f32[8,8,8]{2,1,0:T(8,128)S(1)}, f32[8,8,8]{2,1,0:T(8,128)}, u32[]{:S(2)}) copy-start(f32[8,8,8]{2,1,0:T(8,128)} %param.10) | copy-start | bytes 6148
  3.6 4.1 %collective-permute-start = (f32[16,8,128]{2,1,0:T(8,128)S(1)}, f32[16,8,128]{2,1,0:T(8,128)S(1)}, u32[]{:S(2)}, u32[]{:S(2)}) collective-permute-start(f32[16,8,128]{2,1,0:T(8,128)S(1)} %get-tuple-element.23), channel_id=1, source_target_pairs={{0,1},{1,2},{2,3},{3,4},{4,5},{5,6},{6,7},{7,8},{8,9},{9,10},{10,1... | collective-permute-start | bytes 196616 | tf_op jit(solution)/shard_map/ppermute | solution.py:403
  5.8 5.8 %collective-permute-start.1 = (f32[16,8,128]{2,1,0:T(8,128)S(1)}, f32[16,8,128]{2,1,0:T(8,128)S(1)}, u32[]{:S(2)}, u32[]{:S(2)}) collective-permute-start(f32[16,8,128]{2,1,0:T(8,128)S(1)} %get-tuple-element.24), channel_id=1, source_target_pairs={{0,15},{1,0},{2,1},{3,2},{4,3},{5,4},{6,5},{7,6},{8,7},{9,8},{10,9... | collective-permute-start | bytes 196616 | tf_op jit(solution)/shard_map/ppermute | solution.py:403
  5.8 13.6 %copy-start.6 = (f32[3,32]{1,0:T(4,128)S(1)}, f32[3,32]{1,0:T(4,128)}, u32[]{:S(2)}) copy-start(f32[3,32]{1,0:T(4,128)} %param.13) | copy-start | bytes 1156
  5.8 13.7 %copy-start.7 = (s32[4,1]{0,1:T(1,128)S(1)}, s32[4,1]{0,1:T(1,128)}, u32[]{:S(2)}) copy-start(s32[4,1]{0,1:T(1,128)} %param.15) | copy-start | bytes 52
  11.6 19.2 %collective-permute-start.2 = (f32[608,128]{1,0:T(8,128)S(1)}, f32[608,128]{1,0:T(8,128)S(1)}, u32[]{:S(2)}, u32[]{:S(2)}) collective-permute-start(f32[608,128]{1,0:T(8,128)S(1)} %get-tuple-element.34), channel_id=1, source_target_pairs={{0,16},{16,32},{32,48},{48,64},{64,80},{80,96},{96,112},{112,128},... | collective-permute-start | bytes 933896 | tf_op jit(solution)/shard_map/ppermute | solution.py:403
  14.7 16.2 %collective-permute-start.3 = (f32[608,128]{1,0:T(8,128)S(1)}, f32[608,128]{1,0:T(8,128)S(1)}, u32[]{:S(2)}, u32[]{:S(2)}) collective-permute-start(f32[608,128]{1,0:T(8,128)S(1)} %get-tuple-element.35), channel_id=1, source_target_pairs={{0,240},{16,0},{32,16},{48,32},{64,48},{80,64},{96,80},{112,96},{1... | collective-permute-start | bytes 933896 | tf_op jit(solution)/shard_map/ppermute | solution.py:403
  19.6 8.0 %copy-start.3 = (s32[4096]{0:T(1024)S(1)}, s32[4096]{0:T(1024)}, u32[]{:S(2)}) copy-start(s32[4096]{0:T(1024)} %param.12) | copy-start | bytes 49156
  30.9 6.8 %copy-start.2 = (f32[32,4096]{1,0:T(8,128)S(1)}, f32[32,4096]{1,0:T(8,128)}, u32[]{:S(2)}) copy-start(f32[32,4096]{1,0:T(8,128)} %rec_ref.1) | copy-start | bytes 1572868
  30.9 6.8 %copy-start.5 = (s32[4,512]{1,0:T(4,128)S(1)}, s32[4,512]{1,0:T(4,128)}, u32[]{:S(2)}) copy-start(s32[4,512]{1,0:T(4,128)} %list_ref.1) | copy-start | bytes 24580
  44.7 10.3 %collective-permute-start.4 = (f32[32,512]{1,0:T(8,128)S(1)}, f32[32,512]{1,0:T(8,128)S(1)}, u32[]{:S(2)}, u32[]{:S(2)}) collective-permute-start(f32[32,512]{1,0:T(8,128)S(1)} %get-tuple-element.44), channel_id=1, source_target_pairs={{0,16},{16,32},{32,48},{48,64},{64,80},{80,96},{96,112},{112,128},... | collective-permute-start | bytes 196616 | tf_op jit(solution)/shard_map/ppermute | solution.py:403
  47.7 7.3 %collective-permute-start.5 = (f32[32,512]{1,0:T(8,128)S(1)}, f32[32,512]{1,0:T(8,128)S(1)}, u32[]{:S(2)}, u32[]{:S(2)}) collective-permute-start(f32[32,512]{1,0:T(8,128)S(1)} %get-tuple-element.43), channel_id=1, source_target_pairs={{0,240},{16,0},{32,16},{48,32},{64,48},{80,64},{96,80},{112,96},{1... | collective-permute-start | bytes 196616 | tf_op jit(solution)/shard_map/ppermute | solution.py:403
  50.5 4.6 %collective-permute-start.6 = (f32[32,512]{1,0:T(8,128)S(1)}, f32[32,512]{1,0:T(8,128)S(1)}, u32[]{:S(2)}, u32[]{:S(2)}) collective-permute-start(f32[32,512]{1,0:T(8,128)S(1)} %get-tuple-element.42), channel_id=1, source_target_pairs={{0,1},{1,2},{2,3},{3,4},{4,5},{5,6},{6,7},{7,8},{8,9},{9,10},{10,1... | collective-permute-start | bytes 196616 | tf_op jit(solution)/shard_map/ppermute | solution.py:403
  53.7 5.8 %collective-permute-start.7 = (f32[32,512]{1,0:T(8,128)S(1)}, f32[32,512]{1,0:T(8,128)S(1)}, u32[]{:S(2)}, u32[]{:S(2)}) collective-permute-start(f32[32,512]{1,0:T(8,128)S(1)} %get-tuple-element.41), channel_id=1, source_target_pairs={{0,15},{1,0},{2,1},{3,2},{4,3},{5,4},{6,5},{7,6},{8,7},{9,8},{10,9... | collective-permute-start | bytes 196616 | tf_op jit(solution)/shard_map/ppermute | solution.py:403

commit v5 on v4

--- a/solution.py
+++ b/solution.py
@@ -15,8 +15,8 @@
 MID = CX - 2 * WIDE
 OUT = CX - MID
 NX, NY = 256, 2048
-NSIDE = WIDE - 1
-ESEND = (WIDE + NSIDE) * HALF + NSIDE * 8
+SPAN = HALF + 8
+ESEND = 7 * SPAN
 STEP = 0.25
 F32 = jnp.float32
 VMEM = pl.BlockSpec(memory_space=pltpu.VMEM)
@@ -48,19 +48,6 @@
         st_ref[x] = s
         nlo_ref[x] = jnp.where(low, swap(ht_ref[x, HALF - 8 :]), s[HALF - 8 :])
         nhi_ref[x] = jnp.where(low, ht_ref[x, :8], swap(s[:8]))
-
-
-def pack_kernel(ht_ref, st_ref, nlo_ref, nhi_ref, elo_ref, ehi_ref):
-    upper = lax.broadcasted_iota(jnp.int32, (8, 128), 0) < 4
-    for ref, at, at_s in ((elo_ref, CX - WIDE, CX - NSIDE), (ehi_ref, 0, 0)):
-        row = 0
-        for source, start, count in ((ht_ref, at, WIDE), (st_ref, at_s, NSIDE)):
-            for i in range(count):
-                ref[row : row + HALF] = source[start + i]
-                row += HALF
-        for i in range(NSIDE):
-            ref[row : row + 8] = jnp.where(upper, nhi_ref[at_s + i], nlo_ref[at_s + i])
-            row += 8
 
 
 def cond_kernel(modes_ref, out_ref, work_ref, xrow_ref):
@@ -208,6 +195,37 @@
             split(table_ref, pl.ds(pl.multiple_of(row + c * size + r, 16), 16), flow)
 
 
+def own_row(x, at, ht_ref, st_ref, nlo_ref, nhi_ref, cond_ref, ha, ka, sto_ref, src_ref):
+    cond = lambda r: cond_ref[x + WIDE, r : r + 8]
+    start_row(at, ht_ref[x], st_ref[x], nlo_ref[x], nhi_ref[x], cond, ha, ka, sto_ref, src_ref)
+
+
+def edge_kernel(
+    ht_ref, st_ref, nlo_ref, nhi_ref, cond_ref, up_ref, down_ref,
+    ha, hb, ka, kb, sto_ref, src_ref, count_ref, mask_ref,
+):
+    grid_tables(count_ref, mask_ref)
+    clear_pads((hb, kb))
+    tables = (cond_ref, sto_ref, src_ref, count_ref, mask_ref)
+    for send_ref, first_x, a, b in ((up_ref, CX - WIDE, WIDE - 1, WIDE - 2), (down_ref, 0, 0, 1)):
+
+        def own(at, carry, first_x=first_x):
+            own_row(first_x + at, at, ht_ref, st_ref, nlo_ref, nhi_ref, cond_ref, ha, ka, sto_ref, src_ref)
+            return carry
+
+        lax.fori_loop(0, WIDE, own, 0)
+
+        def sweep(at, carry, first_x=first_x):
+            sweep_row(at, WIDE + first_x + at, ha, ka, hb, kb, *tables)
+            return carry
+
+        lax.fori_loop(1, 4, sweep, 0)
+        sweep_row(2, WIDE + first_x + 2, hb, kb, ha, ka, *tables)
+        parts = ((ha, a, 8), (ha, b, 8), (src_ref, a, 4), (src_ref, b, 4), (hb, b, 8), (hb, 2, 8), (ha, 2, 8))
+        for n, (source, at, r) in enumerate(parts):
+            send_ref[n * SPAN : (n + 1) * SPAN] = source[at, r : r + SPAN]
+
+
 def inner_kernel(
     ht_ref, st_ref, nlo_ref, nhi_ref, cond_ref,
     ha, hb, ka, kb, sto_ref, src_ref, table_ref,
@@ -246,7 +264,7 @@
 ):
     east = lax.axis_index("east")
     grid_tables(count_ref, mask_ref)
-    clear_pads((hb, kb))
+    clear_pads((ha, hb, ka, kb))
     for x in range(CX):
         depth = min(x, CX - 1 - x)
         if depth <= WIDE:
@@ -257,30 +275,27 @@
         for i in range(ITERS):
             big[WIDE + i] = small[i]
             big[EXT - 1 - WIDE - i] = small[CX - 1 - i]
-    zero = jnp.zeros((8, 128), F32)
-    for ref, valid, first, flip in ((elo_ref, east > 0, 0, 0), (ehi_ref, east < 15, EXT - WIDE, 1)):
-        for i in range(WIDE):
-            xi = first + i
-            h = jnp.where(valid, ref[i * HALF : (i + 1) * HALF], 0.0)
-            s, corner = None, zero
-            j = i if flip else i - 1
-            if 0 <= j < NSIDE:
-                s_at = (WIDE + j) * HALF
-                c_at = (WIDE + NSIDE) * HALF + j * 8
-                s = jnp.where(valid, ref[s_at : s_at + HALF], 0.0)
-                corner = jnp.where(valid, ref[c_at : c_at + 8], 0.0)
-            cond = lambda r, xi=xi: cond_ref[xi, r : r + 8]
-            start_row(xi, h, s, corner, corner, cond, ha, ka, sto_ref, src_ref)
+    for ref, valid, near, out in ((elo_ref, east > 0, WIDE - 1, -1), (ehi_ref, east < 15, EXT - WIDE, 1)):
+        block = lambda n, ref=ref, valid=valid: jnp.where(valid, ref[n * SPAN : (n + 1) * SPAN], 0.0)
+        for n, big_h, big_k, depth in ((0, ha, ka, 0), (1, ha, ka, 1), (4, hb, kb, 1), (5, hb, kb, 2), (6, ha, ka, 2)):
+            xi = near + out * depth
+            h = block(n)
+            relative = rel(h)
+            big_h[xi, 8 : 8 + SPAN] = h
+            big_k[xi, 8 : 8 + SPAN] = cond_ref[xi, 4 : 4 + SPAN] * relative
+            if n < 2:
+                sto_ref[xi, 4 : 4 + SPAN] = 0.5 + 0.5 * relative
+                src_ref[xi, 4 : 4 + SPAN] = block(n + 2)
 
     hin, kin, hout, kout = ha, ka, hb, kb
-    for number in range(1, ITERS + 1):
-
-        def sweep(i, carry, number=number, hin=hin, kin=kin, hout=hout, kout=kout):
-            xi = number + i + jnp.where(i < WIDE, 0, EXT - 2 * WIDE - 2 * number)
+    for first, count in ((4, 2), (3, 4), (3, 5), (4, 5)):
+
+        def sweep(i, carry, first=first, count=count, hin=hin, kin=kin, hout=hout, kout=kout):
+            xi = jnp.where(i < count, first + i, EXT - 1 - first - (i - count))
             sweep_row(xi, xi, hin, kin, hout, kout, cond_ref, sto_ref, src_ref, count_ref, mask_ref)
             return carry
 
-        lax.fori_loop(0, 2 * WIDE, sweep, 0)
+        lax.fori_loop(0, 2 * count, sweep, 0)
         hin, kin, hout, kout = hout, kout, hin, kin
 
     for x in range(CX):
@@ -420,10 +435,17 @@
     )
     nlo, nhi, cond = lax.optimization_barrier((nlo, nhi, cond))
     edge = ((ESEND, 128), F32)
-    e_up, e_down = call(pack_kernel, [edge, edge], [ht, st, nlo, nhi])
+    plane = pltpu.VMEM((ROWS, 128), F32)
+    some, some_base = pltpu.VMEM((WIDE, PAD, 128), F32), pltpu.VMEM((WIDE, ROWS, 128), F32)
+    e_up, e_down = call(
+        edge_kernel,
+        [edge, edge],
+        [ht, st, nlo, nhi, cond],
+        [some] * 4 + [some_base] * 2 + [plane, plane],
+        limit=8,
+    )
     elo = ring(e_up, "east", 1)
     ehi = ring(e_down, "east", -1)
-    plane = pltpu.VMEM((ROWS, 128), F32)
     level = ((CX, PAD, 128), F32)
     base = ((CX, ROWS, 128), F32)
     cells = cell_index.reshape(32, 128)

time: 60.3 us -> 58.8 us (0.975)
  starting transfers between devices: 18.9 us -> 16.6 us
  Pallas kernels: 30.3 us -> 31.1 us
    ppermute x8, starting transfers between devices: 18.9 us -> 16.6 us  [ring(): lax.ppermute(value, axis, [(i, (i + steps) % count) for i in range(count)])]
    pallas_call x10, Pallas kernels: 30.3 us -> 31.1 us  [call(): pl.pallas_call(kernel, out_shape=[jax.ShapeDtypeStruct(s, t) for s, t in...]
  transfers between devices with their start and end apart: 8 -> 8, of which waited for: 2 -> 2; matrix products, arithmetic and copies ran while one was open for 0% -> 0% of each run, Pallas kernels for 24% -> 25%
where the time goes in v5:
time: 58.8 us; the launch traced here: 58.7 us
  Pallas kernels  31.1 us (53%)
  starting transfers between devices  16.6 us (28%)
  waiting for transfers between devices  8.35 us (14%)
  local copies, waits for them, and re-layouts  1.87 us (3%)
  between operations  0.76 us (1%)
    pallas_call x10, Pallas kernels, call(): pl.pallas_call(kernel, out_shape=[jax.ShapeDtypeStruct(s, t) for s, t in...  31.1 us
    ppermute x8, starting transfers between devices, ring(): lax.ppermute(value, axis, [(i, (i + steps) % count) for i in range(count)])  16.6 us
    ppermute x8, waiting for transfers between devices, ring(): lax.ppermute(value, axis, [(i, (i + steps) % count) for i in range(count)])  8.35 us
    unnamed x17, local copies, waits for them, and re-layouts  1.69 us
  transfers between devices with their start and end apart: 8, of which 2 were waited for; matrix products, arithmetic and copies ran while one was open for 0% of the time, Pallas kernels for 25%

profile of v5, /device:TPU:7, one launch (start us, length us, event | category | flops | bytes accessed | tf_op | source)
XLA Modules:
  0.0 58.7 jit_solution(15070707456663622170)
XLA Ops:
  0.6 0.0 copy-start
  0.6 1.0 %copy-done = f32[64,16,128]{2,1,0:T(8,128)S(1)} copy-done((f32[64,16,128]{2,1,0:T(8,128)S(1)}, f32[64,16,128]{2,1,0:T(8,128)}, u32[]{:S(2)}) %copy-start) | copy-done | bytes 524312
  1.7 0.0 copy-start.1
  1.7 0.0 copy-start.4
  1.7 0.5 shard_map.103.ht_ref
  2.2 0.5 copy-done.1
  2.7 0.9 %shard_map.104 = (f32[16,64,128]{2,1,0:T(8,128)S(1)}, f32[16,8,128]{2,1,0:T(8,128)S(1)}, f32[16,8,128]{2,1,0:T(8,128)S(1)}) custom-call(f32[1024,128]{1,0:T(8,128)S(1)} %bitcast.14, f32[16,64,128]{2,1,0:T(8,128)S(1)} %shard_map.103.ht_ref), custom_call_target="tpu_custom_call" | custom-call | tf_op jit(solution)/shard_map/pallas_call | solution.py:406
  3.6 2.2 %collective-permute-start = (f32[16,8,128]{2,1,0:T(8,128)S(1)}, f32[16,8,128]{2,1,0:T(8,128)S(1)}, u32[]{:S(2)}, u32[]{:S(2)}) collective-permute-start(f32[16,8,128]{2,1,0:T(8,128)S(1)} %get-tuple-element.23), channel_id=1, source_target_pairs={{0,1},{1,2},{2,3},{3,4},{4,5},{5,6},{6,7},{7,8},{8,9},{9,10},{10,1... | collective-permute-start | bytes 196616 | tf_op jit(solution)/shard_map/ppermute | solution.py:418
  5.8 0.0 collective-permute-start.1
  5.8 0.0 copy-done.4
  5.8 1.9 %shard_map.105.cond_ref = f32[26,80,128]{2,1,0:T(8,128)S(1)} custom-call(f32[64,8]{1,0:T(8,128)S(1)} %bitcast.17), custom_call_target="tpu_custom_call" | custom-call | tf_op jit(solution)/shard_map/pallas_call | solution.py:406
  7.7 0.0 collective-permute-done.nlo_ref
  7.7 3.9 %collective-permute-done.1.nhi_ref = f32[16,8,128]{2,1,0:T(8,128)S(1)} collective-permute-done((f32[16,8,128]{2,1,0:T(8,128)S(1)}, f32[16,8,128]{2,1,0:T(8,128)S(1)}, u32[]{:S(2)}, u32[]{:S(2)}) %collective-permute-start.1) | collective-permute-done | bytes 65568 | tf_op jit(solution)/shard_map/ppermute | solution.py:418
  11.6 0.0 copy-start.6
  11.6 0.0 copy-start.7
  11.6 2.0 %shard_map.107 = (f32[504,128]{1,0:T(8,128)S(1)}, f32[504,128]{1,0:T(8,128)S(1)}) custom-call(f32[16,64,128]{2,1,0:T(8,128)S(1)} %shard_map.103.ht_ref, f32[16,64,128]{2,1,0:T(8,128)S(1)} %get-tuple-element.22.st_ref, f32[16,8,128]{2,1,0:T(8,128)S(1)} %collective-permute-done.nlo_ref, f32[16,8,128]{2,1,0:T(8,128)S(1)} %collective-permute-done.1.nhi_ref, ...), custom_call_target="tpu_custom_call" | custom-call | tf_op jit(solution)/shard_map/pallas_call | solution.py:406
  13.6 3.1 %collective-permute-start.2 = (f32[504,128]{1,0:T(8,128)S(1)}, f32[504,128]{1,0:T(8,128)S(1)}, u32[]{:S(2)}, u32[]{:S(2)}) collective-permute-start(f32[504,128]{1,0:T(8,128)S(1)} %get-tuple-element.34), channel_id=1, source_target_pairs={{0,16},{16,32},{32,48},{48,64},{64,80},{80,96},{96,112},{112,128},... | collective-permute-start | bytes 774152 | tf_op jit(solution)/shard_map/ppermute | solution.py:418
  16.6 4.7 %collective-permute-start.3 = (f32[504,128]{1,0:T(8,128)S(1)}, f32[504,128]{1,0:T(8,128)S(1)}, u32[]{:S(2)}, u32[]{:S(2)}) collective-permute-start(f32[504,128]{1,0:T(8,128)S(1)} %get-tuple-element.35), channel_id=1, source_target_pairs={{0,240},{16,0},{32,16},{48,32},{64,48},{80,64},{96,80},{112,96},{1... | collective-permute-start | bytes 774152 | tf_op jit(solution)/shard_map/ppermute | solution.py:418
  21.3 0.0 copy-done.6
  21.3 0.1 broadcast_in_dim.8
  21.4 0.0 copy-done.7
  21.4 0.1 copy.11.count_ref
  21.5 0.0 copy-start.3
  21.5 8.0 %shard_map.106 = (f32[16,88,128]{2,1,0:T(8,128)S(1)}, f32[16,88,128]{2,1,0:T(8,128)S(1)}, f32[16,88,128]{2,1,0:T(8,128)S(1)}, f32[16,88,128]{2,1,0:T(8,128)S(1)}...) custom-call(f32[16,64,128]{2,1,0:T(8,128)S(1)} %shard_map.103.ht_ref, ...), custom_call_target="tpu_custom_call" | custom-call | tf_op jit(solution)/shard_map/pallas_call | solution.py:406
  29.5 0.0 copy-done.3
  29.5 3.3 %shard_map.110.part_ref = f32[8,4096]{1,0:T(8,128)S(1)} custom-call(bf16[1152,256]{1,0:T(8,128)(2,1)S(1)} %get-tuple-element.38.table_ref, s32[32,128]{1,0:T(8,128)S(1)} %bitcast.15), custom_call_target="tpu_custom_call" | custom-call | tf_op jit(solution)/shard_map/pallas_call | solution.py:406
  32.8 0.0 collective-permute-done.2.elo_ref
  32.8 0.0 collective-permute-done.3.ehi_ref
  32.8 0.0 copy-start.2
  32.8 0.0 copy-start.5
  32.9 5.5 %shard_map.108 = (f32[16,64,128]{2,1,0:T(8,128)S(1)}, bf16[1920,256]{1,0:T(8,128)(2,1)S(1)}) custom-call(f32[16,88,128]{2,1,0:T(8,128)S(1)} %get-tuple-element.28.ha0, f32[16,88,128]{2,1,0:T(8,128)S(1)} %get-tuple-element.29.hb0, f32[16,88,128]{2,1,0:T(8,128)S(1)} %get-tuple-element.30.ka0, f32[16,88,128]{2,1,0:T(8,128)S(1)} %get-tuple-element.31.kb0, ...), custom_call_target="tpu_custom_call" | custom-call | tf_op jit(solution)/shard_map/pallas_call | solution.py:406
  38.4 0.1 broadcast_in_dim.9.couple_ref
  38.5 0.0 copy-done.2
  38.5 0.0 copy-done.5
  38.5 6.9 %shard_map.111 = (f32[32,4096]{1,0:T(8,128)}, f32[4,32,512]{2,1,0:T(8,128)S(1)}) custom-call(bf16[1920,256]{1,0:T(8,128)(2,1)S(1)} %get-tuple-element.37.table_ref, s32[32,128]{1,0:T(8,128)S(1)} %bitcast.16, f32[8,4096]{1,0:T(8,128)S(1)} %shard_map.110.part_ref, f32[32,4096]{1,0:T(8,128)S(1)} %copy-done.2, f32[96,128]{1,0:T(8,128)S(1)} %broadcast_in_dim.9.couple_ref, ...), custom_call_target="tpu_custom_call" | custom-call | tf_op jit(solution)/shard_map/pallas_call | solution.py:406
  45.4 0.7 %collective-permute-start.4 = (f32[32,512]{1,0:T(8,128)S(1)}, f32[32,512]{1,0:T(8,128)S(1)}, u32[]{:S(2)}, u32[]{:S(2)}) collective-permute-start(f32[32,512]{1,0:T(8,128)S(1)} %get-tuple-element.44), channel_id=1, source_target_pairs={{0,16},{16,32},{32,48},{48,64},{64,80},{80,96},{96,112},{112,128},... | collective-permute-start | bytes 196616 | tf_op jit(solution)/shard_map/ppermute | solution.py:418
  46.1 5.1 %collective-permute-start.5 = (f32[32,512]{1,0:T(8,128)S(1)}, f32[32,512]{1,0:T(8,128)S(1)}, u32[]{:S(2)}, u32[]{:S(2)}) collective-permute-start(f32[32,512]{1,0:T(8,128)S(1)} %get-tuple-element.43), channel_id=1, source_target_pairs={{0,240},{16,0},{32,16},{48,32},{64,48},{80,64},{96,80},{112,96},{1... | collective-permute-start | bytes 196616 | tf_op jit(solution)/shard_map/ppermute | solution.py:418
  51.2 0.9 %collective-permute-start.6 = (f32[32,512]{1,0:T(8,128)S(1)}, f32[32,512]{1,0:T(8,128)S(1)}, u32[]{:S(2)}, u32[]{:S(2)}) collective-permute-start(f32[32,512]{1,0:T(8,128)S(1)} %get-tuple-element.42), channel_id=1, source_target_pairs={{0,1},{1,2},{2,3},{3,4},{4,5},{5,6},{6,7},{7,8},{8,9},{9,10},{10,1... | collective-permute-start | bytes 196616 | tf_op jit(solution)/shard_map/ppermute | solution.py:418
  52.1 0.0 collective-permute-start.7
  52.1 1.3 %shard_map.109 = f32[1024,128]{1,0:T(8,128)} custom-call(f32[16,64,128]{2,1,0:T(8,128)S(1)} %get-tuple-element.36.ht_ref), custom_call_target="tpu_custom_call" | custom-call | tf_op jit(solution)/shard_map/pallas_call | solution.py:406
  53.5 0.0 collective-permute-done.4.a_ref
  53.5 0.0 collective-permute-done.5.b_ref
  53.5 0.0 collective-permute-done.6.c_ref
  53.5 4.4 %collective-permute-done.7.d_ref = f32[32,512]{1,0:T(8,128)S(1)} collective-permute-done((f32[32,512]{1,0:T(8,128)S(1)}, f32[32,512]{1,0:T(8,128)S(1)}, u32[]{:S(2)}, u32[]{:S(2)}) %collective-permute-start.7) | collective-permute-done | bytes 65568 | tf_op jit(solution)/shard_map/ppermute | solution.py:418
  57.9 0.7 %shard_map.112 = f32[4,32,512]{2,1,0:T(8,128)} custom-call(f32[32,512]{1,0:T(8,128)S(1)} %collective-permute-done.4.a_ref, f32[32,512]{1,0:T(8,128)S(1)} %collective-permute-done.5.b_ref, f32[32,512]{1,0:T(8,128)S(1)} %collective-permute-done.6.c_ref, f32[32,512]{1,0:T(8,128)S(1)} %collective-permute-done.7.d_ref), custom_call_target="tpu_custom_call" | custom-call | tf_op jit(solution)/shard_map/pallas_call | solution.py:406
  (2 shorter events, 0.0 us)
Async XLA Ops:
  0.6 1.0 %copy-start = (f32[64,16,128]{2,1,0:T(8,128)S(1)}, f32[64,16,128]{2,1,0:T(8,128)}, u32[]{:S(2)}) copy-start(f32[64,16,128]{2,1,0:T(8,128)} %param.8) | copy-start | bytes 1572868
  1.7 1.0 %copy-start.1 = (f32[64,16,128]{2,1,0:T(8,128)S(1)}, f32[64,16,128]{2,1,0:T(8,128)}, u32[]{:S(2)}) copy-start(f32[64,16,128]{2,1,0:T(8,128)} %param.9) | copy-start | bytes 1572868
  1.7 4.1 %copy-start.4 = (f32[8,8,8]{2,1,0:T(8,128)S(1)}, f32[8,8,8]{2,1,0:T(8,128)}, u32[]{:S(2)}) copy-start(f32[8,8,8]{2,1,0:T(8,128)} %param.10) | copy-start | bytes 6148
  3.6 4.1 %collective-permute-start = (f32[16,8,128]{2,1,0:T(8,128)S(1)}, f32[16,8,128]{2,1,0:T(8,128)S(1)}, u32[]{:S(2)}, u32[]{:S(2)}) collective-permute-start(f32[16,8,128]{2,1,0:T(8,128)S(1)} %get-tuple-element.23), channel_id=1, source_target_pairs={{0,1},{1,2},{2,3},{3,4},{4,5},{5,6},{6,7},{7,8},{8,9},{9,10},{10,1... | collective-permute-start | bytes 196616 | tf_op jit(solution)/shard_map/ppermute | solution.py:418
  5.8 5.8 %collective-permute-start.1 = (f32[16,8,128]{2,1,0:T(8,128)S(1)}, f32[16,8,128]{2,1,0:T(8,128)S(1)}, u32[]{:S(2)}, u32[]{:S(2)}) collective-permute-start(f32[16,8,128]{2,1,0:T(8,128)S(1)} %get-tuple-element.24), channel_id=1, source_target_pairs={{0,15},{1,0},{2,1},{3,2},{4,3},{5,4},{6,5},{7,6},{8,7},{9,8},{10,9... | collective-permute-start | bytes 196616 | tf_op jit(solution)/shard_map/ppermute | solution.py:418
  11.6 9.7 %copy-start.6 = (f32[3,32]{1,0:T(4,128)S(1)}, f32[3,32]{1,0:T(4,128)}, u32[]{:S(2)}) copy-start(f32[3,32]{1,0:T(4,128)} %param.13) | copy-start | bytes 1156
  11.6 9.8 %copy-start.7 = (s32[4,1]{0,1:T(1,128)S(1)}, s32[4,1]{0,1:T(1,128)}, u32[]{:S(2)}) copy-start(s32[4,1]{0,1:T(1,128)} %param.15) | copy-start | bytes 52
  13.6 19.2 %collective-permute-start.2 = (f32[504,128]{1,0:T(8,128)S(1)}, f32[504,128]{1,0:T(8,128)S(1)}, u32[]{:S(2)}, u32[]{:S(2)}) collective-permute-start(f32[504,128]{1,0:T(8,128)S(1)} %get-tuple-element.34), channel_id=1, source_target_pairs={{0,16},{16,32},{32,48},{48,64},{64,80},{80,96},{96,112},{112,128},... | collective-permute-start | bytes 774152 | tf_op jit(solution)/shard_map/ppermute | solution.py:418
  16.6 16.2 %collective-permute-start.3 = (f32[504,128]{1,0:T(8,128)S(1)}, f32[504,128]{1,0:T(8,128)S(1)}, u32[]{:S(2)}, u32[]{:S(2)}) collective-permute-start(f32[504,128]{1,0:T(8,128)S(1)} %get-tuple-element.35), channel_id=1, source_target_pairs={{0,240},{16,0},{32,16},{48,32},{64,48},{80,64},{96,80},{112,96},{1... | collective-permute-start | bytes 774152 | tf_op jit(solution)/shard_map/ppermute | solution.py:418
  21.5 8.0 %copy-start.3 = (s32[4096]{0:T(1024)S(1)}, s32[4096]{0:T(1024)}, u32[]{:S(2)}) copy-start(s32[4096]{0:T(1024)} %param.12) | copy-start | bytes 49156
  32.8 5.7 %copy-start.2 = (f32[32,4096]{1,0:T(8,128)S(1)}, f32[32,4096]{1,0:T(8,128)}, u32[]{:S(2)}) copy-start(f32[32,4096]{1,0:T(8,128)} %rec_ref.1) | copy-start | bytes 1572868
  32.8 5.6 %copy-start.5 = (s32[4,512]{1,0:T(4,128)S(1)}, s32[4,512]{1,0:T(4,128)}, u32[]{:S(2)}) copy-start(s32[4,512]{1,0:T(4,128)} %list_ref.1) | copy-start | bytes 24580
  45.4 8.1 %collective-permute-start.4 = (f32[32,512]{1,0:T(8,128)S(1)}, f32[32,512]{1,0:T(8,128)S(1)}, u32[]{:S(2)}, u32[]{:S(2)}) collective-permute-start(f32[32,512]{1,0:T(8,128)S(1)} %get-tuple-element.44), channel_id=1, source_target_pairs={{0,16},{16,32},{32,48},{48,64},{64,80},{80,96},{96,112},{112,128},... | collective-permute-start | bytes 196616 | tf_op jit(solution)/shard_map/ppermute | solution.py:418
  46.1 7.4 %collective-permute-start.5 = (f32[32,512]{1,0:T(8,128)S(1)}, f32[32,512]{1,0:T(8,128)S(1)}, u32[]{:S(2)}, u32[]{:S(2)}) collective-permute-start(f32[32,512]{1,0:T(8,128)S(1)} %get-tuple-element.43), channel_id=1, source_target_pairs={{0,240},{16,0},{32,16},{48,32},{64,48},{80,64},{96,80},{112,96},{1... | collective-permute-start | bytes 196616 | tf_op jit(solution)/shard_map/ppermute | solution.py:418
  51.2 2.3 %collective-permute-start.6 = (f32[32,512]{1,0:T(8,128)S(1)}, f32[32,512]{1,0:T(8,128)S(1)}, u32[]{:S(2)}, u32[]{:S(2)}) collective-permute-start(f32[32,512]{1,0:T(8,128)S(1)} %get-tuple-element.42), channel_id=1, source_target_pairs={{0,1},{1,2},{2,3},{3,4},{4,5},{5,6},{6,7},{7,8},{8,9},{9,10},{10,1... | collective-permute-start | bytes 196616 | tf_op jit(solution)/shard_map/ppermute | solution.py:418
  52.1 5.8 %collective-permute-start.7 = (f32[32,512]{1,0:T(8,128)S(1)}, f32[32,512]{1,0:T(8,128)S(1)}, u32[]{:S(2)}, u32[]{:S(2)}) collective-permute-start(f32[32,512]{1,0:T(8,128)S(1)} %get-tuple-element.41), channel_id=1, source_target_pairs={{0,15},{1,0},{2,1},{3,2},{4,3},{5,4},{6,5},{7,6},{8,7},{9,8},{10,9... | collective-permute-start | bytes 196616 | tf_op jit(solution)/shard_map/ppermute | solution.py:418

commit v6 on v5

--- a/solution.py
+++ b/solution.py
@@ -355,7 +355,7 @@
             part_ref[c : c + 1, at] = sampled
         return carry
 
-    lax.fori_loop(0, 4096 // BLOCK, block, 0, unroll=2)
+    lax.fori_loop(0, 4096 // BLOCK, block, 0, unroll=4)
 
 
 def sample_kernel(
@@ -377,7 +377,7 @@
             split(pick_ref, rows, total[:, i * 128 : (i + 1) * 128])
         return carry
 
-    lax.fori_loop(0, 4096 // BLOCK, block, 0, unroll=2)
+    lax.fori_loop(0, 4096 // BLOCK, block, 0, unroll=4)
     for d in range(4):
         index = list_ref[d : d + 1, :]
         got = jnp.dot(pick_ref[...], onehot_pair(index & 127), preferred_element_type=F32)

time: 58.8 us -> 58.4 us (level)
  Pallas kernels: 31.1 us -> 30.3 us
    pallas_call x10, Pallas kernels: 31.1 us -> 30.3 us  [call(): pl.pallas_call(kernel, out_shape=[jax.ShapeDtypeStruct(s, t) for s, t in...]
  transfers between devices with their start and end apart: 8 -> 8, of which waited for: 2 -> 2; matrix products, arithmetic and copies ran while one was open for 0% -> 0% of each run, Pallas kernels for 25% -> 24%
where the time goes in v6:
time: 58.4 us; the launch traced here: 58.2 us
  Pallas kernels  30.3 us (52%)
  starting transfers between devices  17 us (29%)
  waiting for transfers between devices  8.35 us (14%)
  local copies, waits for them, and re-layouts  1.87 us (3%)
  between operations  0.77 us (1%)
    pallas_call x10, Pallas kernels, call(): pl.pallas_call(kernel, out_shape=[jax.ShapeDtypeStruct(s, t) for s, t in...  30.3 us
    ppermute x8, starting transfers between devices, ring(): lax.ppermute(value, axis, [(i, (i + steps) % count) for i in range(count)])  17 us
    ppermute x8, waiting for transfers between devices, ring(): lax.ppermute(value, axis, [(i, (i + steps) % count) for i in range(count)])  8.35 us
    unnamed x17, local copies, waits for them, and re-layouts  1.69 us
  transfers between devices with their start and end apart: 8, of which 2 were waited for; matrix products, arithmetic and copies ran while one was open for 0% of the time, Pallas kernels for 24%

profile of v6, /device:TPU:7, one launch (start us, length us, event | category | flops | bytes accessed | tf_op | source)
XLA Modules:
  0.0 58.2 jit_solution(8387785960065075926)
XLA Ops:
  0.6 0.0 copy-start
  0.6 1.0 %copy-done = f32[64,16,128]{2,1,0:T(8,128)S(1)} copy-done((f32[64,16,128]{2,1,0:T(8,128)S(1)}, f32[64,16,128]{2,1,0:T(8,128)}, u32[]{:S(2)}) %copy-start) | copy-done | bytes 524312
  1.7 0.0 copy-start.1
  1.7 0.0 copy-start.4
  1.7 0.5 shard_map.103.ht_ref
  2.2 0.5 copy-done.1
  2.7 0.9 %shard_map.104 = (f32[16,64,128]{2,1,0:T(8,128)S(1)}, f32[16,8,128]{2,1,0:T(8,128)S(1)}, f32[16,8,128]{2,1,0:T(8,128)S(1)}) custom-call(f32[1024,128]{1,0:T(8,128)S(1)} %bitcast.14, f32[16,64,128]{2,1,0:T(8,128)S(1)} %shard_map.103.ht_ref), custom_call_target="tpu_custom_call" | custom-call | tf_op jit(solution)/shard_map/pallas_call | solution.py:406
  3.6 2.2 %collective-permute-start = (f32[16,8,128]{2,1,0:T(8,128)S(1)}, f32[16,8,128]{2,1,0:T(8,128)S(1)}, u32[]{:S(2)}, u32[]{:S(2)}) collective-permute-start(f32[16,8,128]{2,1,0:T(8,128)S(1)} %get-tuple-element.23), channel_id=1, source_target_pairs={{0,1},{1,2},{2,3},{3,4},{4,5},{5,6},{6,7},{7,8},{8,9},{9,10},{10,1... | collective-permute-start | bytes 196616 | tf_op jit(solution)/shard_map/ppermute | solution.py:418
  5.8 0.0 collective-permute-start.1
  5.8 0.0 copy-done.4
  5.8 1.9 %shard_map.105.cond_ref = f32[26,80,128]{2,1,0:T(8,128)S(1)} custom-call(f32[64,8]{1,0:T(8,128)S(1)} %bitcast.17), custom_call_target="tpu_custom_call" | custom-call | tf_op jit(solution)/shard_map/pallas_call | solution.py:406
  7.7 0.0 collective-permute-done.nlo_ref
  7.7 3.9 %collective-permute-done.1.nhi_ref = f32[16,8,128]{2,1,0:T(8,128)S(1)} collective-permute-done((f32[16,8,128]{2,1,0:T(8,128)S(1)}, f32[16,8,128]{2,1,0:T(8,128)S(1)}, u32[]{:S(2)}, u32[]{:S(2)}) %collective-permute-start.1) | collective-permute-done | bytes 65568 | tf_op jit(solution)/shard_map/ppermute | solution.py:418
  11.6 0.0 copy-start.6
  11.6 0.0 copy-start.7
  11.6 2.0 %shard_map.107 = (f32[504,128]{1,0:T(8,128)S(1)}, f32[504,128]{1,0:T(8,128)S(1)}) custom-call(f32[16,64,128]{2,1,0:T(8,128)S(1)} %shard_map.103.ht_ref, f32[16,64,128]{2,1,0:T(8,128)S(1)} %get-tuple-element.22.st_ref, f32[16,8,128]{2,1,0:T(8,128)S(1)} %collective-permute-done.nlo_ref, f32[16,8,128]{2,1,0:T(8,128)S(1)} %collective-permute-done.1.nhi_ref, ...), custom_call_target="tpu_custom_call" | custom-call | tf_op jit(solution)/shard_map/pallas_call | solution.py:406
  13.6 3.1 %collective-permute-start.2 = (f32[504,128]{1,0:T(8,128)S(1)}, f32[504,128]{1,0:T(8,128)S(1)}, u32[]{:S(2)}, u32[]{:S(2)}) collective-permute-start(f32[504,128]{1,0:T(8,128)S(1)} %get-tuple-element.34), channel_id=1, source_target_pairs={{0,16},{16,32},{32,48},{48,64},{64,80},{80,96},{96,112},{112,128},... | collective-permute-start | bytes 774152 | tf_op jit(solution)/shard_map/ppermute | solution.py:418
  16.6 4.9 %collective-permute-start.3 = (f32[504,128]{1,0:T(8,128)S(1)}, f32[504,128]{1,0:T(8,128)S(1)}, u32[]{:S(2)}, u32[]{:S(2)}) collective-permute-start(f32[504,128]{1,0:T(8,128)S(1)} %get-tuple-element.35), channel_id=1, source_target_pairs={{0,240},{16,0},{32,16},{48,32},{64,48},{80,64},{96,80},{112,96},{1... | collective-permute-start | bytes 774152 | tf_op jit(solution)/shard_map/ppermute | solution.py:418
  21.5 0.0 copy-done.6
  21.5 0.1 broadcast_in_dim.8
  21.6 0.0 copy-done.7
  21.6 0.1 copy.11.count_ref
  21.7 0.0 copy-start.3
  21.7 8.0 %shard_map.106 = (f32[16,88,128]{2,1,0:T(8,128)S(1)}, f32[16,88,128]{2,1,0:T(8,128)S(1)}, f32[16,88,128]{2,1,0:T(8,128)S(1)}, f32[16,88,128]{2,1,0:T(8,128)S(1)}...) custom-call(f32[16,64,128]{2,1,0:T(8,128)S(1)} %shard_map.103.ht_ref, ...), custom_call_target="tpu_custom_call" | custom-call | tf_op jit(solution)/shard_map/pallas_call | solution.py:406
  29.7 0.0 copy-done.3
  29.7 2.9 %shard_map.110.part_ref = f32[8,4096]{1,0:T(8,128)S(1)} custom-call(bf16[1152,256]{1,0:T(8,128)(2,1)S(1)} %get-tuple-element.38.table_ref, s32[32,128]{1,0:T(8,128)S(1)} %bitcast.15), custom_call_target="tpu_custom_call" | custom-call | tf_op jit(solution)/shard_map/pallas_call | solution.py:406
  32.6 0.0 collective-permute-done.2.elo_ref
  32.6 0.0 collective-permute-done.3.ehi_ref
  32.6 0.0 copy-start.2
  32.6 0.0 copy-start.5
  32.6 5.5 %shard_map.108 = (f32[16,64,128]{2,1,0:T(8,128)S(1)}, bf16[1920,256]{1,0:T(8,128)(2,1)S(1)}) custom-call(f32[16,88,128]{2,1,0:T(8,128)S(1)} %get-tuple-element.28.ha0, f32[16,88,128]{2,1,0:T(8,128)S(1)} %get-tuple-element.29.hb0, f32[16,88,128]{2,1,0:T(8,128)S(1)} %get-tuple-element.30.ka0, f32[16,88,128]{2,1,0:T(8,128)S(1)} %get-tuple-element.31.kb0, ...), custom_call_target="tpu_custom_call" | custom-call | tf_op jit(solution)/shard_map/pallas_call | solution.py:406
  38.2 0.1 broadcast_in_dim.9.couple_ref
  38.3 0.0 copy-done.2
  38.3 0.0 copy-done.5
  38.3 6.5 %shard_map.111 = (f32[32,4096]{1,0:T(8,128)}, f32[4,32,512]{2,1,0:T(8,128)S(1)}) custom-call(bf16[1920,256]{1,0:T(8,128)(2,1)S(1)} %get-tuple-element.37.table_ref, s32[32,128]{1,0:T(8,128)S(1)} %bitcast.16, f32[8,4096]{1,0:T(8,128)S(1)} %shard_map.110.part_ref, f32[32,4096]{1,0:T(8,128)S(1)} %copy-done.2, f32[96,128]{1,0:T(8,128)S(1)} %broadcast_in_dim.9.couple_ref, ...), custom_call_target="tpu_custom_call" | custom-call | tf_op jit(solution)/shard_map/pallas_call | solution.py:406
  44.8 0.9 %collective-permute-start.4 = (f32[32,512]{1,0:T(8,128)S(1)}, f32[32,512]{1,0:T(8,128)S(1)}, u32[]{:S(2)}, u32[]{:S(2)}) collective-permute-start(f32[32,512]{1,0:T(8,128)S(1)} %get-tuple-element.44), channel_id=1, source_target_pairs={{0,16},{16,32},{32,48},{48,64},{64,80},{80,96},{96,112},{112,128},... | collective-permute-start | bytes 196616 | tf_op jit(solution)/shard_map/ppermute | solution.py:418
  45.7 4.8 %collective-permute-start.5 = (f32[32,512]{1,0:T(8,128)S(1)}, f32[32,512]{1,0:T(8,128)S(1)}, u32[]{:S(2)}, u32[]{:S(2)}) collective-permute-start(f32[32,512]{1,0:T(8,128)S(1)} %get-tuple-element.43), channel_id=1, source_target_pairs={{0,240},{16,0},{32,16},{48,32},{64,48},{80,64},{96,80},{112,96},{1... | collective-permute-start | bytes 196616 | tf_op jit(solution)/shard_map/ppermute | solution.py:418
  50.6 1.1 %collective-permute-start.6 = (f32[32,512]{1,0:T(8,128)S(1)}, f32[32,512]{1,0:T(8,128)S(1)}, u32[]{:S(2)}, u32[]{:S(2)}) collective-permute-start(f32[32,512]{1,0:T(8,128)S(1)} %get-tuple-element.42), channel_id=1, source_target_pairs={{0,1},{1,2},{2,3},{3,4},{4,5},{5,6},{6,7},{7,8},{8,9},{9,10},{10,1... | collective-permute-start | bytes 196616 | tf_op jit(solution)/shard_map/ppermute | solution.py:418
  51.7 0.0 collective-permute-start.7
  51.7 1.3 %shard_map.109 = f32[1024,128]{1,0:T(8,128)} custom-call(f32[16,64,128]{2,1,0:T(8,128)S(1)} %get-tuple-element.36.ht_ref), custom_call_target="tpu_custom_call" | custom-call | tf_op jit(solution)/shard_map/pallas_call | solution.py:406
  53.0 0.0 collective-permute-done.4.a_ref
  53.0 0.0 collective-permute-done.5.b_ref
  53.1 0.0 collective-permute-done.6.c_ref
  53.1 4.5 %collective-permute-done.7.d_ref = f32[32,512]{1,0:T(8,128)S(1)} collective-permute-done((f32[32,512]{1,0:T(8,128)S(1)}, f32[32,512]{1,0:T(8,128)S(1)}, u32[]{:S(2)}, u32[]{:S(2)}) %collective-permute-start.7) | collective-permute-done | bytes 65568 | tf_op jit(solution)/shard_map/ppermute | solution.py:418
  57.5 0.7 %shard_map.112 = f32[4,32,512]{2,1,0:T(8,128)} custom-call(f32[32,512]{1,0:T(8,128)S(1)} %collective-permute-done.4.a_ref, f32[32,512]{1,0:T(8,128)S(1)} %collective-permute-done.5.b_ref, f32[32,512]{1,0:T(8,128)S(1)} %collective-permute-done.6.c_ref, f32[32,512]{1,0:T(8,128)S(1)} %collective-permute-done.7.d_ref), custom_call_target="tpu_custom_call" | custom-call | tf_op jit(solution)/shard_map/pallas_call | solution.py:406
  (2 shorter events, 0.0 us)
Async XLA Ops:
  0.6 1.0 %copy-start = (f32[64,16,128]{2,1,0:T(8,128)S(1)}, f32[64,16,128]{2,1,0:T(8,128)}, u32[]{:S(2)}) copy-start(f32[64,16,128]{2,1,0:T(8,128)} %param.8) | copy-start | bytes 1572868
  1.7 1.0 %copy-start.1 = (f32[64,16,128]{2,1,0:T(8,128)S(1)}, f32[64,16,128]{2,1,0:T(8,128)}, u32[]{:S(2)}) copy-start(f32[64,16,128]{2,1,0:T(8,128)} %param.9) | copy-start | bytes 1572868
  1.7 4.1 %copy-start.4 = (f32[8,8,8]{2,1,0:T(8,128)S(1)}, f32[8,8,8]{2,1,0:T(8,128)}, u32[]{:S(2)}) copy-start(f32[8,8,8]{2,1,0:T(8,128)} %param.10) | copy-start | bytes 6148
  3.6 4.1 %collective-permute-start = (f32[16,8,128]{2,1,0:T(8,128)S(1)}, f32[16,8,128]{2,1,0:T(8,128)S(1)}, u32[]{:S(2)}, u32[]{:S(2)}) collective-permute-start(f32[16,8,128]{2,1,0:T(8,128)S(1)} %get-tuple-element.23), channel_id=1, source_target_pairs={{0,1},{1,2},{2,3},{3,4},{4,5},{5,6},{6,7},{7,8},{8,9},{9,10},{10,1... | collective-permute-start | bytes 196616 | tf_op jit(solution)/shard_map/ppermute | solution.py:418
  5.8 5.8 %collective-permute-start.1 = (f32[16,8,128]{2,1,0:T(8,128)S(1)}, f32[16,8,128]{2,1,0:T(8,128)S(1)}, u32[]{:S(2)}, u32[]{:S(2)}) collective-permute-start(f32[16,8,128]{2,1,0:T(8,128)S(1)} %get-tuple-element.24), channel_id=1, source_target_pairs={{0,15},{1,0},{2,1},{3,2},{4,3},{5,4},{6,5},{7,6},{8,7},{9,8},{10,9... | collective-permute-start | bytes 196616 | tf_op jit(solution)/shard_map/ppermute | solution.py:418
  11.6 9.9 %copy-start.6 = (f32[3,32]{1,0:T(4,128)S(1)}, f32[3,32]{1,0:T(4,128)}, u32[]{:S(2)}) copy-start(f32[3,32]{1,0:T(4,128)} %param.13) | copy-start | bytes 1156
  11.6 10.0 %copy-start.7 = (s32[4,1]{0,1:T(1,128)S(1)}, s32[4,1]{0,1:T(1,128)}, u32[]{:S(2)}) copy-start(s32[4,1]{0,1:T(1,128)} %param.15) | copy-start | bytes 52
  13.6 19.0 %collective-permute-start.2 = (f32[504,128]{1,0:T(8,128)S(1)}, f32[504,128]{1,0:T(8,128)S(1)}, u32[]{:S(2)}, u32[]{:S(2)}) collective-permute-start(f32[504,128]{1,0:T(8,128)S(1)} %get-tuple-element.34), channel_id=1, source_target_pairs={{0,16},{16,32},{32,48},{48,64},{64,80},{80,96},{96,112},{112,128},... | collective-permute-start | bytes 774152 | tf_op jit(solution)/shard_map/ppermute | solution.py:418
  16.6 16.0 %collective-permute-start.3 = (f32[504,128]{1,0:T(8,128)S(1)}, f32[504,128]{1,0:T(8,128)S(1)}, u32[]{:S(2)}, u32[]{:S(2)}) collective-permute-start(f32[504,128]{1,0:T(8,128)S(1)} %get-tuple-element.35), channel_id=1, source_target_pairs={{0,240},{16,0},{32,16},{48,32},{64,48},{80,64},{96,80},{112,96},{1... | collective-permute-start | bytes 774152 | tf_op jit(solution)/shard_map/ppermute | solution.py:418
  21.7 8.0 %copy-start.3 = (s32[4096]{0:T(1024)S(1)}, s32[4096]{0:T(1024)}, u32[]{:S(2)}) copy-start(s32[4096]{0:T(1024)} %param.12) | copy-start | bytes 49156
  32.6 5.7 %copy-start.2 = (f32[32,4096]{1,0:T(8,128)S(1)}, f32[32,4096]{1,0:T(8,128)}, u32[]{:S(2)}) copy-start(f32[32,4096]{1,0:T(8,128)} %rec_ref.1) | copy-start | bytes 1572868
  32.6 5.6 %copy-start.5 = (s32[4,512]{1,0:T(4,128)S(1)}, s32[4,512]{1,0:T(4,128)}, u32[]{:S(2)}) copy-start(s32[4,512]{1,0:T(4,128)} %list_ref.1) | copy-start | bytes 24580
  44.8 8.2 %collective-permute-start.4 = (f32[32,512]{1,0:T(8,128)S(1)}, f32[32,512]{1,0:T(8,128)S(1)}, u32[]{:S(2)}, u32[]{:S(2)}) collective-permute-start(f32[32,512]{1,0:T(8,128)S(1)} %get-tuple-element.44), channel_id=1, source_target_pairs={{0,16},{16,32},{32,48},{48,64},{64,80},{80,96},{96,112},{112,128},... | collective-permute-start | bytes 196616 | tf_op jit(solution)/shard_map/ppermute | solution.py:418
  45.7 7.3 %collective-permute-start.5 = (f32[32,512]{1,0:T(8,128)S(1)}, f32[32,512]{1,0:T(8,128)S(1)}, u32[]{:S(2)}, u32[]{:S(2)}) collective-permute-start(f32[32,512]{1,0:T(8,128)S(1)} %get-tuple-element.43), channel_id=1, source_target_pairs={{0,240},{16,0},{32,16},{48,32},{64,48},{80,64},{96,80},{112,96},{1... | collective-permute-start | bytes 196616 | tf_op jit(solution)/shard_map/ppermute | solution.py:418
  50.6 2.5 %collective-permute-start.6 = (f32[32,512]{1,0:T(8,128)S(1)}, f32[32,512]{1,0:T(8,128)S(1)}, u32[]{:S(2)}, u32[]{:S(2)}) collective-permute-start(f32[32,512]{1,0:T(8,128)S(1)} %get-tuple-element.42), channel_id=1, source_target_pairs={{0,1},{1,2},{2,3},{3,4},{4,5},{5,6},{6,7},{7,8},{8,9},{9,10},{10,1... | collective-permute-start | bytes 196616 | tf_op jit(solution)/shard_map/ppermute | solution.py:418
  51.7 5.8 %collective-permute-start.7 = (f32[32,512]{1,0:T(8,128)S(1)}, f32[32,512]{1,0:T(8,128)S(1)}, u32[]{:S(2)}, u32[]{:S(2)}) collective-permute-start(f32[32,512]{1,0:T(8,128)S(1)} %get-tuple-element.41), channel_id=1, source_target_pairs={{0,15},{1,0},{2,1},{3,2},{4,3},{5,4},{6,5},{7,6},{8,7},{9,8},{10,9... | collective-permute-start | bytes 196616 | tf_op jit(solution)/shard_map/ppermute | solution.py:418

commit v7 on v6

--- a/solution.py
+++ b/solution.py
@@ -355,7 +355,7 @@
             part_ref[c : c + 1, at] = sampled
         return carry
 
-    lax.fori_loop(0, 4096 // BLOCK, block, 0, unroll=4)
+    lax.fori_loop(0, 4096 // BLOCK, block, 0, unroll=8)
 
 
 def sample_kernel(
@@ -377,7 +377,7 @@
             split(pick_ref, rows, total[:, i * 128 : (i + 1) * 128])
         return carry
 
-    lax.fori_loop(0, 4096 // BLOCK, block, 0, unroll=4)
+    lax.fori_loop(0, 4096 // BLOCK, block, 0, unroll=8)
     for d in range(4):
         index = list_ref[d : d + 1, :]
         got = jnp.dot(pick_ref[...], onehot_pair(index & 127), preferred_element_type=F32)

time: 58.4 us -> 58 us (level)
  Pallas kernels: 30.3 us -> 29.7 us
where the time goes in v7:
time: 58 us; the launch traced here: 57.9 us
  Pallas kernels  29.7 us (51%)
  starting transfers between devices  17.2 us (30%)
  waiting for transfers between devices  8.35 us (14%)
  local copies, waits for them, and re-layouts  1.87 us (3%)
  between operations  0.76 us (1%)
    pallas_call x10, Pallas kernels, call(): pl.pallas_call(kernel, out_shape=[jax.ShapeDtypeStruct(s, t) for s, t in...  29.7 us
    ppermute x8, starting transfers between devices, ring(): lax.ppermute(value, axis, [(i, (i + steps) % count) for i in range(count)])  17.2 us
    ppermute x8, waiting for transfers between devices, ring(): lax.ppermute(value, axis, [(i, (i + steps) % count) for i in range(count)])  8.35 us
    unnamed x17, local copies, waits for them, and re-layouts  1.69 us
  transfers between devices with their start and end apart: 8, of which 2 were waited for; matrix products, arithmetic and copies ran while one was open for 0% of the time, Pallas kernels for 24%

profile of v7, /device:TPU:7, one launch (start us, length us, event | category | flops | bytes accessed | tf_op | source)
XLA Modules:
  0.0 57.9 jit_solution(4834336401107946770)
XLA Ops:
  0.6 0.0 copy-start
  0.6 1.0 %copy-done = f32[64,16,128]{2,1,0:T(8,128)S(1)} copy-done((f32[64,16,128]{2,1,0:T(8,128)S(1)}, f32[64,16,128]{2,1,0:T(8,128)}, u32[]{:S(2)}) %copy-start) | copy-done | bytes 524312
  1.7 0.0 copy-start.1
  1.7 0.0 copy-start.4
  1.7 0.5 shard_map.103.ht_ref
  2.2 0.5 copy-done.1
  2.7 0.9 %shard_map.104 = (f32[16,64,128]{2,1,0:T(8,128)S(1)}, f32[16,8,128]{2,1,0:T(8,128)S(1)}, f32[16,8,128]{2,1,0:T(8,128)S(1)}) custom-call(f32[1024,128]{1,0:T(8,128)S(1)} %bitcast.14, f32[16,64,128]{2,1,0:T(8,128)S(1)} %shard_map.103.ht_ref), custom_call_target="tpu_custom_call" | custom-call | tf_op jit(solution)/shard_map/pallas_call | solution.py:406
  3.6 2.2 %collective-permute-start = (f32[16,8,128]{2,1,0:T(8,128)S(1)}, f32[16,8,128]{2,1,0:T(8,128)S(1)}, u32[]{:S(2)}, u32[]{:S(2)}) collective-permute-start(f32[16,8,128]{2,1,0:T(8,128)S(1)} %get-tuple-element.23), channel_id=1, source_target_pairs={{0,1},{1,2},{2,3},{3,4},{4,5},{5,6},{6,7},{7,8},{8,9},{9,10},{10,1... | collective-permute-start | bytes 196616 | tf_op jit(solution)/shard_map/ppermute | solution.py:418
  5.8 0.0 collective-permute-start.1
  5.8 0.0 copy-done.4
  5.8 1.9 %shard_map.105.cond_ref = f32[26,80,128]{2,1,0:T(8,128)S(1)} custom-call(f32[64,8]{1,0:T(8,128)S(1)} %bitcast.17), custom_call_target="tpu_custom_call" | custom-call | tf_op jit(solution)/shard_map/pallas_call | solution.py:406
  7.7 0.0 collective-permute-done.nlo_ref
  7.7 3.9 %collective-permute-done.1.nhi_ref = f32[16,8,128]{2,1,0:T(8,128)S(1)} collective-permute-done((f32[16,8,128]{2,1,0:T(8,128)S(1)}, f32[16,8,128]{2,1,0:T(8,128)S(1)}, u32[]{:S(2)}, u32[]{:S(2)}) %collective-permute-start.1) | collective-permute-done | bytes 65568 | tf_op jit(solution)/shard_map/ppermute | solution.py:418
  11.6 0.0 copy-start.6
  11.6 0.0 copy-start.7
  11.6 2.0 %shard_map.107 = (f32[504,128]{1,0:T(8,128)S(1)}, f32[504,128]{1,0:T(8,128)S(1)}) custom-call(f32[16,64,128]{2,1,0:T(8,128)S(1)} %shard_map.103.ht_ref, f32[16,64,128]{2,1,0:T(8,128)S(1)} %get-tuple-element.22.st_ref, f32[16,8,128]{2,1,0:T(8,128)S(1)} %collective-permute-done.nlo_ref, f32[16,8,128]{2,1,0:T(8,128)S(1)} %collective-permute-done.1.nhi_ref, ...), custom_call_target="tpu_custom_call" | custom-call | tf_op jit(solution)/shard_map/pallas_call | solution.py:406
  13.6 3.1 %collective-permute-start.2 = (f32[504,128]{1,0:T(8,128)S(1)}, f32[504,128]{1,0:T(8,128)S(1)}, u32[]{:S(2)}, u32[]{:S(2)}) collective-permute-start(f32[504,128]{1,0:T(8,128)S(1)} %get-tuple-element.34), channel_id=1, source_target_pairs={{0,16},{16,32},{32,48},{48,64},{64,80},{80,96},{96,112},{112,128},... | collective-permute-start | bytes 774152 | tf_op jit(solution)/shard_map/ppermute | solution.py:418
  16.6 4.9 %collective-permute-start.3 = (f32[504,128]{1,0:T(8,128)S(1)}, f32[504,128]{1,0:T(8,128)S(1)}, u32[]{:S(2)}, u32[]{:S(2)}) collective-permute-start(f32[504,128]{1,0:T(8,128)S(1)} %get-tuple-element.35), channel_id=1, source_target_pairs={{0,240},{16,0},{32,16},{48,32},{64,48},{80,64},{96,80},{112,96},{1... | collective-permute-start | bytes 774152 | tf_op jit(solution)/shard_map/ppermute | solution.py:418
  21.5 0.0 copy-done.6
  21.5 0.1 broadcast_in_dim.8
  21.6 0.0 copy-done.7
  21.6 0.1 copy.11.count_ref
  21.7 0.0 copy-start.3
  21.7 8.0 %shard_map.106 = (f32[16,88,128]{2,1,0:T(8,128)S(1)}, f32[16,88,128]{2,1,0:T(8,128)S(1)}, f32[16,88,128]{2,1,0:T(8,128)S(1)}, f32[16,88,128]{2,1,0:T(8,128)S(1)}...) custom-call(f32[16,64,128]{2,1,0:T(8,128)S(1)} %shard_map.103.ht_ref, ...), custom_call_target="tpu_custom_call" | custom-call | tf_op jit(solution)/shard_map/pallas_call | solution.py:406
  29.7 0.0 copy-done.3
  29.7 2.7 %shard_map.110.part_ref = f32[8,4096]{1,0:T(8,128)S(1)} custom-call(bf16[1152,256]{1,0:T(8,128)(2,1)S(1)} %get-tuple-element.38.table_ref, s32[32,128]{1,0:T(8,128)S(1)} %bitcast.15), custom_call_target="tpu_custom_call" | custom-call | tf_op jit(solution)/shard_map/pallas_call | solution.py:406
  32.4 0.0 collective-permute-done.2.elo_ref
  32.4 0.0 collective-permute-done.3.ehi_ref
  32.4 0.0 copy-start.2
  32.4 0.0 copy-start.5
  32.5 5.5 %shard_map.108 = (f32[16,64,128]{2,1,0:T(8,128)S(1)}, bf16[1920,256]{1,0:T(8,128)(2,1)S(1)}) custom-call(f32[16,88,128]{2,1,0:T(8,128)S(1)} %get-tuple-element.28.ha0, f32[16,88,128]{2,1,0:T(8,128)S(1)} %get-tuple-element.29.hb0, f32[16,88,128]{2,1,0:T(8,128)S(1)} %get-tuple-element.30.ka0, f32[16,88,128]{2,1,0:T(8,128)S(1)} %get-tuple-element.31.kb0, ...), custom_call_target="tpu_custom_call" | custom-call | tf_op jit(solution)/shard_map/pallas_call | solution.py:406
  38.0 0.1 broadcast_in_dim.9.couple_ref
  38.1 0.0 copy-done.2
  38.1 0.0 copy-done.5
  38.1 6.1 %shard_map.111 = (f32[32,4096]{1,0:T(8,128)}, f32[4,32,512]{2,1,0:T(8,128)S(1)}) custom-call(bf16[1920,256]{1,0:T(8,128)(2,1)S(1)} %get-tuple-element.37.table_ref, s32[32,128]{1,0:T(8,128)S(1)} %bitcast.16, f32[8,4096]{1,0:T(8,128)S(1)} %shard_map.110.part_ref, f32[32,4096]{1,0:T(8,128)S(1)} %copy-done.2, f32[96,128]{1,0:T(8,128)S(1)} %broadcast_in_dim.9.couple_ref, ...), custom_call_target="tpu_custom_call" | custom-call | tf_op jit(solution)/shard_map/pallas_call | solution.py:406
  44.3 1.1 %collective-permute-start.4 = (f32[32,512]{1,0:T(8,128)S(1)}, f32[32,512]{1,0:T(8,128)S(1)}, u32[]{:S(2)}, u32[]{:S(2)}) collective-permute-start(f32[32,512]{1,0:T(8,128)S(1)} %get-tuple-element.44), channel_id=1, source_target_pairs={{0,16},{16,32},{32,48},{48,64},{64,80},{80,96},{96,112},{112,128},... | collective-permute-start | bytes 196616 | tf_op jit(solution)/shard_map/ppermute | solution.py:418
  45.4 4.6 %collective-permute-start.5 = (f32[32,512]{1,0:T(8,128)S(1)}, f32[32,512]{1,0:T(8,128)S(1)}, u32[]{:S(2)}, u32[]{:S(2)}) collective-permute-start(f32[32,512]{1,0:T(8,128)S(1)} %get-tuple-element.43), channel_id=1, source_target_pairs={{0,240},{16,0},{32,16},{48,32},{64,48},{80,64},{96,80},{112,96},{1... | collective-permute-start | bytes 196616 | tf_op jit(solution)/shard_map/ppermute | solution.py:418
  50.0 1.3 %collective-permute-start.6 = (f32[32,512]{1,0:T(8,128)S(1)}, f32[32,512]{1,0:T(8,128)S(1)}, u32[]{:S(2)}, u32[]{:S(2)}) collective-permute-start(f32[32,512]{1,0:T(8,128)S(1)} %get-tuple-element.42), channel_id=1, source_target_pairs={{0,1},{1,2},{2,3},{3,4},{4,5},{5,6},{6,7},{7,8},{8,9},{9,10},{10,1... | collective-permute-start | bytes 196616 | tf_op jit(solution)/shard_map/ppermute | solution.py:418
  51.3 0.0 collective-permute-start.7
  51.3 1.3 %shard_map.109 = f32[1024,128]{1,0:T(8,128)} custom-call(f32[16,64,128]{2,1,0:T(8,128)S(1)} %get-tuple-element.36.ht_ref), custom_call_target="tpu_custom_call" | custom-call | tf_op jit(solution)/shard_map/pallas_call | solution.py:406
  52.7 0.0 collective-permute-done.4.a_ref
  52.7 0.0 collective-permute-done.5.b_ref
  52.7 0.0 collective-permute-done.6.c_ref
  52.7 4.5 %collective-permute-done.7.d_ref = f32[32,512]{1,0:T(8,128)S(1)} collective-permute-done((f32[32,512]{1,0:T(8,128)S(1)}, f32[32,512]{1,0:T(8,128)S(1)}, u32[]{:S(2)}, u32[]{:S(2)}) %collective-permute-start.7) | collective-permute-done | bytes 65568 | tf_op jit(solution)/shard_map/ppermute | solution.py:418
  57.1 0.7 %shard_map.112 = f32[4,32,512]{2,1,0:T(8,128)} custom-call(f32[32,512]{1,0:T(8,128)S(1)} %collective-permute-done.4.a_ref, f32[32,512]{1,0:T(8,128)S(1)} %collective-permute-done.5.b_ref, f32[32,512]{1,0:T(8,128)S(1)} %collective-permute-done.6.c_ref, f32[32,512]{1,0:T(8,128)S(1)} %collective-permute-done.7.d_ref), custom_call_target="tpu_custom_call" | custom-call | tf_op jit(solution)/shard_map/pallas_call | solution.py:406
  (2 shorter events, 0.0 us)
Async XLA Ops:
  0.6 1.0 %copy-start = (f32[64,16,128]{2,1,0:T(8,128)S(1)}, f32[64,16,128]{2,1,0:T(8,128)}, u32[]{:S(2)}) copy-start(f32[64,16,128]{2,1,0:T(8,128)} %param.8) | copy-start | bytes 1572868
  1.7 1.0 %copy-start.1 = (f32[64,16,128]{2,1,0:T(8,128)S(1)}, f32[64,16,128]{2,1,0:T(8,128)}, u32[]{:S(2)}) copy-start(f32[64,16,128]{2,1,0:T(8,128)} %param.9) | copy-start | bytes 1572868
  1.7 4.1 %copy-start.4 = (f32[8,8,8]{2,1,0:T(8,128)S(1)}, f32[8,8,8]{2,1,0:T(8,128)}, u32[]{:S(2)}) copy-start(f32[8,8,8]{2,1,0:T(8,128)} %param.10) | copy-start | bytes 6148
  3.6 4.1 %collective-permute-start = (f32[16,8,128]{2,1,0:T(8,128)S(1)}, f32[16,8,128]{2,1,0:T(8,128)S(1)}, u32[]{:S(2)}, u32[]{:S(2)}) collective-permute-start(f32[16,8,128]{2,1,0:T(8,128)S(1)} %get-tuple-element.23), channel_id=1, source_target_pairs={{0,1},{1,2},{2,3},{3,4},{4,5},{5,6},{6,7},{7,8},{8,9},{9,10},{10,1... | collective-permute-start | bytes 196616 | tf_op jit(solution)/shard_map/ppermute | solution.py:418
  5.8 5.8 %collective-permute-start.1 = (f32[16,8,128]{2,1,0:T(8,128)S(1)}, f32[16,8,128]{2,1,0:T(8,128)S(1)}, u32[]{:S(2)}, u32[]{:S(2)}) collective-permute-start(f32[16,8,128]{2,1,0:T(8,128)S(1)} %get-tuple-element.24), channel_id=1, source_target_pairs={{0,15},{1,0},{2,1},{3,2},{4,3},{5,4},{6,5},{7,6},{8,7},{9,8},{10,9... | collective-permute-start | bytes 196616 | tf_op jit(solution)/shard_map/ppermute | solution.py:418
  11.6 9.9 %copy-start.6 = (f32[3,32]{1,0:T(4,128)S(1)}, f32[3,32]{1,0:T(4,128)}, u32[]{:S(2)}) copy-start(f32[3,32]{1,0:T(4,128)} %param.13) | copy-start | bytes 1156
  11.6 10.0 %copy-start.7 = (s32[4,1]{0,1:T(1,128)S(1)}, s32[4,1]{0,1:T(1,128)}, u32[]{:S(2)}) copy-start(s32[4,1]{0,1:T(1,128)} %param.15) | copy-start | bytes 52
  13.6 18.8 %collective-permute-start.2 = (f32[504,128]{1,0:T(8,128)S(1)}, f32[504,128]{1,0:T(8,128)S(1)}, u32[]{:S(2)}, u32[]{:S(2)}) collective-permute-start(f32[504,128]{1,0:T(8,128)S(1)} %get-tuple-element.34), channel_id=1, source_target_pairs={{0,16},{16,32},{32,48},{48,64},{64,80},{80,96},{96,112},{112,128},... | collective-permute-start | bytes 774152 | tf_op jit(solution)/shard_map/ppermute | solution.py:418
  16.6 15.8 %collective-permute-start.3 = (f32[504,128]{1,0:T(8,128)S(1)}, f32[504,128]{1,0:T(8,128)S(1)}, u32[]{:S(2)}, u32[]{:S(2)}) collective-permute-start(f32[504,128]{1,0:T(8,128)S(1)} %get-tuple-element.35), channel_id=1, source_target_pairs={{0,240},{16,0},{32,16},{48,32},{64,48},{80,64},{96,80},{112,96},{1... | collective-permute-start | bytes 774152 | tf_op jit(solution)/shard_map/ppermute | solution.py:418
  21.7 8.0 %copy-start.3 = (s32[4096]{0:T(1024)S(1)}, s32[4096]{0:T(1024)}, u32[]{:S(2)}) copy-start(s32[4096]{0:T(1024)} %param.12) | copy-start | bytes 49156
  32.4 5.7 %copy-start.2 = (f32[32,4096]{1,0:T(8,128)S(1)}, f32[32,4096]{1,0:T(8,128)}, u32[]{:S(2)}) copy-start(f32[32,4096]{1,0:T(8,128)} %rec_ref.1) | copy-start | bytes 1572868
  32.4 5.6 %copy-start.5 = (s32[4,512]{1,0:T(4,128)S(1)}, s32[4,512]{1,0:T(4,128)}, u32[]{:S(2)}) copy-start(s32[4,512]{1,0:T(4,128)} %list_ref.1) | copy-start | bytes 24580
  44.3 8.4 %collective-permute-start.4 = (f32[32,512]{1,0:T(8,128)S(1)}, f32[32,512]{1,0:T(8,128)S(1)}, u32[]{:S(2)}, u32[]{:S(2)}) collective-permute-start(f32[32,512]{1,0:T(8,128)S(1)} %get-tuple-element.44), channel_id=1, source_target_pairs={{0,16},{16,32},{32,48},{48,64},{64,80},{80,96},{96,112},{112,128},... | collective-permute-start | bytes 196616 | tf_op jit(solution)/shard_map/ppermute | solution.py:418
  45.4 7.3 %collective-permute-start.5 = (f32[32,512]{1,0:T(8,128)S(1)}, f32[32,512]{1,0:T(8,128)S(1)}, u32[]{:S(2)}, u32[]{:S(2)}) collective-permute-start(f32[32,512]{1,0:T(8,128)S(1)} %get-tuple-element.43), channel_id=1, source_target_pairs={{0,240},{16,0},{32,16},{48,32},{64,48},{80,64},{96,80},{112,96},{1... | collective-permute-start | bytes 196616 | tf_op jit(solution)/shard_map/ppermute | solution.py:418
  50.0 2.7 %collective-permute-start.6 = (f32[32,512]{1,0:T(8,128)S(1)}, f32[32,512]{1,0:T(8,128)S(1)}, u32[]{:S(2)}, u32[]{:S(2)}) collective-permute-start(f32[32,512]{1,0:T(8,128)S(1)} %get-tuple-element.42), channel_id=1, source_target_pairs={{0,1},{1,2},{2,3},{3,4},{4,5},{5,6},{6,7},{7,8},{8,9},{9,10},{10,1... | collective-permute-start | bytes 196616 | tf_op jit(solution)/shard_map/ppermute | solution.py:418
  51.3 5.8 %collective-permute-start.7 = (f32[32,512]{1,0:T(8,128)S(1)}, f32[32,512]{1,0:T(8,128)S(1)}, u32[]{:S(2)}, u32[]{:S(2)}) collective-permute-start(f32[32,512]{1,0:T(8,128)S(1)} %get-tuple-element.41), channel_id=1, source_target_pairs={{0,15},{1,0},{2,1},{3,2},{4,3},{5,4},{6,5},{7,6},{8,7},{9,8},{10,9... | collective-permute-start | bytes 196616 | tf_op jit(solution)/shard_map/ppermute | solution.py:418
